TPU v7x, 32 devices: a whole 2x2x4 slice. The times are simulated.
32 devices in a mesh: box: 8 (over z, y), field: 4 (over x, core).
Axes of the slice: x: 2, y: 2, z: 4, core: 2. Of those that a mesh axis runs over, the one named last changes fastest.
Arguments:
- incident: bfloat16 [2, 2048, 4096], P(None, 'field', 'box'), may hold values from -6 to 6
- leaf_inverse: bfloat16 [8, 2, 512, 512], P('box', None, 'field'), may hold values from -0.1875 to 0.1875
- contrast: float32 [4096], P('box'), may hold values from 0.2 to 1
- skel_index: int32 [8, 2, 256], replicated, may hold values from 0 to 511
- ranks: int32 [8, 2], replicated, may hold values from 128 to 256, as said below
- top_core: bfloat16 [2, 256, 512], P(None, None, 'box'), may hold values from -0.25 to 0.25
Outputs:
- total_field: float32 [2, 2048, 4096], P(None, 'field', 'box')
Inputs may be any that keep to these rules, and one draw needn't show every extreme that they name: At each level some box has rank exactly 256; most ranks lie near 256 // 2.
All inputs are finite; a program needn't handle non-finite values.
Results may differ from a plain program's by a relative error of at most 0.0003.
Values may be sent and summed in bfloat16 or wider, within the bound.
No kernel may reach another device: no remote copies, remote signals or barrier semaphores. Data moves between devices by JAX's collectives and lax.ppermute only.
A program may use at most 64 MiB of HBM per device.

v0:
```python
import jax
import jax.numpy as jnp
from jax import lax
from jax.sharding import PartitionSpec as P

SIDE = 8


WAVENUM = 0.7
HIGH = lax.Precision.HIGHEST


def from_partner(value, axis, apart):
    mask = 2**apart
    pairs = [(source, source ^ mask) for source in range(lax.axis_size(axis))]
    return lax.ppermute(value, axis, pairs)


def positions(box_at, index_list):
    px = (SIDE * box_at + index_list % SIDE).astype(jnp.float32)
    py = (index_list // SIDE % SIDE).astype(jnp.float32)
    pz = (index_list // (SIDE * SIDE)).astype(jnp.float32)
    return jnp.stack([px, py, pz])


def selector(index_list, rank_now, width):
    rows = jnp.arange(index_list.shape[0], dtype=jnp.int32)[:, None]
    cols = jnp.arange(width, dtype=jnp.int32)[None, :]
    hit = (index_list[:, None] == cols) & (rows < rank_now)
    return hit.astype(jnp.float32)


def kernel_parts(own_pos, far_pos):
    diff = own_pos[:, :, None] - far_pos[:, None, :]
    dist = jnp.sqrt(jnp.sum(diff * diff, axis=0))
    return (jnp.cos(WAVENUM * dist) / dist, jnp.sin(WAVENUM * dist) / dist)


def complex_apply(mat_re, mat_im, vec):
    out_re = jnp.einsum("km,fm->fk", mat_re, vec[0], precision=HIGH) - jnp.einsum(
        "km,fm->fk", mat_im, vec[1], precision=HIGH
    )
    out_im = jnp.einsum("km,fm->fk", mat_re, vec[1], precision=HIGH) + jnp.einsum(
        "km,fm->fk", mat_im, vec[0], precision=HIGH
    )
    return jnp.stack([out_re, out_im])


def leaf_product(real_in, imag_in, mat_re, mat_im):
    dims = (((1,), (1,)), ((), ()))
    out_re = lax.dot_general(
        real_in, mat_re, dims, preferred_element_type=jnp.float32
    ) - lax.dot_general(imag_in, mat_im, dims, preferred_element_type=jnp.float32)
    out_im = lax.dot_general(
        imag_in, mat_re, dims, preferred_element_type=jnp.float32
    ) + lax.dot_general(real_in, mat_im, dims, preferred_element_type=jnp.float32)
    return jnp.stack([out_re, out_im])


def body(incident, leaf_inverse, contrast, skel_index, ranks, top_core):
    width = incident.shape[2]
    box_at = lax.axis_index("box")
    real_in = incident[0]
    imag_in = incident[1]
    block_rows = lax.all_gather(leaf_inverse, "field", axis=2, tiled=True)
    state = leaf_product(real_in, imag_in, block_rows[0, 0], block_rows[0, 1])
    for merge_level in range(2):
        far_at = jnp.bitwise_xor(box_at, 1 << merge_level)
        idx_own = skel_index[box_at, merge_level]
        idx_far = skel_index[far_at, merge_level]
        sel = selector(idx_own, ranks[box_at, merge_level], width)
        skel_vals = jnp.einsum("cfn,kn->cfk", state, sel, precision=HIGH)
        skel_q = jnp.dot(sel, contrast, precision=HIGH)
        far_vals = from_partner(skel_vals * skel_q, "box", merge_level)
        green_re, green_im = kernel_parts(positions(box_at, idx_own), positions(far_at, idx_far))
        pushed = complex_apply(green_re, green_im, far_vals)
        state = state - jnp.einsum("cfk,kn->cfn", pushed, sel, precision=HIGH)
    core_part = top_core
    for core_bit in range(2):
        other_part = from_partner(core_part, "box", core_bit)
        upper = box_at >> core_bit & 1 == 1
        core_part = jnp.where(
            upper,
            jnp.concatenate([other_part, core_part], 2),
            jnp.concatenate([core_part, other_part], 2),
        )
    core_full = core_part.astype(jnp.float32)
    sel_top = selector(skel_index[box_at, 1], ranks[box_at, 1], width)
    coarse = jnp.einsum("cfn,kn->cfk", state, sel_top, precision=HIGH)
    pushed = complex_apply(core_full[0], core_full[1], coarse)
    return state - jnp.einsum("cfk,kn->cfn", pushed, sel_top, precision=HIGH)


def solution(mesh):
    return jax.shard_map(
        body,
        mesh=mesh,
        in_specs=(
            P(None, "field", "box"),
            P("box", None, "field", None),
            P("box"),
            P(),
            P(),
            P(None, None, "box"),
        ),
        out_specs=P(None, "field", "box"),
        check_vma=False,
    )
```

profile of v0, /device:TPU:0, one launch (start us, length us, event | category | flops | bytes accessed | tf_op | source)
XLA Modules:
  0.0 114.8 jit_solution(15218451915131716726)
XLA Ops:
  6.5 0.0 copy-start
  6.5 0.0 all-gather.2.cloned.1.call-start
  6.5 0.7 all-gather.2.cloned.1.call-update
  7.3 1.4 %constant_dynamic-slice_fusion.5 = (s32[1,1]{0,1:T(1,128)}, s32[1,1]{0,1:T(1,128)}) fusion(s32[8,2]{0,1:T(2,128)} %param.10, s32[]{:T(128)S(6)} %select_n.203), kind=kLoop, calls=%fused_computation.164 | loop fusion | bytes 20 | tf_op jit(solution)/shard_map/dynamic_slice | solution.py:71
  8.7 0.7 iota_compare_fusion.3
  9.4 0.7 fusion.71
  10.1 0.8 fusion.72
  10.9 0.0 copy-done
  10.9 0.4 fusion.27
  11.3 17.0 %all-gather.2.cloned.1.call-done = bf16[1,2,512,512]{3,2,1,0:T(8,128)(2,1)} async-done(((bf16[1,2,128,512]{3,2,1,0:T(8,128)(2,1)}), bf16[1,2,512,512]{3,2,1,0:T(8,128)(2,1)}) %all-gather.2.cloned.1.call-update) | async-done | bytes 1048592 | tf_op jit(solution)/shard_map/all_gather | solution.py:65
  28.4 1.8 %fusion.24 = f32[512,512]{1,0:T(8,128)S(1)} fusion(bf16[1,2,512,512]{3,2,1,0:T(8,128)(2,1)} %all-gather.2.cloned.1.call-done, bf16[2,512,512]{2,1,0:T(8,128)(2,1)} %param.6), kind=kOutput, calls=%fused_computation.46 | convolution fusion | flops 268435456 | bytes 2097152 | tf_op jit(solution)/shard_map/dot_general | solution.py:51
  30.1 0.0 copy-done.1
  30.1 0.0 copy-done.2
  30.2 0.5 fusion.20
  30.6 0.5 fusion.4
  31.1 0.5 fusion.3
  31.6 1.2 %fusion.2 = f32[2,512,256]{2,1,0:T(8,128)S(1)} fusion(f32[1,512,512]{2,1,0:T(8,128)S(1)} %fusion.3, f32[1,512,512]{2,1,0:T(8,128)S(1)} %fusion.4, f32[256]{0:T(256)S(1)} %bitcast.169, s32[256]{0:T(256)S(1)} %bitcast.166, pred[256]{0:T(512)(128)(4,1)S(1)} %iota_compare_fusion.3), kind=kOutput, calls=%fused_computation.5 | convolution fusion | flops 1611661312 | bytes 3148032 | tf_op jit(solution)/shard_map/cfn,kn->cfk/dot_general | solution.py:72
  32.8 1.5 %collective-permute-start = (f32[2,512,256]{2,1,0:T(8,128)S(1)}, f32[2,512,256]{2,1,0:T(8,128)S(1)}, u32[]{:S(2)}, u32[]{:S(2)}) collective-permute-start(f32[2,512,256]{2,1,0:T(8,128)S(1)} %fusion.2), channel_id=1, source_target_pairs={{0,4},{4,0},{8,12},{12,8},{16,20},{20,16},{24,28},{28,24},{1,5},{5... | collective-permute-start | bytes 3145736 | tf_op jit(solution)/shard_map/ppermute | solution.py:16
  34.3 0.6 iota_compare_fusion.2
  35.1 0.2 multiply_reduce_fusion.1
  35.2 0.4 fusion.31
  35.6 22.5 %collective-permute-done = f32[2,512,256]{2,1,0:T(8,128)S(1)} collective-permute-done((f32[2,512,256]{2,1,0:T(8,128)S(1)}, f32[2,512,256]{2,1,0:T(8,128)S(1)}, u32[]{:S(2)}, u32[]{:S(2)}) %collective-permute-start) | collective-permute-done | bytes 1048608 | tf_op jit(solution)/shard_map/ppermute | solution.py:16
  58.2 1.5 %fusion.35 = f32[512,256]{1,0:T(8,128)S(1)} fusion(f32[2,512,256]{2,1,0:T(8,128)S(1)} %collective-permute-done, f32[256,256]{1,0:T(8,128)S(1)} %multiply_reduce_fusion.1), kind=kOutput, calls=%fused_computation.57 | convolution fusion | flops 402784256 | bytes 1310720 | tf_op jit(solution)/shard_map/km,fm->fk/dot_general | solution.py:40
  59.7 1.5 %fusion.34 = f32[512,256]{1,0:T(8,128)S(1)} fusion(f32[2,512,256]{2,1,0:T(8,128)S(1)} %collective-permute-done, f32[256,256]{1,0:T(8,128)S(1)} %multiply_reduce_fusion.1), kind=kOutput, calls=%fused_computation.56 | convolution fusion | flops 402784256 | bytes 1310720 | tf_op jit(solution)/shard_map/km,fm->fk/dot_general | solution.py:43
  61.3 1.5 %fusion.10 = f32[1,512,256]{2,1,0:T(8,128)S(1)} fusion(f32[512,256]{1,0:T(8,128)S(1)} %fusion.35, f32[2,512,256]{2,1,0:T(8,128)S(1)} %collective-permute-done, f32[256,256]{1,0:T(8,128)S(1)} %multiply_reduce_fusion.1), kind=kOutput, calls=%fused_computation.22 | convolution fusion | flops 402915328 | bytes 1835008 | tf_op jit(solution)/shard_map/km,fm->fk/dot_general | solution.py:40
  62.8 1.5 %fusion.9 = f32[1,512,256]{2,1,0:T(8,128)S(1)} fusion(f32[512,256]{1,0:T(8,128)S(1)} %fusion.34, f32[2,512,256]{2,1,0:T(8,128)S(1)} %collective-permute-done, f32[256,256]{1,0:T(8,128)S(1)} %multiply_reduce_fusion.1), kind=kOutput, calls=%fused_computation.20 | convolution fusion | flops 402915328 | bytes 1835008 | tf_op jit(solution)/shard_map/km,fm->fk/dot_general | solution.py:43
  64.3 1.2 %fusion = f32[2,512,512]{2,1,0:T(8,128)S(1)} fusion(f32[1,512,512]{2,1,0:T(8,128)S(1)} %fusion.3, f32[1,512,512]{2,1,0:T(8,128)S(1)} %fusion.4, f32[1,512,256]{2,1,0:T(8,128)S(1)} %fusion.9, f32[1,512,256]{2,1,0:T(8,128)S(1)} %fusion.10, s32[256]{0:T(256)S(1)} %bitcast.167, pred[256]{0:T(512)(128)(4,1)S(1)} %iota_compare_fusion.3), kind=kOutput, calls=%fused_computation.1 | convolution fusion | flops 1612185600 | bytes 5244160 | tf_op jit(solution)/shard_map/cfk,kn->cfn/dot_general | solution.py:77
  65.5 0.0 copy-start.3
  65.5 2.2 %convolution_multiply_fusion = f32[2,512,256]{2,1,0:T(8,128)} fusion(f32[2,512,512]{2,1,0:T(8,128)S(1)} %fusion, f32[256]{0:T(256)S(1)} %bitcast.168, s32[256]{0:T(256)S(1)} %bitcast.161, pred[256]{0:T(512)(128)(4,1)S(1)} %iota_compare_fusion.2), kind=kOutput, calls=%fused_computation.6 | convolution fusion | flops 1611137024 | bytes 3148032 | tf_op jit(solution)/shard_map/cfn,kn->cfk/dot_general | solution.py:72
  67.7 1.5 %collective-permute-start.1 = (f32[2,512,256]{2,1,0:T(8,128)}, f32[2,512,256]{2,1,0:T(8,128)S(1)}, u32[]{:S(2)}, u32[]{:S(2)}) collective-permute-start(f32[2,512,256]{2,1,0:T(8,128)} %convolution_multiply_fusion), channel_id=1, source_target_pairs={{0,8},{4,12},{8,0},{12,4},{16,24},{20,28},{24,16},{28,20},{1,9},{5... | collective-permute-start | bytes 3145736 | tf_op jit(solution)/shard_map/ppermute | solution.py:16
  69.2 1.5 %collective-permute-start.2 = (bf16[2,256,64]{1,2,0:T(8,128)(2,1)S(1)}, bf16[2,256,64]{1,2,0:T(8,128)(2,1)S(1)}, u32[]{:S(2)}, u32[]{:S(2)}) collective-permute-start(bf16[2,256,64]{1,2,0:T(8,128)(2,1)S(1)} %copy-done.3), channel_id=1, source_target_pairs={{0,4},{4,0},{8,12},{12,8},{16,20},{20,16},{24,28},{28,24},{1,5},{5... | collective-permute-start | bytes 196616 | tf_op jit(solution)/shard_map/ppermute | solution.py:16
  70.7 2.8 %collective-permute-done.2 = bf16[2,256,64]{1,2,0:T(8,128)(2,1)S(1)} collective-permute-done((bf16[2,256,64]{1,2,0:T(8,128)(2,1)S(1)}, bf16[2,256,64]{1,2,0:T(8,128)(2,1)S(1)}, u32[]{:S(2)}, u32[]{:S(2)}) %collective-permute-start.2) | collective-permute-done | bytes 65568 | tf_op jit(solution)/shard_map/ppermute | solution.py:16
  73.5 0.6 collective-permute-start.3
  74.1 0.2 multiply_reduce_fusion
  74.3 20.9 %collective-permute-done.3 = bf16[2,256,128]{1,2,0:T(8,128)(2,1)S(1)} collective-permute-done((bf16[2,256,128]{1,2,0:T(8,128)(2,1)S(1)}, bf16[2,256,128]{1,2,0:T(8,128)(2,1)S(1)}, u32[]{:S(2)}, u32[]{:S(2)}) %collective-permute-start.3) | collective-permute-done | bytes 131104 | tf_op jit(solution)/shard_map/ppermute | solution.py:16
  95.2 0.1 maximum_select_fusion
  95.3 0.0 collective-permute-done.1
  95.3 1.5 %fusion.37 = f32[512,256]{1,0:T(8,128)S(1)} fusion(f32[2,512,256]{2,1,0:T(8,128)S(1)} %collective-permute-done.1, f32[256,256]{1,0:T(8,128)S(1)} %multiply_reduce_fusion), kind=kOutput, calls=%fused_computation.59 | convolution fusion | flops 402784256 | bytes 1310720 | tf_op jit(solution)/shard_map/km,fm->fk/dot_general | solution.py:40
  96.9 1.5 %fusion.36 = f32[512,256]{1,0:T(8,128)S(1)} fusion(f32[2,512,256]{2,1,0:T(8,128)S(1)} %collective-permute-done.1, f32[256,256]{1,0:T(8,128)S(1)} %multiply_reduce_fusion), kind=kOutput, calls=%fused_computation.58 | convolution fusion | flops 402784256 | bytes 1310720 | tf_op jit(solution)/shard_map/km,fm->fk/dot_general | solution.py:43
  98.4 1.5 %fusion.8 = f32[1,512,256]{2,1,0:T(8,128)S(1)} fusion(f32[512,256]{1,0:T(8,128)S(1)} %fusion.37, f32[2,512,256]{2,1,0:T(8,128)S(1)} %collective-permute-done.1, f32[256,256]{1,0:T(8,128)S(1)} %multiply_reduce_fusion), kind=kOutput, calls=%fused_computation.18 | convolution fusion | flops 402915328 | bytes 1835008 | tf_op jit(solution)/shard_map/km,fm->fk/dot_general | solution.py:40
  99.9 1.5 %fusion.7 = f32[1,512,256]{2,1,0:T(8,128)S(1)} fusion(f32[512,256]{1,0:T(8,128)S(1)} %fusion.36, f32[2,512,256]{2,1,0:T(8,128)S(1)} %collective-permute-done.1, f32[256,256]{1,0:T(8,128)S(1)} %multiply_reduce_fusion), kind=kOutput, calls=%fused_computation.16 | convolution fusion | flops 402915328 | bytes 1835008 | tf_op jit(solution)/shard_map/km,fm->fk/dot_general | solution.py:43
  101.5 1.2 %convolution_subtract_fusion.1 = f32[2,512,512]{2,1,0:T(8,128)S(1)} fusion(f32[2,512,512]{2,1,0:T(8,128)S(1)} %fusion, f32[1,512,256]{2,1,0:T(8,128)S(1)} %fusion.7, f32[1,512,256]{2,1,0:T(8,128)S(1)} %fusion.8, s32[256]{0:T(256)S(1)} %bitcast.162, pred[256]{0:T(512)(128)(4,1)S(1)} %iota_compare_fusion.2), kind=kOutput, calls=%fused_computation.4 | convolution fusion | flops 1611661312 | bytes 5244160 | tf_op jit(solution)/shard_map/cfk,kn->cfn/dot_general | solution.py:77
  102.7 1.2 %fusion.55 = f32[2,512,256]{2,1,0:T(8,128)S(1)} fusion(f32[2,512,512]{2,1,0:T(8,128)S(1)} %convolution_subtract_fusion.1, s32[256]{0:T(256)S(1)} %bitcast.163, pred[256]{0:T(512)(128)(4,1)S(1)} %iota_compare_fusion.2), kind=kOutput, calls=%fused_computation.79 | convolution fusion | flops 1610874880 | bytes 3147008 | tf_op jit(solution)/shard_map/cfn,kn->cfk/dot_general | solution.py:89
  103.9 0.4 fusion.38
  104.3 0.4 fusion.39
  104.7 0.4 fusion.6
  105.1 0.4 fusion.5
  105.5 2.4 %convolution_subtract_fusion = f32[2,512,512]{2,1,0:T(8,128)} fusion(f32[2,512,512]{2,1,0:T(8,128)S(1)} %convolution_subtract_fusion.1, f32[1,512,256]{2,1,0:T(8,128)S(1)} %fusion.5, f32[1,512,256]{2,1,0:T(8,128)S(1)} %fusion.6, s32[256]{0:T(256)S(1)} %bitcast.164, pred[256]{0:T(512)(128)(4,1)S(1)} %iota_compare_fusion.2), kind=kOutput, calls=%fused_computation.3 | convolution fusion | flops 1611661312 | bytes 5244160 | tf_op jit(solution)/shard_map/cfk,kn->cfn/dot_general | solution.py:91
  (8 shorter events, 0.1 us)
Async XLA Ops:
  6.5 4.4 %copy-start = (f32[512]{0:T(512)S(1)}, f32[512]{0:T(512)}, u32[]{:S(2)}) copy-start(f32[512]{0:T(512)} %param.8) | copy-start | bytes 6148
  6.5 23.6 %copy-start.1 = (bf16[2,512,512]{2,1,0:T(8,128)(2,1)S(1)}, bf16[2,512,512]{2,1,0:T(8,128)(2,1)}, u32[]{:S(2)}) copy-start(bf16[2,512,512]{2,1,0:T(8,128)(2,1)} %param.6) | copy-start | bytes 3145732
  6.5 21.8 %all-gather.2.cloned.1.call-start = ((), (), s32[]{:S(2)}) async-start(), calls=%async_computation | async-start | bytes 1310720 | tf_op jit(solution)/shard_map/all_gather | solution.py:65
  28.4 1.8 %copy-start.2 = (bf16[1,2,512,512]{3,2,1,0:T(8,128)(2,1)S(1)}, bf16[1,2,512,512]{3,2,1,0:T(8,128)(2,1)}, u32[]{:S(2)}) copy-start(bf16[1,2,512,512]{3,2,1,0:T(8,128)(2,1)} %all-gather.2.cloned.1.call-done) | copy-start | bytes 3145732
  32.8 25.4 %collective-permute-start = (f32[2,512,256]{2,1,0:T(8,128)S(1)}, f32[2,512,256]{2,1,0:T(8,128)S(1)}, u32[]{:S(2)}, u32[]{:S(2)}) collective-permute-start(f32[2,512,256]{2,1,0:T(8,128)S(1)} %fusion.2), channel_id=1, source_target_pairs={{0,4},{4,0},{8,12},{12,8},{16,20},{20,16},{24,28},{28,24},{1,5},{5... | collective-permute-start | bytes 3145736 | tf_op jit(solution)/shard_map/ppermute | solution.py:16
  65.5 3.7 %copy-start.3 = (bf16[2,256,64]{1,2,0:T(8,128)(2,1)S(1)}, bf16[2,256,64]{1,2,0:T(8,128)(2,1)}, u32[]{:S(2)}) copy-start(bf16[2,256,64]{1,2,0:T(8,128)(2,1)} %param.11) | copy-start | bytes 196612
  67.7 27.6 %collective-permute-start.1 = (f32[2,512,256]{2,1,0:T(8,128)}, f32[2,512,256]{2,1,0:T(8,128)S(1)}, u32[]{:S(2)}, u32[]{:S(2)}) collective-permute-start(f32[2,512,256]{2,1,0:T(8,128)} %convolution_multiply_fusion), channel_id=1, source_target_pairs={{0,8},{4,12},{8,0},{12,4},{16,24},{20,28},{24,16},{28,20},{1,9},{5... | collective-permute-start | bytes 3145736 | tf_op jit(solution)/shard_map/ppermute | solution.py:16
  69.2 4.3 %collective-permute-start.2 = (bf16[2,256,64]{1,2,0:T(8,128)(2,1)S(1)}, bf16[2,256,64]{1,2,0:T(8,128)(2,1)S(1)}, u32[]{:S(2)}, u32[]{:S(2)}) collective-permute-start(bf16[2,256,64]{1,2,0:T(8,128)(2,1)S(1)} %copy-done.3), channel_id=1, source_target_pairs={{0,4},{4,0},{8,12},{12,8},{16,20},{20,16},{24,28},{28,24},{1,5},{5... | collective-permute-start | bytes 196616 | tf_op jit(solution)/shard_map/ppermute | solution.py:16
  73.5 21.7 %collective-permute-start.3 = (bf16[2,256,128]{1,2,0:T(8,128)(2,1)S(1)}, bf16[2,256,128]{1,2,0:T(8,128)(2,1)S(1)}, u32[]{:S(2)}, u32[]{:S(2)}) collective-permute-start(bf16[2,256,128]{1,2,0:T(8,128)(2,1)S(1)} %maximum_select_fusion.1), channel_id=1, source_target_pairs={{0,8},{4,12},{8,0},{12,4},{16,24},{20,28},{24,16},{28,20},{1,9},{5... | collective-permute-start | bytes 393224 | tf_op jit(solution)/shard_map/ppermute | solution.py:16
Sparse Core Ops, SparseCore 0:
  8.9 19.4 all-gather.1
where the time goes:
time: 115 us
  waiting for transfers between devices  63.9 us (56%)
  matrix products  27.2 us (24%)
  between operations  13.7 us (12%)
  starting transfers between devices  5.1 us (4%)
  other arithmetic  3.4 us (3%)
  local copies, waits for them, and re-layouts  1.44 us (1%)
    ppermute x4, waiting for transfers between devices, from_partner(): return lax.ppermute(value, axis, pairs)  46.2 us
    all_gather x1, waiting for transfers between devices, body(): block_rows = lax.all_gather(leaf_inverse, 'field', axis=2, tiled=True)  17 us
    ppermute x4, starting transfers between devices, from_partner(): return lax.ppermute(value, axis, pairs)  5.1 us
    dot_general x3, matrix products, complex_apply(): jnp.einsum('km,fm->fk', mat_im, vec[1], precision=HIGH)  3.47 us
    dot_general x3, matrix products, complex_apply(): jnp.einsum('km,fm->fk', mat_im, vec[0], precision=HIGH)  3.46 us
    dot_general x3, matrix products, complex_apply(): jnp.einsum('km,fm->fk', mat_re, vec[1], precision=HIGH)  3.44 us
    dot_general x3, matrix products, complex_apply(): jnp.einsum('km,fm->fk', mat_re, vec[0], precision=HIGH)  3.44 us
    dot_general x2, matrix products, body(): skel_vals = jnp.einsum('cfn,kn->cfk', state, sel, precision=HIGH)  3.41 us
  transfers between devices with their start and end apart: 5, of which 4 were waited for; matrix products, arithmetic and copies ran while one was open for 5% of the time, Pallas kernels for 0%

commit v1 on v0

v1 whole, which is shorter than its diff:
```python
import jax
import jax.numpy as jnp
from jax import lax
from jax.experimental import pallas as pl
from jax.experimental.pallas import tpu as pltpu
from jax.sharding import PartitionSpec as P

SIDE = 8
WAVENUM = 0.7
BF = jnp.bfloat16
F32 = jnp.float32
CHUNKS = (128, 128, 128, 128)
TOP = 32766.0
STEPS = 128.0
VMEM = pl.BlockSpec(memory_space=pltpu.VMEM)
SMEM = pl.BlockSpec(memory_space=pltpu.SMEM)
ANY = pl.BlockSpec(memory_space=pl.ANY)
PARAMS = pltpu.CompilerParams(vmem_limit_bytes=40 * 1024 * 1024)


def swap(value, axis, mask):
    return lax.ppermute(value, axis, [(s, s ^ mask) for s in range(lax.axis_size(axis))])


def call(body, name, outs, ins, specs=None, scratch=(), **kw):
    return pl.pallas_call(
        body,
        name=name,
        out_shape=outs,
        in_specs=specs or [VMEM] * len(ins),
        out_specs=kw.pop("out_specs", [VMEM] * len(outs)),
        scratch_shapes=list(scratch),
        compiler_params=PARAMS,
        **kw,
    )(*ins)


def shape(*dims, dtype=F32):
    return jax.ShapeDtypeStruct(dims, dtype)


def nn(a, b):
    return lax.dot_general(a, b, (((1,), (0,)), ((), ())), preferred_element_type=F32)


def nt(a, b):
    return lax.dot_general(a, b, (((1,), (1,)), ((), ())), preferred_element_type=F32)


def halves(v):
    hi = v.astype(BF)
    return hi, (v - hi.astype(F32)).astype(BF)


def iota(dims, axis):
    return lax.broadcasted_iota(jnp.int32, dims, axis)


def to_column(row):
    n = row.shape[1]
    return jnp.sum(jnp.where(iota((n, n), 0) == iota((n, n), 1), row, 0.0), axis=1, keepdims=True)


def to_row(col, width):
    n = col.shape[0]
    return jnp.sum(jnp.where(iota((n, width), 0) == iota((n, width), 1), col, 0.0), axis=0, keepdims=True)


def cos_sin(angle):
    turns = jnp.floor(angle * 0.6366197723675814 + 0.5)
    t = angle - turns * 1.5707855224609375
    t = t - turns * 1.0804334124e-05
    t2 = t * t
    c = 1.0 + t2 * (-0.5 + t2 * (4.1666667e-2 + t2 * (-1.3888889e-3 + t2 * 2.4801587e-5)))
    s = t * (1.0 + t2 * (-1.6666667e-1 + t2 * (8.3333333e-3 + t2 * (-1.9841270e-4 + t2 * 2.7557319e-6))))
    quad = turns.astype(jnp.int32) & 3
    odd = (quad & 1) == 1
    cc = jnp.where(odd, s, c)
    ss = jnp.where(odd, c, s)
    cc = jnp.where((quad == 1) | (quad == 2), -cc, cc)
    ss = jnp.where(quad >= 2, -ss, ss)
    return cc, ss


def place(index, box):
    return (
        (index & (SIDE - 1)).astype(F32) + (box * SIDE).astype(F32),
        ((index >> 3) & (SIDE - 1)).astype(F32),
        (index >> 6).astype(F32),
    )


def plan_body(at_ref, ranks_ref, skel_ref, contrast_ref, e0_ref, e1_ref, q_ref, ghi_ref, glo_ref, g1_ref, j_ref, d_ref):
    box = at_ref[0]
    kmax = skel_ref.shape[1]
    width = contrast_ref.shape[1]
    contrast = contrast_ref[...]
    rows = []
    cols = []
    rank = []
    for level in range(2):
        far = box ^ (1 << level)
        own_row = skel_ref[pl.ds(box * 2 + level, 1), :]
        far_row = skel_ref[pl.ds(far * 2 + level, 1), :]
        own_col = to_column(own_row.astype(F32)).astype(jnp.int32)
        far_col = to_column(far_row.astype(F32)).astype(jnp.int32)
        r = ranks_ref[box * 2 + level]
        rows.append(own_row)
        cols.append(own_col)
        rank.append(r)
        hit = (own_col == iota((kmax, width), 1)) & (iota((kmax, width), 0) < r)
        (e0_ref, e1_ref)[level][...] = hit.astype(F32).astype(BF)
        q_col = jnp.sum(jnp.where(hit, contrast, 0.0), axis=1, keepdims=True)
        q_ref[pl.ds(level, 1), :] = to_row(q_col, kmax)
        ox, oy, oz = place(own_row, box)
        fx, fy, fz = place(far_col, far)
        d2 = (fx - ox) * (fx - ox) + (fy - oy) * (fy - oy) + (fz - oz) * (fz - oz)
        dist = jnp.sqrt(d2)
        inv = 1.0 / dist
        c, s = cos_sin(WAVENUM * dist)
        c = c * inv
        s = s * inv
        if level == 0:
            chi, clo = halves(c)
            shi, slo = halves(s)
            ghi_ref[0:kmax, 0:kmax] = chi
            ghi_ref[0:kmax, kmax:] = shi
            ghi_ref[kmax:, 0:kmax] = -shi
            ghi_ref[kmax:, kmax:] = chi
            glo_ref[0:kmax, 0:kmax] = clo
            glo_ref[0:kmax, kmax:] = slo
            glo_ref[kmax:, 0:kmax] = -slo
            glo_ref[kmax:, kmax:] = clo
        else:
            g1_ref[:, 0:kmax] = c
            g1_ref[:, kmax:] = s
    mine = iota((kmax, kmax), 0)
    other = iota((kmax, kmax), 1)
    j_ref[...] = ((cols[0] == rows[1]) & (mine < rank[0]) & (other < rank[1])).astype(F32).astype(BF)
    d_ref[...] = ((cols[1] == rows[1]) & (mine < rank[1]) & (other < rank[1])).astype(F32).astype(BF)


def core_body(at_ref, own_ref, near_ref, far_ref, g1_ref, d_ref, mc_ref, khi_ref, klo_ref, ct_ref):
    slot = at_ref[0] & 3
    quarter = own_ref.shape[0] // 2
    kmax = own_ref.shape[1]
    pieces = (own_ref[...], near_ref[...], far_ref[0], far_ref[1])
    for mask, piece in enumerate(pieces):
        start = pl.multiple_of((slot ^ mask) * quarter, quarter)
        ct_ref[pl.ds(start, quarter), 0:kmax] = piece[:quarter]
        ct_ref[pl.ds(start, quarter), kmax:] = piece[quarter:]
    cr = ct_ref[:, 0:kmax]
    ci = ct_ref[:, kmax:]
    mc_ref[0:kmax, 0:kmax] = cr
    mc_ref[0:kmax, kmax:] = ci
    mc_ref[kmax:, 0:kmax] = -ci
    mc_ref[kmax:, kmax:] = cr
    dup = d_ref[...]
    gr = g1_ref[:, 0:kmax]
    gi = g1_ref[:, kmax:]
    grh, grl = halves(gr)
    gih, gil = halves(gi)
    dr = nn(grh, dup) + nn(grl, dup)
    di = nn(gih, dup) + nn(gil, dup)
    drh, drl = halves(dr)
    dih, dil = halves(di)
    kr = gr - ((nn(drh, cr) + nn(drl, cr)) - (nn(dih, ci) + nn(dil, ci)))
    ki = gi - ((nn(drh, ci) + nn(drl, ci)) + (nn(dih, cr) + nn(dil, cr)))
    krh, krl = halves(kr)
    kih, kil = halves(ki)
    for ref, a, b in ((khi_ref, krh, kih), (klo_ref, krl, kil)):
        ref[0:kmax, 0:kmax] = a
        ref[0:kmax, kmax:] = b
        ref[kmax:, 0:kmax] = -b
        ref[kmax:, kmax:] = a


def rows_body(at_ref, p0_ref, p1_ref, p2_ref, p3_ref, e_ref, a_ref, b_ref):
    me = at_ref[1]
    n = p0_ref.shape[1]
    width = p0_ref.shape[2]
    kmax = e_ref.shape[0]
    for mask, ref in enumerate((p0_ref, p1_ref, p2_ref, p3_ref)):
        start = pl.multiple_of((me ^ mask) * n, n)
        a_ref[pl.ds(start, n), 0:width] = ref[0]
        a_ref[pl.ds(start, n), width:] = ref[1]
    picked = nn(e_ref[...], a_ref[...]).astype(BF)
    re = picked[:, :width]
    im = picked[:, width:]
    b_ref[0:kmax, 0:width] = re
    b_ref[0:kmax, width:] = -im
    b_ref[kmax:, 0:width] = im
    b_ref[kmax:, width:] = re


def leaf_body(x_ref, a_ref, e_ref, y_ref, v_ref):
    width = x_ref.shape[2]
    kmax = e_ref.shape[0]
    x = jnp.concatenate([x_ref[0], x_ref[1]], axis=1)
    xs = jnp.concatenate([-x_ref[1], x_ref[0]], axis=1)
    a = a_ref[...]
    y_ref[:, 0:width] = nt(jnp.concatenate([x_ref[0], -x_ref[1]], axis=1), a)
    y_ref[:, width:] = nt(jnp.concatenate([x_ref[1], x_ref[0]], axis=1), a)
    picked = nn(e_ref[...], a).astype(BF)
    v_ref[:, 0:kmax] = nt(jnp.concatenate([x_ref[0], -x_ref[1]], axis=1), picked)
    v_ref[:, kmax:] = nt(jnp.concatenate([x_ref[1], x_ref[0]], axis=1), picked)


def pack(w, out_ref):
    n, both = w.shape
    k = both // 2
    most = jnp.max(jnp.abs(w), axis=1, keepdims=True)
    step = jnp.ceil(jnp.log2(jnp.maximum(most, 1e-30)) * STEPS)
    inv = TOP / jnp.exp2(step / STEPS)
    v = jnp.floor(w * inv + 0.5).astype(jnp.int32).astype(jnp.int16)
    out_ref[0:n, :] = v[:, :k]
    out_ref[n : 2 * n, :] = v[:, k:]
    out_ref[2 * n :, :] = jnp.broadcast_to(to_row(step, k), (16, k)).astype(jnp.int32).astype(jnp.int16)


def apply_packed(in_ref, mhi, mlo):
    n = (in_ref.shape[0] - 16) // 2
    k = in_ref.shape[1]
    steps = in_ref[2 * n :, :].astype(jnp.int32).astype(F32)[0:1, :]
    step = jnp.sum(jnp.where(iota((n, k), 0) == iota((n, k), 1), steps, 0.0), axis=1, keepdims=True)
    scale = jnp.exp2(step / STEPS) * (1.0 / TOP)
    v = jnp.concatenate([in_ref[0:n, :], in_ref[n : 2 * n, :]], axis=1).astype(jnp.int32)
    upper = (v + 128) & -256
    lower = (v - upper).astype(F32).astype(BF)
    upper = upper.astype(F32).astype(BF)
    return (nn(upper, mhi) + (nn(lower, mhi) + nn(upper, mlo))) * scale


def first_body(x_ref, b_ref, q_ref, *outs, parts):
    q = q_ref[0:1, :]
    q = jnp.concatenate([q, q], axis=1)
    for ref, (start, n) in zip(outs, parts):
        x = jnp.concatenate([x_ref[0, start : start + n], x_ref[1, start : start + n]], axis=1)
        pack(nt(x, b_ref[...]) * q, ref)


def second_body(in_ref, ghi_ref, glo_ref, v_ref, j_ref, q_ref, out_ref, gs_ref, us_ref, *, start):
    n = (in_ref.shape[0] - 16) // 2
    k = in_ref.shape[1]
    g = apply_packed(in_ref, ghi_ref[...], glo_ref[...])
    hi, lo = halves(g)
    gs_ref[0] = hi
    gs_ref[1] = lo
    j = j_ref[...]
    q = q_ref[1:2, :]
    re = v_ref[start : start + n, :k] - (nn(hi[:, :k], j) + nn(lo[:, :k], j))
    im = v_ref[start : start + n, k:] - (nn(hi[:, k:], j) + nn(lo[:, k:], j))
    u = jnp.concatenate([re, im], axis=1)
    pack(u * jnp.concatenate([q, q], axis=1), out_ref)
    hi, lo = halves(u)
    us_ref[0] = hi
    us_ref[1] = lo


def third_body(gs_ref, us_ref, y_ref, e0_ref, mc_ref, part_ref, p_ref, *, start):
    n = gs_ref.shape[1]
    k = e0_ref.shape[0]
    width = e0_ref.shape[1]
    e = e0_ref[...]
    for i in range(2):
        cols = slice(i * k, i * k + k)
        part_ref[i] = y_ref[start : start + n, i * width : (i + 1) * width] - (
            nn(gs_ref[0, :, cols], e) + nn(gs_ref[1, :, cols], e)
        )
    mc = mc_ref[...]
    p_ref[...] = nn(us_ref[0], mc) + nn(us_ref[1], mc)


def fourth_body(in_ref, khi_ref, klo_ref, part_ref, p_ref, e1_ref, *rest, start):
    out_ref, hold_ref, sem = rest[-3:]
    n = part_ref.shape[1]
    k = e1_ref.shape[0]
    p = p_ref[...] + apply_packed(in_ref, khi_ref[...], klo_ref[...])
    hi, lo = halves(p)
    e = e1_ref[...]
    copies = []
    for i in range(2):
        cols = slice(i * k, i * k + k)
        hold_ref[i] = part_ref[i] - (nn(hi[:, cols], e) + nn(lo[:, cols], e))
        copy = pltpu.make_async_copy(hold_ref.at[i], out_ref.at[i, pl.ds(start, n), :], sem.at[i])
        copy.start()
        copies.append(copy)
    for copy in copies:
        copy.wait()


def body(incident, leaf_inverse, contrast, skel_index, ranks, top_core):
    nf, width = incident.shape[1:]
    boxes, _, kmax = skel_index.shape
    quarter = top_core.shape[2]
    at = jnp.stack([lax.axis_index("box"), lax.axis_index("field")]).astype(jnp.int32)
    own = leaf_inverse[0]
    across = swap(own, "field", 2)
    beside = swap(own, "field", 1)
    core_own = jnp.swapaxes(top_core, 1, 2).reshape(2 * quarter, kmax)
    core_near = swap(core_own, "box", 1)
    core_far = swap(jnp.stack([core_own, core_near]), "box", 2)
    e0, e1, q, ghi, glo, g1, dup01, dup11 = call(
        plan_body,
        "plan",
        [
            shape(kmax, width, dtype=BF),
            shape(kmax, width, dtype=BF),
            shape(8, kmax),
            shape(2 * kmax, 2 * kmax, dtype=BF),
            shape(2 * kmax, 2 * kmax, dtype=BF),
            shape(kmax, 2 * kmax),
            shape(kmax, kmax, dtype=BF),
            shape(kmax, kmax, dtype=BF),
        ],
        [at, ranks.reshape(-1), skel_index.reshape(boxes * 2, kmax), contrast.reshape(1, width)],
        [SMEM, SMEM, VMEM, VMEM],
    )
    beyond = swap(across, "field", 1)
    a_all, b0 = call(
        rows_body,
        "rows",
        [shape(width, 2 * width, dtype=BF), shape(2 * kmax, 2 * width, dtype=BF)],
        [at, own, beside, across, beyond, e0],
        [SMEM] + [VMEM] * 5,
    )
    starts = [sum(CHUNKS[:i]) for i in range(len(CHUNKS))]
    sizes = list(zip(starts, CHUNKS))
    packed = []
    for name, parts in (("send_first", sizes[:1]), ("send_rest", sizes[1:])):
        packed += call(
            lambda *refs, parts=parts: first_body(*refs, parts=parts),
            name,
            [shape(2 * n + 16, kmax, dtype=jnp.int16) for _, n in parts],
            [incident, b0, q],
        )
    got = [swap(v, "box", 1) for v in packed]
    y, v1 = call(leaf_body, "leaf", [shape(nf, 2 * width), shape(nf, 2 * kmax)], [incident, a_all, e1])
    mc, khi, klo = call(
        core_body,
        "core",
        [shape(2 * kmax, 2 * kmax, dtype=BF)] * 3,
        [at, core_own, core_near, core_far, g1, dup11],
        [SMEM] + [VMEM] * 5,
        [pltpu.VMEM((kmax, 2 * kmax), BF)],
    )
    out = None
    late = []
    for i, (start, n) in enumerate(sizes):
        send, gs, us = call(
            lambda *refs, start=start: second_body(*refs, start=start),
            f"second{i}",
            [shape(2 * n + 16, kmax, dtype=jnp.int16), shape(2, n, 2 * kmax, dtype=BF), shape(2, n, 2 * kmax, dtype=BF)],
            [got[i], ghi, glo, v1, dup01, q],
        )
        back = swap(send, "box", 2)
        part, p = call(
            lambda *refs, start=start: third_body(*refs, start=start),
            f"third{i}",
            [shape(2, n, width), shape(n, 2 * kmax)],
            [gs, us, y, e0, mc],
        )
        late.append((back, part, p))
    for i, (start, n) in enumerate(sizes):
        back, part, p = late[i]
        ins = [back, khi, klo, part, p, e1] + ([] if out is None else [out])
        specs = [VMEM] * 6 + ([] if out is None else [ANY])
        (out,) = call(
            lambda *refs, start=start: fourth_body(*refs, start=start),
            f"fourth{i}",
            [shape(2, nf, width)],
            ins,
            specs,
            [pltpu.VMEM((2, n, width), F32), pltpu.SemaphoreType.DMA((2,))],
            out_specs=[ANY],
            input_output_aliases={} if out is None else {6: 0},
        )
    return out


def solution(mesh):
    return jax.shard_map(
        body,
        mesh=mesh,
        in_specs=(P(None, "field", "box"), P("box", None, "field", None), P("box"), P(), P(), P(None, None, "box")),
        out_specs=P(None, "field", "box"),
        check_vma=False,
    )
```

time: 115 us -> 52.6 us (0.46)
  waiting for transfers between devices: 63.9 us -> 15.3 us
  matrix products: 27.2 us -> 0 us
  Pallas kernels: 0 us -> 18.7 us
  between operations: 13.7 us -> 0.23 us
  starting transfers between devices: 5.1 us -> 14.9 us
  other arithmetic: 3.4 us -> 0.09 us
  local copies, waits for them, and re-layouts: 1.44 us -> 3.21 us
    ppermute x4 -> x13, waiting for transfers between devices: 46.2 us -> 15.3 us  [swap(): lax.ppermute(value, axis, [(s, s ^ mask) for s in range(lax.axis_size(axi...]
    dot_general x24 -> x0, matrix products: 27.2 us -> none  [the longest x3 3.47 us: complex_apply(): jnp.einsum('km,fm->fk', mat_im, vec[1], precision=HIGH)]
    pallas_call x0 -> x18, Pallas kernels: none -> 18.7 us  [call(): pl.pallas_call(body, name=name, out_shape=outs, in_specs=specs or [VMEM]...]
    all_gather x1 -> x0, waiting for transfers between devices: 17 us -> none  [body(): block_rows = lax.all_gather(leaf_inverse, 'field', axis=2, tiled=True)]
    ppermute x4 -> x13, starting transfers between devices: 5.1 us -> 14.9 us  [swap(): lax.ppermute(value, axis, [(s, s ^ mask) for s in range(lax.axis_size(axi...]
    unnamed x8 -> x9, local copies, waits for them, and re-layouts: 0.02 us -> 2.39 us
    convert_element_type x4 -> x0, other arithmetic: 1.57 us -> none  [the longest x3 0.85 us: positions(): py = (index_list // SIDE % SIDE).astype(jnp.float32)]
    dynamic_slice x1 -> x0, local copies, waits for them, and re-layouts: 1.42 us -> none  [body(): sel = selector(idx_own, ranks[box_at, merge_level], width)]
  transfers between devices with their start and end apart: 5 -> 13, of which waited for: 4 -> 3; matrix products, arithmetic and copies ran while one was open for 5% -> 3% of each run, Pallas kernels for 0% -> 30%
where the time goes in v1:
time: 52.6 us; the launch traced here: 52.3 us
  Pallas kernels  18.7 us (36%)
  waiting for transfers between devices  15.3 us (29%)
  starting transfers between devices  14.9 us (28%)
  local copies, waits for them, and re-layouts  3.21 us (6%)
    pallas_call x18, Pallas kernels, call(): pl.pallas_call(body, name=name, out_shape=outs, in_specs=specs or [VMEM]...  18.7 us
    ppermute x13, waiting for transfers between devices, swap(): lax.ppermute(value, axis, [(s, s ^ mask) for s in range(lax.axis_size(axi...  15.3 us
    ppermute x13, starting transfers between devices, swap(): lax.ppermute(value, axis, [(s, s ^ mask) for s in range(lax.axis_size(axi...  14.9 us
    unnamed x9, local copies, waits for them, and re-layouts  2.39 us
  transfers between devices with their start and end apart: 13, of which 3 were waited for; matrix products, arithmetic and copies ran while one was open for 3% of the time, Pallas kernels for 30%

profile of v1, /device:TPU:0, one launch (start us, length us, event | category | flops | bytes accessed | tf_op | source)
XLA Modules:
  0.0 52.3 jit_solution(8460777022952402414)
XLA Ops:
  0.0 2.9 %collective-permute-start.1 = (bf16[2,128,512]{2,1,0:T(8,128)(2,1)}, bf16[2,128,512]{2,1,0:T(8,128)(2,1)S(1)}, u32[]{:S(2)}, u32[]{:S(2)}) collective-permute-start(bf16[2,128,512]{2,1,0:T(8,128)(2,1)} %bitcast.10), channel_id=1, source_target_pairs={{0,2},{1,3},{2,0},{3,1},{4,6},{5,7},{6,4},{7,5},{8,10},{9,11},{10,... | collective-permute-start | bytes 786440 | tf_op jit(solution)/shard_map/ppermute | solution.py:22
  2.9 0.0 collective-permute-start
  2.9 6.5 %collective-permute-done.1.p2_ref = bf16[2,128,512]{2,1,0:T(8,128)(2,1)S(1)} collective-permute-done((bf16[2,128,512]{2,1,0:T(8,128)(2,1)}, bf16[2,128,512]{2,1,0:T(8,128)(2,1)S(1)}, u32[]{:S(2)}, u32[]{:S(2)}) %collective-permute-start.1) | collective-permute-done | bytes 262176 | tf_op jit(solution)/shard_map/ppermute | solution.py:22
  9.5 0.0 collective-permute-start.2
  9.5 0.8 %copy.11 = s32[8,2]{1,0:T(8,128)S(1)} copy(s32[8,2]{0,1:T(2,128)} %param.10) | data formatting | bytes 128 | tf_op args[4]
  10.2 0.1 reshape.12.ranks_ref
  10.3 0.7 %reshape.13.skel_ref = s32[16,256]{1,0:T(8,128)S(1)} reshape(s32[8,2,256]{2,1,0:T(2,128)} %param.9) | data formatting | bytes 32768 | tf_op jit(solution)/shard_map/reshape | solution.py:316
  11.0 0.1 pad_add_fusion.at_ref
  11.1 0.7 %copy-done.3 = f32[512]{0:T(512)S(1)} copy-done((f32[512]{0:T(512)S(1)}, f32[512]{0:T(512)}, u32[]{:S(2)}) %copy-start.3) | copy-done | bytes 2072
  11.8 2.1 %plan.1 = (bf16[256,512]{1,0:T(8,128)(2,1)S(1)}, bf16[256,512]{1,0:T(8,128)(2,1)S(1)}, f32[8,256]{1,0:T(8,128)S(1)}, bf16[512,512]{1,0:T(8,128)(2,1)S(1)}, bf16[...) custom-call(s32[2]{0:T(128)S(1)} %pad_add_fusion.at_ref, ...), custom_call_target="tpu_custom_call" | custom-call | tf_op jit(solution)/shard_map/plan/pallas_call | solution.py:26
  13.9 0.0 collective-permute-done.p1_ref
  13.9 0.0 collective-permute-done.2.p3_ref
  13.9 0.0 copy-start.1
  13.9 0.9 %copy-done.1 = bf16[1,2,128,512]{3,2,1,0:T(8,128)(2,1)S(1)} copy-done((bf16[1,2,128,512]{3,2,1,0:T(8,128)(2,1)S(1)}, bf16[1,2,128,512]{3,2,1,0:T(8,128)(2,1)}, u32[]{:S(2)}) %copy-start.1) | copy-done | bytes 262168
  14.9 1.1 %rows.1 = (bf16[512,1024]{1,0:T(8,128)(2,1)S(1)}, bf16[512,1024]{1,0:T(8,128)(2,1)S(1)}) custom-call(s32[2]{0:T(128)S(1)} %pad_add_fusion.at_ref, bf16[2,128,512]{2,1,0:T(8,128)(2,1)S(1)} %bitcast.12, bf16[2,128,512]{2,1,0:T(8,128)(2,1)S(1)} %collective-permute-done.p1_ref, bf16[2,128,512]{2,1,0:T(8,128)(2,1)S(1)} %collective-permute-done.1.p2_ref, ...), custom_call_target="tpu_custom_call" | custom-call | tf_op jit(solution)/shard_map/rows/pallas_call | solution.py:26
  15.9 0.0 copy-start.2
  16.0 0.6 %send_first.1 = s16[272,256]{1,0:T(8,128)(2,1)S(1)} custom-call(bf16[2,512,512]{2,1,0:T(8,128)(2,1)S(1)} %copy-done, bf16[512,1024]{1,0:T(8,128)(2,1)S(1)} %get-tuple-element.44.refs_1_, f32[8,256]{1,0:T(8,128)S(1)} %get-tuple-element.45.refs_2_.refs_5_), custom_call_target="tpu_custom_call" | custom-call | tf_op jit(solution)/shard_map/send_first/pallas_call | solution.py:26
  16.6 1.8 %collective-permute-start.11 = (s16[272,256]{1,0:T(8,128)(2,1)S(1)}, s16[272,256]{1,0:T(8,128)(2,1)S(1)}, u32[]{:S(2)}, u32[]{:S(2)}) collective-permute-start(s16[272,256]{1,0:T(8,128)(2,1)S(1)} %send_first.1), channel_id=1, source_target_pairs={{0,4},{4,0},{8,12},{12,8},{16,20},{20,16},{24,28},{28,24},{1,5},{5... | collective-permute-start | bytes 417800 | tf_op jit(solution)/shard_map/ppermute | solution.py:22
  18.4 1.3 %send_rest.1 = (s16[272,256]{1,0:T(8,128)(2,1)S(1)}, s16[272,256]{1,0:T(8,128)(2,1)S(1)}, s16[272,256]{1,0:T(8,128)(2,1)S(1)}) custom-call(bf16[2,512,512]{2,1,0:T(8,128)(2,1)S(1)} %copy-done, bf16[512,1024]{1,0:T(8,128)(2,1)S(1)} %get-tuple-element.44.refs_1_, f32[8,256]{1,0:T(8,128)S(1)} %get-tuple-element.45.refs_2_.refs_5_), custom_call_target="tpu_custom_call" | custom-call | tf_op jit(solution)/shard_map/send_rest/pallas_call | solution.py:26
  19.7 0.3 collective-permute-start.9
  20.0 1.8 %collective-permute-start.7 = (s16[272,256]{1,0:T(8,128)(2,1)S(1)}, s16[272,256]{1,0:T(8,128)(2,1)S(1)}, u32[]{:S(2)}, u32[]{:S(2)}) collective-permute-start(s16[272,256]{1,0:T(8,128)(2,1)S(1)} %get-tuple-element.64), channel_id=1, source_target_pairs={{0,4},{4,0},{8,12},{12,8},{16,20},{20,16},{24,28},{28,24},{1,5},{5... | collective-permute-start | bytes 417800 | tf_op jit(solution)/shard_map/ppermute | solution.py:22
  21.8 0.3 collective-permute-start.3
  22.1 1.8 %collective-permute-start.5 = (bf16[128,256]{1,0:T(8,128)(2,1)S(1)}, bf16[128,256]{1,0:T(8,128)(2,1)S(1)}, u32[]{:S(2)}, u32[]{:S(2)}) collective-permute-start(bf16[128,256]{1,0:T(8,128)(2,1)S(1)} %bitcast.13), channel_id=1, source_target_pairs={{0,4},{4,0},{8,12},{12,8},{16,20},{20,16},{24,28},{28,24},{1,5},{5... | collective-permute-start | bytes 196616 | tf_op jit(solution)/shard_map/ppermute | solution.py:22
  23.8 2.1 %leaf.1 = (f32[512,1024]{1,0:T(8,128)S(1)}, f32[512,512]{1,0:T(8,128)S(1)}) custom-call(bf16[2,512,512]{2,1,0:T(8,128)(2,1)S(1)} %copy-done, bf16[512,1024]{1,0:T(8,128)(2,1)S(1)} %get-tuple-element.49.a_ref, bf16[256,512]{1,0:T(8,128)(2,1)S(1)} %get-tuple-element.50.e_ref.refs_5_), custom_call_target="tpu_custom_call" | custom-call | tf_op jit(solution)/shard_map/leaf/pallas_call | solution.py:26
  25.9 0.0 collective-permute-done.11.refs_0_
  25.9 0.7 %second0.1 = (s16[272,256]{1,0:T(8,128)(2,1)S(1)}, bf16[2,128,512]{2,1,0:T(8,128)(2,1)S(1)}, bf16[2,128,512]{2,1,0:T(8,128)(2,1)S(1)}) custom-call(s16[272,256]{1,0:T(8,128)(2,1)S(1)} %collective-permute-done.11.refs_0_, bf16[512,512]{1,0:T(8,128)(2,1)S(1)} %get-tuple-element.47.refs_1_, bf16[512,512]{1,0:T(8,128)(2,1)S(1)} %get-tuple-element.48.refs_2_, ...), custom_call_target="tpu_custom_call" | custom-call | tf_op jit(solution)/shard_map/second0/pallas_call | solution.py:26
  26.7 1.6 %collective-permute-start.12 = (s16[272,256]{1,0:T(8,128)(2,1)S(1)}, s16[272,256]{1,0:T(8,128)(2,1)S(1)}, u32[]{:S(2)}, u32[]{:S(2)}) collective-permute-start(s16[272,256]{1,0:T(8,128)(2,1)S(1)} %get-tuple-element.76), channel_id=1, source_target_pairs={{0,8},{4,12},{8,0},{12,4},{16,24},{20,28},{24,16},{28,20},{1,9},{5... | collective-permute-start | bytes 417800 | tf_op jit(solution)/shard_map/ppermute | solution.py:22
  28.3 0.0 collective-permute-done.9.refs_0_
  28.3 0.7 %second1.1 = (s16[272,256]{1,0:T(8,128)(2,1)S(1)}, bf16[2,128,512]{2,1,0:T(8,128)(2,1)S(1)}, bf16[2,128,512]{2,1,0:T(8,128)(2,1)S(1)}) custom-call(s16[272,256]{1,0:T(8,128)(2,1)S(1)} %collective-permute-done.9.refs_0_, bf16[512,512]{1,0:T(8,128)(2,1)S(1)} %get-tuple-element.47.refs_1_, bf16[512,512]{1,0:T(8,128)(2,1)S(1)} %get-tuple-element.48.refs_2_, ...), custom_call_target="tpu_custom_call" | custom-call | tf_op jit(solution)/shard_map/second1/pallas_call | solution.py:26
  29.0 0.5 collective-permute-start.10
  29.6 0.7 %second2.1 = (s16[272,256]{1,0:T(8,128)(2,1)S(1)}, bf16[2,128,512]{2,1,0:T(8,128)(2,1)S(1)}, bf16[2,128,512]{2,1,0:T(8,128)(2,1)S(1)}) custom-call(s16[272,256]{1,0:T(8,128)(2,1)S(1)} %collective-permute-done.7.refs_0_, bf16[512,512]{1,0:T(8,128)(2,1)S(1)} %get-tuple-element.47.refs_1_, bf16[512,512]{1,0:T(8,128)(2,1)S(1)} %get-tuple-element.48.refs_2_, ...), custom_call_target="tpu_custom_call" | custom-call | tf_op jit(solution)/shard_map/second2/pallas_call | solution.py:26
  30.3 1.6 %collective-permute-start.8 = (s16[272,256]{1,0:T(8,128)(2,1)S(1)}, s16[272,256]{1,0:T(8,128)(2,1)S(1)}, u32[]{:S(2)}, u32[]{:S(2)}) collective-permute-start(s16[272,256]{1,0:T(8,128)(2,1)S(1)} %get-tuple-element.65), channel_id=1, source_target_pairs={{0,8},{4,12},{8,0},{12,4},{16,24},{20,28},{24,16},{28,20},{1,9},{5... | collective-permute-start | bytes 417800 | tf_op jit(solution)/shard_map/ppermute | solution.py:22
  31.9 0.3 collective-permute-done.3.refs_0_
  32.3 0.7 %second3.1 = (s16[272,256]{1,0:T(8,128)(2,1)S(1)}, bf16[2,128,512]{2,1,0:T(8,128)(2,1)S(1)}, bf16[2,128,512]{2,1,0:T(8,128)(2,1)S(1)}) custom-call(s16[272,256]{1,0:T(8,128)(2,1)S(1)} %collective-permute-done.3.refs_0_, bf16[512,512]{1,0:T(8,128)(2,1)S(1)} %get-tuple-element.47.refs_1_, bf16[512,512]{1,0:T(8,128)(2,1)S(1)} %get-tuple-element.48.refs_2_, ...), custom_call_target="tpu_custom_call" | custom-call | tf_op jit(solution)/shard_map/second3/pallas_call | solution.py:26
  33.0 1.7 %collective-permute-start.4 = (s16[272,256]{1,0:T(8,128)(2,1)S(1)}, s16[272,256]{1,0:T(8,128)(2,1)S(1)}, u32[]{:S(2)}, u32[]{:S(2)}) collective-permute-start(s16[272,256]{1,0:T(8,128)(2,1)S(1)} %get-tuple-element.53), channel_id=1, source_target_pairs={{0,8},{4,12},{8,0},{12,4},{16,24},{20,28},{24,16},{28,20},{1,9},{5... | collective-permute-start | bytes 417800 | tf_op jit(solution)/shard_map/ppermute | solution.py:22
  34.7 0.5 collective-permute-start.6
  35.2 8.4 %collective-permute-done.6.far_ref = bf16[2,128,256]{2,1,0:T(8,128)(2,1)S(1)} collective-permute-done((bf16[2,128,256]{2,1,0:T(8,128)(2,1)S(1)}, bf16[2,128,256]{2,1,0:T(8,128)(2,1)S(1)}, u32[]{:S(2)}, u32[]{:S(2)}) %collective-permute-start.6) | collective-permute-done | bytes 131104 | tf_op jit(solution)/shard_map/ppermute | solution.py:22
  43.6 1.3 %core.1 = (bf16[512,512]{1,0:T(8,128)(2,1)S(1)}, bf16[512,512]{1,0:T(8,128)(2,1)S(1)}, bf16[512,512]{1,0:T(8,128)(2,1)S(1)}) custom-call(s32[2]{0:T(128)S(1)} %pad_add_fusion.at_ref, bf16[128,256]{1,0:T(8,128)(2,1)S(1)} %bitcast.15, bf16[128,256]{1,0:T(8,128)(2,1)S(1)} %collective-permute-done.5.near_ref, ...), custom_call_target="tpu_custom_call" | custom-call | tf_op jit(solution)/shard_map/core/pallas_call | solution.py:26
  44.9 0.5 third2.1
  45.3 0.5 third3.1
  45.8 0.5 third1.1
  46.3 0.5 third0.1
  46.7 1.4 %fourth0.1.refs_6_ = f32[2,512,512]{2,1,0:T(8,128)} custom-call(s16[272,256]{1,0:T(8,128)(2,1)S(1)} %collective-permute-done.12.refs_0_, bf16[512,512]{1,0:T(8,128)(2,1)S(1)} %get-tuple-element.56.refs_1_, bf16[512,512]{1,0:T(8,128)(2,1)S(1)} %get-tuple-element.57.refs_2_, f32[2,128,512]{2,1,0:T(8,128)S(1)} %get-tuple-element.79.refs_3_, ...), custom_call_target="tpu_custom_call" | custom-call | tf_op jit(solution)/shard_map/fourth0/pallas_call | solution.py:26
  48.1 0.0 collective-permute-done.10.refs_0_
  48.1 1.4 %fourth1.1.refs_6_ = f32[2,512,512]{2,1,0:T(8,128)} custom-call(s16[272,256]{1,0:T(8,128)(2,1)S(1)} %collective-permute-done.10.refs_0_, bf16[512,512]{1,0:T(8,128)(2,1)S(1)} %get-tuple-element.56.refs_1_, bf16[512,512]{1,0:T(8,128)(2,1)S(1)} %get-tuple-element.57.refs_2_, ...), custom_call_target="tpu_custom_call", output_to_operand_aliasing={{}: (6, {})} | custom-call | tf_op jit(solution)/shard_map/fourth1/pallas_call | solution.py:26
  49.5 0.0 collective-permute-done.8.refs_0_
  49.6 1.4 %fourth2.1.refs_6_ = f32[2,512,512]{2,1,0:T(8,128)} custom-call(s16[272,256]{1,0:T(8,128)(2,1)S(1)} %collective-permute-done.8.refs_0_, bf16[512,512]{1,0:T(8,128)(2,1)S(1)} %get-tuple-element.56.refs_1_, bf16[512,512]{1,0:T(8,128)(2,1)S(1)} %get-tuple-element.57.refs_2_, ...), custom_call_target="tpu_custom_call", output_to_operand_aliasing={{}: (6, {})} | custom-call | tf_op jit(solution)/shard_map/fourth2/pallas_call | solution.py:26
  51.0 1.4 %fourth3.1 = f32[2,512,512]{2,1,0:T(8,128)} custom-call(s16[272,256]{1,0:T(8,128)(2,1)S(1)} %collective-permute-done.4.refs_0_, bf16[512,512]{1,0:T(8,128)(2,1)S(1)} %get-tuple-element.56.refs_1_, bf16[512,512]{1,0:T(8,128)(2,1)S(1)} %get-tuple-element.57.refs_2_, f32[2,128,512]{2,1,0:T(8,128)S(1)} %get-tuple-element.62.refs_3_, ...), custom_call_target="tpu_custom_call", output_to_operand_aliasing={{}: (6, {})} | custom-call | tf_op jit(solution)/shard_map/fourth3/pallas_call | solution.py:26
  (9 shorter events, 0.0 us)
Async XLA Ops:
  0.0 15.9 %copy-start = (bf16[2,512,512]{2,1,0:T(8,128)(2,1)S(1)}, bf16[2,512,512]{2,1,0:T(8,128)(2,1)}, u32[]{:S(2)}) copy-start(bf16[2,512,512]{2,1,0:T(8,128)(2,1)} %refs_0_.3) | copy-start | bytes 3145732
  0.0 9.5 %collective-permute-start.1 = (bf16[2,128,512]{2,1,0:T(8,128)(2,1)}, bf16[2,128,512]{2,1,0:T(8,128)(2,1)S(1)}, u32[]{:S(2)}, u32[]{:S(2)}) collective-permute-start(bf16[2,128,512]{2,1,0:T(8,128)(2,1)} %bitcast.10), channel_id=1, source_target_pairs={{0,2},{1,3},{2,0},{3,1},{4,6},{5,7},{6,4},{7,5},{8,10},{9,11},{10,... | collective-permute-start | bytes 786440 | tf_op jit(solution)/shard_map/ppermute | solution.py:22
  2.9 11.0 %collective-permute-start = (bf16[2,128,512]{2,1,0:T(8,128)(2,1)}, bf16[2,128,512]{2,1,0:T(8,128)(2,1)S(1)}, u32[]{:S(2)}, u32[]{:S(2)}) collective-permute-start(bf16[2,128,512]{2,1,0:T(8,128)(2,1)} %bitcast.11), channel_id=1, source_target_pairs={{0,1},{1,0},{2,3},{3,2},{4,5},{5,4},{6,7},{7,6},{8,9},{9,8},{10,11... | collective-permute-start | bytes 786440 | tf_op jit(solution)/shard_map/ppermute | solution.py:22
  9.5 4.5 %collective-permute-start.2 = (bf16[2,128,512]{2,1,0:T(8,128)(2,1)S(1)}, bf16[2,128,512]{2,1,0:T(8,128)(2,1)S(1)}, u32[]{:S(2)}, u32[]{:S(2)}) collective-permute-start(bf16[2,128,512]{2,1,0:T(8,128)(2,1)S(1)} %collective-permute-done.1.p2_ref), channel_id=1, source_target_pairs={{0,1},{1,0},{2,3},{3,2},{4,5},{5,4},{6,7},{7,6},{8,9},{9,8},{10,11... | collective-permute-start | bytes 786440 | tf_op jit(solution)/shard_map/ppermute | solution.py:22
  11.1 0.7 %copy-start.3 = (f32[512]{0:T(512)S(1)}, f32[512]{0:T(512)}, u32[]{:S(2)}) copy-start(f32[512]{0:T(512)} %param.8) | copy-start | bytes 6148
  13.9 1.0 %copy-start.1 = (bf16[1,2,128,512]{3,2,1,0:T(8,128)(2,1)S(1)}, bf16[1,2,128,512]{3,2,1,0:T(8,128)(2,1)}, u32[]{:S(2)}) copy-start(bf16[1,2,128,512]{3,2,1,0:T(8,128)(2,1)} %param.7) | copy-start | bytes 786436
  15.9 6.1 %copy-start.2 = (bf16[2,256,64]{1,2,0:T(8,128)(2,1)S(1)}, bf16[2,256,64]{1,2,0:T(8,128)(2,1)}, u32[]{:S(2)}) copy-start(bf16[2,256,64]{1,2,0:T(8,128)(2,1)} %param.11) | copy-start | bytes 196612
  16.6 9.4 %collective-permute-start.11 = (s16[272,256]{1,0:T(8,128)(2,1)S(1)}, s16[272,256]{1,0:T(8,128)(2,1)S(1)}, u32[]{:S(2)}, u32[]{:S(2)}) collective-permute-start(s16[272,256]{1,0:T(8,128)(2,1)S(1)} %send_first.1), channel_id=1, source_target_pairs={{0,4},{4,0},{8,12},{12,8},{16,20},{20,16},{24,28},{28,24},{1,5},{5... | collective-permute-start | bytes 417800 | tf_op jit(solution)/shard_map/ppermute | solution.py:22
  19.7 8.6 %collective-permute-start.9 = (s16[272,256]{1,0:T(8,128)(2,1)S(1)}, s16[272,256]{1,0:T(8,128)(2,1)S(1)}, u32[]{:S(2)}, u32[]{:S(2)}) collective-permute-start(s16[272,256]{1,0:T(8,128)(2,1)S(1)} %get-tuple-element.70), channel_id=1, source_target_pairs={{0,4},{4,0},{8,12},{12,8},{16,20},{20,16},{24,28},{28,24},{1,5},{5... | collective-permute-start | bytes 417800 | tf_op jit(solution)/shard_map/ppermute | solution.py:22
  20.0 9.5 %collective-permute-start.7 = (s16[272,256]{1,0:T(8,128)(2,1)S(1)}, s16[272,256]{1,0:T(8,128)(2,1)S(1)}, u32[]{:S(2)}, u32[]{:S(2)}) collective-permute-start(s16[272,256]{1,0:T(8,128)(2,1)S(1)} %get-tuple-element.64), channel_id=1, source_target_pairs={{0,4},{4,0},{8,12},{12,8},{16,20},{20,16},{24,28},{28,24},{1,5},{5... | collective-permute-start | bytes 417800 | tf_op jit(solution)/shard_map/ppermute | solution.py:22
  21.8 10.5 %collective-permute-start.3 = (s16[272,256]{1,0:T(8,128)(2,1)S(1)}, s16[272,256]{1,0:T(8,128)(2,1)S(1)}, u32[]{:S(2)}, u32[]{:S(2)}) collective-permute-start(s16[272,256]{1,0:T(8,128)(2,1)S(1)} %get-tuple-element.46), channel_id=1, source_target_pairs={{0,4},{4,0},{8,12},{12,8},{16,20},{20,16},{24,28},{28,24},{1,5},{5... | collective-permute-start | bytes 417800 | tf_op jit(solution)/shard_map/ppermute | solution.py:22
  22.1 12.6 %collective-permute-start.5 = (bf16[128,256]{1,0:T(8,128)(2,1)S(1)}, bf16[128,256]{1,0:T(8,128)(2,1)S(1)}, u32[]{:S(2)}, u32[]{:S(2)}) collective-permute-start(bf16[128,256]{1,0:T(8,128)(2,1)S(1)} %bitcast.13), channel_id=1, source_target_pairs={{0,4},{4,0},{8,12},{12,8},{16,20},{20,16},{24,28},{28,24},{1,5},{5... | collective-permute-start | bytes 196616 | tf_op jit(solution)/shard_map/ppermute | solution.py:22
  26.7 20.1 %collective-permute-start.12 = (s16[272,256]{1,0:T(8,128)(2,1)S(1)}, s16[272,256]{1,0:T(8,128)(2,1)S(1)}, u32[]{:S(2)}, u32[]{:S(2)}) collective-permute-start(s16[272,256]{1,0:T(8,128)(2,1)S(1)} %get-tuple-element.76), channel_id=1, source_target_pairs={{0,8},{4,12},{8,0},{12,4},{16,24},{20,28},{24,16},{28,20},{1,9},{5... | collective-permute-start | bytes 417800 | tf_op jit(solution)/shard_map/ppermute | solution.py:22
  29.0 19.1 %collective-permute-start.10 = (s16[272,256]{1,0:T(8,128)(2,1)S(1)}, s16[272,256]{1,0:T(8,128)(2,1)S(1)}, u32[]{:S(2)}, u32[]{:S(2)}) collective-permute-start(s16[272,256]{1,0:T(8,128)(2,1)S(1)} %get-tuple-element.71), channel_id=1, source_target_pairs={{0,8},{4,12},{8,0},{12,4},{16,24},{20,28},{24,16},{28,20},{1,9},{5... | collective-permute-start | bytes 417800 | tf_op jit(solution)/shard_map/ppermute | solution.py:22
  30.3 19.3 %collective-permute-start.8 = (s16[272,256]{1,0:T(8,128)(2,1)S(1)}, s16[272,256]{1,0:T(8,128)(2,1)S(1)}, u32[]{:S(2)}, u32[]{:S(2)}) collective-permute-start(s16[272,256]{1,0:T(8,128)(2,1)S(1)} %get-tuple-element.65), channel_id=1, source_target_pairs={{0,8},{4,12},{8,0},{12,4},{16,24},{20,28},{24,16},{28,20},{1,9},{5... | collective-permute-start | bytes 417800 | tf_op jit(solution)/shard_map/ppermute | solution.py:22
  33.0 18.0 %collective-permute-start.4 = (s16[272,256]{1,0:T(8,128)(2,1)S(1)}, s16[272,256]{1,0:T(8,128)(2,1)S(1)}, u32[]{:S(2)}, u32[]{:S(2)}) collective-permute-start(s16[272,256]{1,0:T(8,128)(2,1)S(1)} %get-tuple-element.53), channel_id=1, source_target_pairs={{0,8},{4,12},{8,0},{12,4},{16,24},{20,28},{24,16},{28,20},{1,9},{5... | collective-permute-start | bytes 417800 | tf_op jit(solution)/shard_map/ppermute | solution.py:22
  34.7 8.9 %collective-permute-start.6 = (bf16[2,128,256]{2,1,0:T(8,128)(2,1)S(1)}, bf16[2,128,256]{2,1,0:T(8,128)(2,1)S(1)}, u32[]{:S(2)}, u32[]{:S(2)}) collective-permute-start(bf16[2,128,256]{2,1,0:T(8,128)(2,1)S(1)} %pad_maximum_fusion), channel_id=1, source_target_pairs={{0,8},{4,12},{8,0},{12,4},{16,24},{20,28},{24,16},{28,20},{1,9},{5... | collective-permute-start | bytes 393224 | tf_op jit(solution)/shard_map/ppermute | solution.py:22

commit v2 on v1

--- a/solution.py
+++ b/solution.py
@@ -9,7 +9,7 @@
 WAVENUM = 0.7
 BF = jnp.bfloat16
 F32 = jnp.float32
-CHUNKS = (128, 128, 128, 128)
+SHARES = (10, 12, 10)
 TOP = 32766.0
 STEPS = 128.0
 VMEM = pl.BlockSpec(memory_space=pltpu.VMEM)
@@ -22,7 +22,7 @@
     return lax.ppermute(value, axis, [(s, s ^ mask) for s in range(lax.axis_size(axis))])
 
 
-def call(body, name, outs, ins, specs=None, scratch=(), **kw):
+def call(body, name, outs, ins, specs=None, scratch=(), cost=1.0, **kw):
     return pl.pallas_call(
         body,
         name=name,
@@ -31,6 +31,7 @@
         out_specs=kw.pop("out_specs", [VMEM] * len(outs)),
         scratch_shapes=list(scratch),
         compiler_params=PARAMS,
+        cost_estimate=pl.CostEstimate(flops=int(cost * 1e9), bytes_accessed=int(cost * 3e6), transcendentals=0),
         **kw,
     )(*ins)
 
@@ -90,26 +91,39 @@
     )
 
 
-def plan_body(at_ref, ranks_ref, skel_ref, contrast_ref, e0_ref, e1_ref, q_ref, ghi_ref, glo_ref, g1_ref, j_ref, d_ref):
-    box = at_ref[0]
-    kmax = skel_ref.shape[1]
+def open_body(out_ref):
+    out_ref[...] = jnp.zeros(out_ref.shape, out_ref.dtype)
+
+
+def plan_body(ranks_ref, skel_ref, contrast_ref, own_ref, beside_ref, dep_ref, *refs, parts):
+    e0_ref, er_ref, e1_ref, q_ref, ghi_ref, glo_ref, g1_ref, j_ref, d_ref, part_ref = refs
+    box = lax.axis_index("box")
+    me = lax.axis_index("field")
+    kmax = skel_ref.shape[2]
     width = contrast_ref.shape[1]
     contrast = contrast_ref[...]
+    ranks = ranks_ref[...].astype(F32)
+    ranks = jnp.sum(jnp.where(iota(ranks.shape, 1) == box, ranks, 0.0), axis=1, keepdims=True).astype(jnp.int32)
     rows = []
     cols = []
     rank = []
     for level in range(2):
         far = box ^ (1 << level)
-        own_row = skel_ref[pl.ds(box * 2 + level, 1), :]
-        far_row = skel_ref[pl.ds(far * 2 + level, 1), :]
+        own_row = skel_ref[box][level : level + 1, :]
+        far_row = skel_ref[far][level : level + 1, :]
         own_col = to_column(own_row.astype(F32)).astype(jnp.int32)
         far_col = to_column(far_row.astype(F32)).astype(jnp.int32)
-        r = ranks_ref[box * 2 + level]
+        r = ranks[level : level + 1, :]
         rows.append(own_row)
         cols.append(own_col)
         rank.append(r)
         hit = (own_col == iota((kmax, width), 1)) & (iota((kmax, width), 0) < r)
         (e0_ref, e1_ref)[level][...] = hit.astype(F32).astype(BF)
+        if level == 0:
+            n = width // parts
+            lane = iota((kmax, width), 1)
+            turned = (((lane // n) ^ me) * n) + lane % n
+            er_ref[...] = ((own_col == turned) & (iota((kmax, width), 0) < r)).astype(F32).astype(BF)
         q_col = jnp.sum(jnp.where(hit, contrast, 0.0), axis=1, keepdims=True)
         q_ref[pl.ds(level, 1), :] = to_row(q_col, kmax)
         ox, oy, oz = place(own_row, box)
@@ -138,10 +152,19 @@
     other = iota((kmax, kmax), 1)
     j_ref[...] = ((cols[0] == rows[1]) & (mine < rank[0]) & (other < rank[1])).astype(F32).astype(BF)
     d_ref[...] = ((cols[1] == rows[1]) & (mine < rank[1]) & (other < rank[1])).astype(F32).astype(BF)
-
-
-def core_body(at_ref, own_ref, near_ref, far_ref, g1_ref, d_ref, mc_ref, khi_ref, klo_ref, ct_ref):
-    slot = at_ref[0] & 3
+    n = own_ref.shape[1]
+    both = jnp.concatenate(
+        [
+            jnp.concatenate([own_ref[0], own_ref[1]], axis=1),
+            jnp.concatenate([beside_ref[0], beside_ref[1]], axis=1),
+        ],
+        axis=0,
+    )
+    part_ref[...] = nn(er_ref[:, : 2 * n], both).astype(BF)
+
+
+def core_body(own_ref, near_ref, far_ref, g1_ref, d_ref, dep_ref, mc_ref, khi_ref, klo_ref, ct_ref):
+    slot = lax.axis_index("box") & 3
     quarter = own_ref.shape[0] // 2
     kmax = own_ref.shape[1]
     pieces = (own_ref[...], near_ref[...], far_ref[0], far_ref[1])
@@ -175,35 +198,68 @@
         ref[kmax:, kmax:] = a
 
 
-def rows_body(at_ref, p0_ref, p1_ref, p2_ref, p3_ref, e_ref, a_ref, b_ref):
-    me = at_ref[1]
+def relay_body(in_ref, *rest):
+    rest[-1][...] = in_ref[...]
+
+
+def pair_body(a_ref, b_ref, dep_ref, out_ref):
+    out_ref[0] = a_ref[...]
+    out_ref[1] = b_ref[...]
+
+
+def turned_fields(x_ref, start, n):
+    re = x_ref[0, start : start + n]
+    im = x_ref[1, start : start + n]
+    return jnp.concatenate([re, -im], axis=1), jnp.concatenate([im, re], axis=1)
+
+
+def send(x_ref, picked, q_ref, out_ref, start, n):
+    q = q_ref[0:1, :]
+    left, right = turned_fields(x_ref, start, n)
+    w = jnp.concatenate([nt(left, picked) * q, nt(right, picked) * q], axis=1)
+    pack(w, out_ref)
+
+
+def first_body(part_ref, across_ref, beyond_ref, er_ref, x_ref, q_ref, *outs, start, n):
+    picked_ref, out_ref = outs
+    rows = across_ref.shape[1]
+    both = jnp.concatenate(
+        [
+            jnp.concatenate([across_ref[0], across_ref[1]], axis=1),
+            jnp.concatenate([beyond_ref[0], beyond_ref[1]], axis=1),
+        ],
+        axis=0,
+    )
+    picked = (nn(er_ref[:, 2 * rows :], both) + part_ref[...].astype(F32)).astype(BF)
+    picked_ref[...] = picked
+    send(x_ref, picked, q_ref, out_ref, start, n)
+
+
+def rest_body(x_ref, picked_ref, q_ref, dep_ref, out_ref, *, start, n):
+    send(x_ref, picked_ref[...], q_ref, out_ref, start, n)
+
+
+def rows_body(x_ref, p0_ref, p1_ref, p2_ref, p3_ref, e_ref, v_ref, a_ref):
+    width = x_ref.shape[2]
+    kmax = e_ref.shape[0]
+    me = lax.axis_index("field")
     n = p0_ref.shape[1]
-    width = p0_ref.shape[2]
-    kmax = e_ref.shape[0]
     for mask, ref in enumerate((p0_ref, p1_ref, p2_ref, p3_ref)):
         start = pl.multiple_of((me ^ mask) * n, n)
         a_ref[pl.ds(start, n), 0:width] = ref[0]
         a_ref[pl.ds(start, n), width:] = ref[1]
+    left, right = turned_fields(x_ref, 0, x_ref.shape[1])
     picked = nn(e_ref[...], a_ref[...]).astype(BF)
-    re = picked[:, :width]
-    im = picked[:, width:]
-    b_ref[0:kmax, 0:width] = re
-    b_ref[0:kmax, width:] = -im
-    b_ref[kmax:, 0:width] = im
-    b_ref[kmax:, width:] = re
-
-
-def leaf_body(x_ref, a_ref, e_ref, y_ref, v_ref):
+    v_ref[:, 0:kmax] = nt(left, picked)
+    v_ref[:, kmax:] = nt(right, picked)
+
+
+def leaf_body(x_ref, a_ref, dep_ref, y_ref):
     width = x_ref.shape[2]
-    kmax = e_ref.shape[0]
-    x = jnp.concatenate([x_ref[0], x_ref[1]], axis=1)
-    xs = jnp.concatenate([-x_ref[1], x_ref[0]], axis=1)
+    left, right = turned_fields(x_ref, 0, x_ref.shape[1])
     a = a_ref[...]
-    y_ref[:, 0:width] = nt(jnp.concatenate([x_ref[0], -x_ref[1]], axis=1), a)
-    y_ref[:, width:] = nt(jnp.concatenate([x_ref[1], x_ref[0]], axis=1), a)
-    picked = nn(e_ref[...], a).astype(BF)
-    v_ref[:, 0:kmax] = nt(jnp.concatenate([x_ref[0], -x_ref[1]], axis=1), picked)
-    v_ref[:, kmax:] = nt(jnp.concatenate([x_ref[1], x_ref[0]], axis=1), picked)
+    y_ref[:, 0:width] = nt(left, a)
+    y_ref[:, width:] = nt(right, a)
 
 
 def pack(w, out_ref):
@@ -231,15 +287,8 @@
     return (nn(upper, mhi) + (nn(lower, mhi) + nn(upper, mlo))) * scale
 
 
-def first_body(x_ref, b_ref, q_ref, *outs, parts):
-    q = q_ref[0:1, :]
-    q = jnp.concatenate([q, q], axis=1)
-    for ref, (start, n) in zip(outs, parts):
-        x = jnp.concatenate([x_ref[0, start : start + n], x_ref[1, start : start + n]], axis=1)
-        pack(nt(x, b_ref[...]) * q, ref)
-
-
-def second_body(in_ref, ghi_ref, glo_ref, v_ref, j_ref, q_ref, out_ref, gs_ref, us_ref, *, start):
+def second_body(in_ref, ghi_ref, glo_ref, v_ref, j_ref, q_ref, *rest, start):
+    out_ref, gs_ref, us_ref = rest[-3:]
     n = (in_ref.shape[0] - 16) // 2
     k = in_ref.shape[1]
     g = apply_packed(in_ref, ghi_ref[...], glo_ref[...])
@@ -271,20 +320,27 @@
     p_ref[...] = nn(us_ref[0], mc) + nn(us_ref[1], mc)
 
 
-def fourth_body(in_ref, khi_ref, klo_ref, part_ref, p_ref, e1_ref, *rest, start):
-    out_ref, hold_ref, sem = rest[-3:]
-    n = part_ref.shape[1]
+def fourth_body(*refs, parts):
+    khi_ref, klo_ref, e1_ref = refs[:3]
+    chunks = refs[3 : 3 + 3 * len(parts)]
+    out_ref, hold_ref, sem = refs[-3:]
+    base = parts[0][0]
+    e = e1_ref[...]
+    khi = khi_ref[...]
+    klo = klo_ref[...]
     k = e1_ref.shape[0]
-    p = p_ref[...] + apply_packed(in_ref, khi_ref[...], klo_ref[...])
-    hi, lo = halves(p)
-    e = e1_ref[...]
     copies = []
-    for i in range(2):
-        cols = slice(i * k, i * k + k)
-        hold_ref[i] = part_ref[i] - (nn(hi[:, cols], e) + nn(lo[:, cols], e))
-        copy = pltpu.make_async_copy(hold_ref.at[i], out_ref.at[i, pl.ds(start, n), :], sem.at[i])
-        copy.start()
-        copies.append(copy)
+    for c, (start, n) in enumerate(parts):
+        in_ref, part_ref, p_ref = chunks[3 * c : 3 * c + 3]
+        p = p_ref[...] + apply_packed(in_ref, khi, klo)
+        hi, lo = halves(p)
+        for i in range(2):
+            cols = slice(i * k, i * k + k)
+            spot = pl.ds(start - base, n)
+            hold_ref[i, spot] = part_ref[i] - (nn(hi[:, cols], e) + nn(lo[:, cols], e))
+            copy = pltpu.make_async_copy(hold_ref.at[i, spot], out_ref.at[i, pl.ds(start, n), :], sem.at[2 * c + i])
+            copy.start()
+            copies.append(copy)
     for copy in copies:
         copy.wait()
 
@@ -293,17 +349,18 @@
     nf, width = incident.shape[1:]
     boxes, _, kmax = skel_index.shape
     quarter = top_core.shape[2]
-    at = jnp.stack([lax.axis_index("box"), lax.axis_index("field")]).astype(jnp.int32)
     own = leaf_inverse[0]
     across = swap(own, "field", 2)
     beside = swap(own, "field", 1)
     core_own = jnp.swapaxes(top_core, 1, 2).reshape(2 * quarter, kmax)
     core_near = swap(core_own, "box", 1)
-    core_far = swap(jnp.stack([core_own, core_near]), "box", 2)
-    e0, e1, q, ghi, glo, g1, dup01, dup11 = call(
-        plan_body,
+    n = own.shape[1]
+    (opened,) = call(open_body, "open", [shape(8, 128)], [], cost=4.0)
+    e0, er, e1, q, ghi, glo, g1, dup01, dup11, part = call(
+        lambda *refs: plan_body(*refs, parts=lax.axis_size("field")),
         "plan",
         [
+            shape(kmax, width, dtype=BF),
             shape(kmax, width, dtype=BF),
             shape(kmax, width, dtype=BF),
             shape(8, kmax),
@@ -312,68 +369,122 @@
             shape(kmax, 2 * kmax),
             shape(kmax, kmax, dtype=BF),
             shape(kmax, kmax, dtype=BF),
+            shape(kmax, 2 * width, dtype=BF),
         ],
-        [at, ranks.reshape(-1), skel_index.reshape(boxes * 2, kmax), contrast.reshape(1, width)],
-        [SMEM, SMEM, VMEM, VMEM],
+        [ranks.T, skel_index, contrast.reshape(1, width), own, beside, opened],
+        [VMEM] * 5 + [ANY],
+    )
+    x = incident
+    (pair,) = call(
+        pair_body, "pair", [shape(2, 2 * quarter, kmax, dtype=BF)], [core_own, core_near, part], [VMEM, VMEM, ANY], cost=0.05
+    )
+    core_far = swap(pair, "box", 2)
+    (across,) = call(
+        relay_body, "relay", [shape(*across.shape, dtype=BF)], [across, pair], [VMEM, ANY], cost=0.05
     )
     beyond = swap(across, "field", 1)
-    a_all, b0 = call(
+    chunks = [nf // sum(SHARES) * share for share in SHARES]
+    sizes = [(sum(chunks[:i]), n) for i, n in enumerate(chunks)]
+    start, n = sizes[0]
+    picked, head = call(
+        lambda *refs, start=start, n=n: first_body(*refs, start=start, n=n),
+        "first",
+        [
+            shape(kmax, 2 * width, dtype=BF),
+            shape(2 * n + 16, kmax, dtype=jnp.int16),
+        ],
+        [part, across, beyond, er, x, q],
+        cost=0.8,
+    )
+
+    def ready(i, dep):
+        start, n = sizes[i]
+        (packed,) = call(
+            lambda *refs: rest_body(*refs, start=start, n=n),
+            f"ready{i}",
+            [shape(2 * n + 16, kmax, dtype=jnp.int16)],
+            [x, picked, q, dep],
+            [VMEM] * 3 + [ANY],
+            cost=0.6,
+        )
+        return swap(packed, "box", 1)
+
+    got = swap(head, "box", 1)
+    v1, a_all = call(
         rows_body,
         "rows",
-        [shape(width, 2 * width, dtype=BF), shape(2 * kmax, 2 * width, dtype=BF)],
-        [at, own, beside, across, beyond, e0],
-        [SMEM] + [VMEM] * 5,
-    )
-    starts = [sum(CHUNKS[:i]) for i in range(len(CHUNKS))]
-    sizes = list(zip(starts, CHUNKS))
-    packed = []
-    for name, parts in (("send_first", sizes[:1]), ("send_rest", sizes[1:])):
-        packed += call(
-            lambda *refs, parts=parts: first_body(*refs, parts=parts),
-            name,
-            [shape(2 * n + 16, kmax, dtype=jnp.int16) for _, n in parts],
-            [incident, b0, q],
-        )
-    got = [swap(v, "box", 1) for v in packed]
-    y, v1 = call(leaf_body, "leaf", [shape(nf, 2 * width), shape(nf, 2 * kmax)], [incident, a_all, e1])
-    mc, khi, klo = call(
-        core_body,
-        "core",
-        [shape(2 * kmax, 2 * kmax, dtype=BF)] * 3,
-        [at, core_own, core_near, core_far, g1, dup11],
-        [SMEM] + [VMEM] * 5,
-        [pltpu.VMEM((kmax, 2 * kmax), BF)],
-    )
-    out = None
+        [shape(nf, 2 * kmax), shape(width, 2 * width, dtype=BF)],
+        [x, own, beside, across, beyond, e1],
+    )
     late = []
+    coming = ready(1, q)
+
+    def core(dep):
+        return call(
+            core_body,
+            "core",
+            [shape(2 * kmax, 2 * kmax, dtype=BF)] * 3,
+            [core_own, core_near, core_far, g1, dup11, dep],
+            [VMEM] * 5 + [ANY],
+            [pltpu.VMEM((kmax, 2 * kmax), BF)],
+        )
+
+    def third(i):
+        start, n = sizes[i]
+        late[i][1:] = call(
+            lambda *refs, start=start: third_body(*refs, start=start),
+            f"third{i}",
+            [shape(2, n, width), shape(n, 2 * kmax)],
+            [late[i][1], late[i][2], y, e0, mc],
+            cost=0.5,
+        )
+
     for i, (start, n) in enumerate(sizes):
-        send, gs, us = call(
+        dep = e1
+        if i == 1 and 1:
+            dep = mc
+        if i == 2 and 2:
+            dep = mc if 2 == 1 else late[2 - 2][2]
+        back, gs, us = call(
             lambda *refs, start=start: second_body(*refs, start=start),
             f"second{i}",
             [shape(2 * n + 16, kmax, dtype=jnp.int16), shape(2, n, 2 * kmax, dtype=BF), shape(2, n, 2 * kmax, dtype=BF)],
-            [got[i], ghi, glo, v1, dup01, q],
-        )
-        back = swap(send, "box", 2)
-        part, p = call(
-            lambda *refs, start=start: third_body(*refs, start=start),
-            f"third{i}",
-            [shape(2, n, width), shape(n, 2 * kmax)],
-            [gs, us, y, e0, mc],
-        )
-        late.append((back, part, p))
-    for i, (start, n) in enumerate(sizes):
-        back, part, p = late[i]
-        ins = [back, khi, klo, part, p, e1] + ([] if out is None else [out])
-        specs = [VMEM] * 6 + ([] if out is None else [ANY])
+            [got, ghi, glo, v1, dup01, q, dep],
+            [VMEM] * 6 + [ANY],
+            cost=0.8,
+        )
+        got = coming
+        if 0:
+            late.append([swap(back, "box", 2), gs, us])
+        if i + 2 < len(sizes):
+            coming = ready(i + 2, gs)
+        if not 0:
+            late.append([swap(back, "box", 2), gs, us])
+        if i == 0:
+            mc, khi, klo = core(gs)
+        if i == 1:
+            (y,) = call(leaf_body, "leaf", [shape(nf, 2 * width)], [x, a_all, late[0][0]], [VMEM, VMEM, ANY], cost=1.3)
+            for j in range(i + 1):
+                third(j)
+        if i > 1:
+            third(i)
+    out = None
+    for name, at in (("most", slice(0, -1)), ("last", slice(-1, None))):
+        parts = sizes[at]
+        ins = [khi, klo, e1] + [a for group in late[at] for a in group]
+        specs = [VMEM] * len(ins)
+        if out is not None:
+            ins.append(out)
+            specs.append(ANY)
         (out,) = call(
-            lambda *refs, start=start: fourth_body(*refs, start=start),
-            f"fourth{i}",
+            lambda *refs, parts=parts: fourth_body(*refs, parts=parts),
+            name,
             [shape(2, nf, width)],
             ins,
             specs,
-            [pltpu.VMEM((2, n, width), F32), pltpu.SemaphoreType.DMA((2,))],
+            [pltpu.VMEM((2, sum(n for _, n in parts), width), F32), pltpu.SemaphoreType.DMA((2 * len(parts),))],
             out_specs=[ANY],
-            input_output_aliases={} if out is None else {6: 0},
+            input_output_aliases={} if len(specs) == len(ins) and specs[-1] is VMEM else {len(ins) - 1: 0},
         )
     return out
 

time: 52.6 us -> 37.2 us (0.71)
  waiting for transfers between devices: 15.3 us -> 7.45 us
  Pallas kernels: 18.7 us -> 14.6 us
  local copies, waits for them, and re-layouts: 3.21 us -> 0.03 us
    ppermute x13 -> x11, waiting for transfers between devices: 15.3 us -> 7.45 us  [swap(): lax.ppermute(value, axis, [(s, s ^ mask) for s in range(lax.axis_size(axi...]
    pallas_call x18, Pallas kernels: 18.7 us -> 14.6 us  [call(): pl.pallas_call(body, name=name, out_shape=outs, in_specs=specs or [VMEM]...]
    unnamed x9 -> x12, local copies, waits for them, and re-layouts: 2.39 us -> 0.03 us
    reshape x2 -> x0, local copies, waits for them, and re-layouts: 0.82 us -> none  [the longest x1 0.73 us: body(): skel_index.reshape(boxes * 2, kmax)]
    ppermute x13 -> x11, starting transfers between devices: 14.9 us -> 14.9 us  [swap(): lax.ppermute(value, axis, [(s, s ^ mask) for s in range(lax.axis_size(axi...]
  transfers between devices with their start and end apart: 13 -> 11, of which waited for: 3 -> 6; matrix products, arithmetic and copies ran while one was open for 3% -> 0% of each run, Pallas kernels for 30% -> 33%
where the time goes in v2:
time: 37.2 us; the launch traced here: 37.1 us
  starting transfers between devices  14.9 us (40%)
  Pallas kernels  14.6 us (39%)
  waiting for transfers between devices  7.45 us (20%)
    ppermute x11, starting transfers between devices, swap(): lax.ppermute(value, axis, [(s, s ^ mask) for s in range(lax.axis_size(axi...  14.9 us
    pallas_call x18, Pallas kernels, call(): pl.pallas_call(body, name=name, out_shape=outs, in_specs=specs or [VMEM]...  14.6 us
    ppermute x11, waiting for transfers between devices, swap(): lax.ppermute(value, axis, [(s, s ^ mask) for s in range(lax.axis_size(axi...  7.45 us
  transfers between devices with their start and end apart: 11, of which 6 were waited for; matrix products, arithmetic and copies ran while one was open for 0% of the time, Pallas kernels for 33%

profile of v2, /device:TPU:0, one launch (start us, length us, event | category | flops | bytes accessed | tf_op | source)
XLA Modules:
  0.0 37.1 jit_solution(2271169846927769638)
XLA Ops:
  0.0 2.9 %collective-permute-start.3 = (bf16[2,128,512]{2,1,0:T(8,128)(2,1)}, bf16[2,128,512]{2,1,0:T(8,128)(2,1)S(1)}, u32[]{:S(2)}, u32[]{:S(2)}) collective-permute-start(bf16[2,128,512]{2,1,0:T(8,128)(2,1)} %bitcast.9), channel_id=1, source_target_pairs={{0,2},{1,3},{2,0},{3,1},{4,6},{5,7},{6,4},{7,5},{8,10},{9,11},{10,... | collective-permute-start | bytes 786440 | tf_op jit(solution)/shard_map/ppermute | solution.py:22
  2.9 0.0 collective-permute-start.1
  2.9 0.0 copy-start.2
  2.9 0.0 copy-start.3
  2.9 0.0 copy-start.4
  3.0 0.0 copy-start.5
  3.0 1.6 %collective-permute-start = (bf16[128,256]{1,0:T(8,128)(2,1)}, bf16[128,256]{1,0:T(8,128)(2,1)S(1)}, u32[]{:S(2)}, u32[]{:S(2)}) collective-permute-start(bf16[128,256]{1,0:T(8,128)(2,1)} %bitcast.6), channel_id=1, source_target_pairs={{0,4},{4,0},{8,12},{12,8},{16,20},{20,16},{24,28},{28,24},{1,5},{5... | collective-permute-start | bytes 196616 | tf_op jit(solution)/shard_map/ppermute | solution.py:22
  4.6 0.1 collective-permute-done.1.refs_4_.p1_ref
  4.7 0.0 copy-done.2
  4.7 0.0 copy-done.3
  4.7 0.0 copy-done.4
  4.7 0.0 copy-done.5
  4.7 0.0 copy-start.1
  4.7 1.7 %plan.1 = (bf16[256,512]{1,0:T(8,128)(2,1)S(1)}, bf16[256,512]{1,0:T(8,128)(2,1)S(1)}, bf16[256,512]{1,0:T(8,128)(2,1)S(1)}, f32[8,256]{1,0:T(8,128)S(1)}, bf16[...) custom-call(s32[2,8]{1,0:T(2,128)S(1)} %bitcast.14, ...), custom_call_target="tpu_custom_call" | custom-call | flops 1000000000 | bytes 3000000 | tf_op jit(solution)/shard_map/plan/pallas_call | solution.py:26
  6.4 1.3 %collective-permute-done.b_ref.near_ref = bf16[128,256]{1,0:T(8,128)(2,1)S(1)} collective-permute-done((bf16[128,256]{1,0:T(8,128)(2,1)}, bf16[128,256]{1,0:T(8,128)(2,1)S(1)}, u32[]{:S(2)}, u32[]{:S(2)}) %collective-permute-start) | collective-permute-done | bytes 65568 | tf_op jit(solution)/shard_map/ppermute | solution.py:22
  7.7 0.0 copy-done
  7.8 1.7 %collective-permute-done.3.in_ref = bf16[2,128,512]{2,1,0:T(8,128)(2,1)S(1)} collective-permute-done((bf16[2,128,512]{2,1,0:T(8,128)(2,1)}, bf16[2,128,512]{2,1,0:T(8,128)(2,1)S(1)}, u32[]{:S(2)}, u32[]{:S(2)}) %collective-permute-start.3) | collective-permute-done | bytes 262176 | tf_op jit(solution)/shard_map/ppermute | solution.py:22
  9.5 0.1 collective-permute-start.4
  9.6 1.5 %collective-permute-done.4.refs_2_.p3_ref = bf16[2,128,512]{2,1,0:T(8,128)(2,1)S(1)} collective-permute-done((bf16[2,128,512]{2,1,0:T(8,128)(2,1)S(1)}, bf16[2,128,512]{2,1,0:T(8,128)(2,1)S(1)}, u32[]{:S(2)}, u32[]{:S(2)}) %collective-permute-start.4) | collective-permute-done | bytes 262176 | tf_op jit(solution)/shard_map/ppermute | solution.py:22
  11.1 0.0 copy-done.1
  11.1 0.8 %first.1 = (bf16[256,1024]{1,0:T(8,128)(2,1)S(1)}, s16[336,256]{1,0:T(8,128)(2,1)S(1)}) custom-call(bf16[256,1024]{1,0:T(8,128)(2,1)S(1)} %get-tuple-element.37.dep_ref.refs_0_, bf16[2,128,512]{2,1,0:T(8,128)(2,1)S(1)} %relay.1.refs_1_.p2_ref, bf16[2,128,512]{2,1,0:T(8,128)(2,1)S(1)} %collective-permute-done.4.refs_2_.p3_ref, ...), custom_call_target="tpu_custom_call" | custom-call | flops 800000000 | bytes 2400000 | tf_op jit(solution)/shard_map/first/pallas_call | solution.py:26
  11.9 1.8 %collective-permute-start.5 = (s16[336,256]{1,0:T(8,128)(2,1)S(1)}, s16[336,256]{1,0:T(8,128)(2,1)S(1)}, u32[]{:S(2)}, u32[]{:S(2)}) collective-permute-start(s16[336,256]{1,0:T(8,128)(2,1)S(1)} %get-tuple-element.42), channel_id=1, source_target_pairs={{0,4},{4,0},{8,12},{12,8},{16,20},{20,16},{24,28},{28,24},{1,5},{5... | collective-permute-start | bytes 516104 | tf_op jit(solution)/shard_map/ppermute | solution.py:22
  13.7 1.6 %collective-permute-start.2 = (bf16[2,128,256]{2,1,0:T(8,128)(2,1)S(1)}, bf16[2,128,256]{2,1,0:T(8,128)(2,1)S(1)}, u32[]{:S(2)}, u32[]{:S(2)}) collective-permute-start(bf16[2,128,256]{2,1,0:T(8,128)(2,1)S(1)} %pair.1.rest_0_), channel_id=1, source_target_pairs={{0,8},{4,12},{8,0},{12,4},{16,24},{20,28},{24,16},{28,20},{1,9},{5... | collective-permute-start | bytes 393224 | tf_op jit(solution)/shard_map/ppermute | solution.py:22
  15.3 0.6 %ready1.1 = s16[400,256]{1,0:T(8,128)(2,1)S(1)} custom-call(bf16[2,512,512]{2,1,0:T(8,128)(2,1)S(1)} %copy-done.1, bf16[256,1024]{1,0:T(8,128)(2,1)S(1)} %get-tuple-element.51.refs_1_, f32[8,256]{1,0:T(8,128)S(1)} %get-tuple-element.41.refs_5_.refs_2_.refs_3_, f32[8,256]{1,0:T(8,128)S(1)} %get-tuple-element.41.refs_5_.refs_2_.refs_3_), custom_call_target="tpu_custom_call" | custom-call | flops 600000000 | bytes 1800000 | tf_op jit(solution)/shard_map/ready1/pallas_call | solution.py:26
  16.0 0.6 %collective-permute-start.9 = (s16[400,256]{1,0:T(8,128)(2,1)S(1)}, s16[400,256]{1,0:T(8,128)(2,1)S(1)}, u32[]{:S(2)}, u32[]{:S(2)}) collective-permute-start(s16[400,256]{1,0:T(8,128)(2,1)S(1)} %ready1.1), channel_id=1, source_target_pairs={{0,4},{4,0},{8,12},{12,8},{16,20},{20,16},{24,28},{28,24},{1,5},{5... | collective-permute-start | bytes 614408 | tf_op jit(solution)/shard_map/ppermute | solution.py:22
  16.5 1.1 %rows.1 = (f32[512,512]{1,0:T(8,128)S(1)}, bf16[512,1024]{1,0:T(8,128)(2,1)S(1)}) custom-call(bf16[2,512,512]{2,1,0:T(8,128)(2,1)S(1)} %copy-done.1, bf16[2,128,512]{2,1,0:T(8,128)(2,1)S(1)} %bitcast.12, bf16[2,128,512]{2,1,0:T(8,128)(2,1)S(1)} %collective-permute-done.1.refs_4_.p1_ref, bf16[2,128,512]{2,1,0:T(8,128)(2,1)S(1)} %relay.1.refs_1_.p2_ref, ...), custom_call_target="tpu_custom_call" | custom-call | flops 1000000000 | bytes 3000000 | tf_op jit(solution)/shard_map/rows/pallas_call | solution.py:26
  17.6 0.9 %collective-permute-done.5.refs_0_ = s16[336,256]{1,0:T(8,128)(2,1)S(1)} collective-permute-done((s16[336,256]{1,0:T(8,128)(2,1)S(1)}, s16[336,256]{1,0:T(8,128)(2,1)S(1)}, u32[]{:S(2)}, u32[]{:S(2)}) %collective-permute-start.5) | collective-permute-done | bytes 172064 | tf_op jit(solution)/shard_map/ppermute | solution.py:22
  18.5 0.8 %second0.1 = (s16[336,256]{1,0:T(8,128)(2,1)S(1)}, bf16[2,160,512]{2,1,0:T(8,128)(2,1)S(1)}, bf16[2,160,512]{2,1,0:T(8,128)(2,1)S(1)}) custom-call(s16[336,256]{1,0:T(8,128)(2,1)S(1)} %collective-permute-done.5.refs_0_, bf16[512,512]{1,0:T(8,128)(2,1)S(1)} %get-tuple-element.43.refs_1_, bf16[512,512]{1,0:T(8,128)(2,1)S(1)} %get-tuple-element.44.refs_2_, ...), custom_call_target="tpu_custom_call" | custom-call | flops 800000000 | bytes 2400000 | tf_op jit(solution)/shard_map/second0/pallas_call | solution.py:26
  19.3 2.5 %collective-permute-start.7 = (s16[336,256]{1,0:T(8,128)(2,1)S(1)}, s16[336,256]{1,0:T(8,128)(2,1)S(1)}, u32[]{:S(2)}, u32[]{:S(2)}) collective-permute-start(s16[336,256]{1,0:T(8,128)(2,1)S(1)} %get-tuple-element.54), channel_id=1, source_target_pairs={{0,8},{4,12},{8,0},{12,4},{16,24},{20,28},{24,16},{28,20},{1,9},{5... | collective-permute-start | bytes 516104 | tf_op jit(solution)/shard_map/ppermute | solution.py:22
  21.9 0.6 %ready2.1 = s16[336,256]{1,0:T(8,128)(2,1)S(1)} custom-call(bf16[2,512,512]{2,1,0:T(8,128)(2,1)S(1)} %copy-done.1, bf16[256,1024]{1,0:T(8,128)(2,1)S(1)} %get-tuple-element.51.refs_1_, f32[8,256]{1,0:T(8,128)S(1)} %get-tuple-element.41.refs_5_.refs_2_.refs_3_, bf16[2,160,512]{2,1,0:T(8,128)(2,1)S(1)} %get-tuple-element.48.dep_ref.refs_3_.refs_0_), custom_call_target="tpu_custom_call" | custom-call | flops 600000000 | bytes 1800000 | tf_op jit(solution)/shard_map/ready2/pallas_call | solution.py:26
  22.5 1.6 %collective-permute-start.6 = (s16[336,256]{1,0:T(8,128)(2,1)S(1)}, s16[336,256]{1,0:T(8,128)(2,1)S(1)}, u32[]{:S(2)}, u32[]{:S(2)}) collective-permute-start(s16[336,256]{1,0:T(8,128)(2,1)S(1)} %ready2.1), channel_id=1, source_target_pairs={{0,4},{4,0},{8,12},{12,8},{16,20},{20,16},{24,28},{28,24},{1,5},{5... | collective-permute-start | bytes 516104 | tf_op jit(solution)/shard_map/ppermute | solution.py:22
  24.1 0.0 collective-permute-done.2.far_ref
  24.1 0.8 %core.1 = (bf16[512,512]{1,0:T(8,128)(2,1)S(1)}, bf16[512,512]{1,0:T(8,128)(2,1)S(1)}, bf16[512,512]{1,0:T(8,128)(2,1)S(1)}) custom-call(bf16[128,256]{1,0:T(8,128)(2,1)S(1)} %bitcast.8, bf16[128,256]{1,0:T(8,128)(2,1)S(1)} %collective-permute-done.b_ref.near_ref, bf16[2,128,256]{2,1,0:T(8,128)(2,1)S(1)} %collective-permute-done.2.far_ref, ...), custom_call_target="tpu_custom_call" | custom-call | flops 1000000000 | bytes 3000000 | tf_op jit(solution)/shard_map/core/pallas_call | solution.py:26
  24.9 0.0 collective-permute-done.9.refs_0_
  24.9 0.9 %second1.1 = (s16[400,256]{1,0:T(8,128)(2,1)S(1)}, bf16[2,192,512]{2,1,0:T(8,128)(2,1)S(1)}, bf16[2,192,512]{2,1,0:T(8,128)(2,1)S(1)}) custom-call(s16[400,256]{1,0:T(8,128)(2,1)S(1)} %collective-permute-done.9.refs_0_, bf16[512,512]{1,0:T(8,128)(2,1)S(1)} %get-tuple-element.43.refs_1_, bf16[512,512]{1,0:T(8,128)(2,1)S(1)} %get-tuple-element.44.refs_2_, ...), custom_call_target="tpu_custom_call" | custom-call | flops 800000000 | bytes 2400000 | tf_op jit(solution)/shard_map/second1/pallas_call | solution.py:26
  25.8 0.6 %collective-permute-start.10 = (s16[400,256]{1,0:T(8,128)(2,1)S(1)}, s16[400,256]{1,0:T(8,128)(2,1)S(1)}, u32[]{:S(2)}, u32[]{:S(2)}) collective-permute-start(s16[400,256]{1,0:T(8,128)(2,1)S(1)} %get-tuple-element.64), channel_id=1, source_target_pairs={{0,8},{4,12},{8,0},{12,4},{16,24},{20,28},{24,16},{28,20},{1,9},{5... | collective-permute-start | bytes 614408 | tf_op jit(solution)/shard_map/ppermute | solution.py:22
  26.3 0.0 collective-permute-done.7.dep_ref.refs_3_
  26.3 1.3 %leaf.1.refs_2_ = f32[512,1024]{1,0:T(8,128)S(1)} custom-call(bf16[2,512,512]{2,1,0:T(8,128)(2,1)S(1)} %copy-done.1, bf16[512,1024]{1,0:T(8,128)(2,1)S(1)} %get-tuple-element.53.a_ref, s16[336,256]{1,0:T(8,128)(2,1)S(1)} %collective-permute-done.7.dep_ref.refs_3_), custom_call_target="tpu_custom_call" | custom-call | flops 1300000000 | bytes 3900000 | tf_op jit(solution)/shard_map/leaf/pallas_call | solution.py:26
  27.6 0.5 %third0.1 = (f32[2,160,512]{2,1,0:T(8,128)S(1)}, f32[160,512]{1,0:T(8,128)S(1)}) custom-call(bf16[2,160,512]{2,1,0:T(8,128)(2,1)S(1)} %get-tuple-element.48.dep_ref.refs_3_.refs_0_, bf16[2,160,512]{2,1,0:T(8,128)(2,1)S(1)} %get-tuple-element.52.refs_1_, f32[512,1024]{1,0:T(8,128)S(1)} %leaf.1.refs_2_, bf16[256,512]{1,0:T(8,128)(2,1)S(1)} %get-tuple-element.55.refs_3_, ...), custom_call_target="tpu_custom_call" | custom-call | flops 500000000 | bytes 1500000 | tf_op jit(solution)/shard_map/third0/pallas_call | solution.py:26
  28.1 0.0 collective-permute-done.6.refs_0_
  28.1 0.8 %second2.1 = (s16[336,256]{1,0:T(8,128)(2,1)S(1)}, bf16[2,160,512]{2,1,0:T(8,128)(2,1)S(1)}, bf16[2,160,512]{2,1,0:T(8,128)(2,1)S(1)}) custom-call(s16[336,256]{1,0:T(8,128)(2,1)S(1)} %collective-permute-done.6.refs_0_, bf16[512,512]{1,0:T(8,128)(2,1)S(1)} %get-tuple-element.43.refs_1_, bf16[512,512]{1,0:T(8,128)(2,1)S(1)} %get-tuple-element.44.refs_2_, ...), custom_call_target="tpu_custom_call" | custom-call | flops 800000000 | bytes 2400000 | tf_op jit(solution)/shard_map/second2/pallas_call | solution.py:26
  28.9 1.6 %collective-permute-start.8 = (s16[336,256]{1,0:T(8,128)(2,1)S(1)}, s16[336,256]{1,0:T(8,128)(2,1)S(1)}, u32[]{:S(2)}, u32[]{:S(2)}) collective-permute-start(s16[336,256]{1,0:T(8,128)(2,1)S(1)} %get-tuple-element.58), channel_id=1, source_target_pairs={{0,8},{4,12},{8,0},{12,4},{16,24},{20,28},{24,16},{28,20},{1,9},{5... | collective-permute-start | bytes 516104 | tf_op jit(solution)/shard_map/ppermute | solution.py:22
  30.5 0.6 %third1.1 = (f32[2,192,512]{2,1,0:T(8,128)S(1)}, f32[192,512]{1,0:T(8,128)S(1)}) custom-call(bf16[2,192,512]{2,1,0:T(8,128)(2,1)S(1)} %get-tuple-element.65.refs_0_, bf16[2,192,512]{2,1,0:T(8,128)(2,1)S(1)} %get-tuple-element.66.refs_1_, f32[512,1024]{1,0:T(8,128)S(1)} %leaf.1.refs_2_, bf16[256,512]{1,0:T(8,128)(2,1)S(1)} %get-tuple-element.55.refs_3_, ...), custom_call_target="tpu_custom_call" | custom-call | flops 500000000 | bytes 1500000 | tf_op jit(solution)/shard_map/third1/pallas_call | solution.py:26
  31.1 0.5 %third2.1 = (f32[2,160,512]{2,1,0:T(8,128)S(1)}, f32[160,512]{1,0:T(8,128)S(1)}) custom-call(bf16[2,160,512]{2,1,0:T(8,128)(2,1)S(1)} %get-tuple-element.59.refs_0_, bf16[2,160,512]{2,1,0:T(8,128)(2,1)S(1)} %get-tuple-element.60.refs_1_, f32[512,1024]{1,0:T(8,128)S(1)} %leaf.1.refs_2_, bf16[256,512]{1,0:T(8,128)(2,1)S(1)} %get-tuple-element.55.refs_3_, ...), custom_call_target="tpu_custom_call" | custom-call | flops 500000000 | bytes 1500000 | tf_op jit(solution)/shard_map/third2/pallas_call | solution.py:26
  31.6 1.8 %collective-permute-done.10.refs_6_ = s16[400,256]{1,0:T(8,128)(2,1)S(1)} collective-permute-done((s16[400,256]{1,0:T(8,128)(2,1)S(1)}, s16[400,256]{1,0:T(8,128)(2,1)S(1)}, u32[]{:S(2)}, u32[]{:S(2)}) %collective-permute-start.10) | collective-permute-done | bytes 204832 | tf_op jit(solution)/shard_map/ppermute | solution.py:22
  33.4 2.2 %most.1.refs_6_ = f32[2,512,512]{2,1,0:T(8,128)} custom-call(bf16[512,512]{1,0:T(8,128)(2,1)S(1)} %get-tuple-element.49.refs_0_, bf16[512,512]{1,0:T(8,128)(2,1)S(1)} %get-tuple-element.50.refs_1_, bf16[256,512]{1,0:T(8,128)(2,1)S(1)} %get-tuple-element.45.e_ref.refs_6_.refs_2_, s16[336,256]{1,0:T(8,128)(2,1)S(1)} %collective-permute-done.7.dep_ref.refs_3_, ...), custom_call_target="tpu_custom_call" | custom-call | flops 1000000000 | bytes 3000000 | tf_op jit(solution)/shard_map/most/pallas_call | solution.py:26
  35.6 0.0 collective-permute-done.8.refs_3_
  35.6 1.5 %last.1 = f32[2,512,512]{2,1,0:T(8,128)} custom-call(bf16[512,512]{1,0:T(8,128)(2,1)S(1)} %get-tuple-element.49.refs_0_, bf16[512,512]{1,0:T(8,128)(2,1)S(1)} %get-tuple-element.50.refs_1_, bf16[256,512]{1,0:T(8,128)(2,1)S(1)} %get-tuple-element.45.e_ref.refs_6_.refs_2_, ...), custom_call_target="tpu_custom_call", output_to_operand_aliasing={{}: (6, {})} | custom-call | flops 1000000000 | bytes 3000000 | tf_op jit(solution)/shard_map/last/pallas_call | solution.py:26
  (4 shorter events, 0.0 us)
Async XLA Ops:
  0.0 9.5 %collective-permute-start.3 = (bf16[2,128,512]{2,1,0:T(8,128)(2,1)}, bf16[2,128,512]{2,1,0:T(8,128)(2,1)S(1)}, u32[]{:S(2)}, u32[]{:S(2)}) collective-permute-start(bf16[2,128,512]{2,1,0:T(8,128)(2,1)} %bitcast.9), channel_id=1, source_target_pairs={{0,2},{1,3},{2,0},{3,1},{4,6},{5,7},{6,4},{7,5},{8,10},{9,11},{10,... | collective-permute-start | bytes 786440 | tf_op jit(solution)/shard_map/ppermute | solution.py:22
  2.9 1.7 %collective-permute-start.1 = (bf16[2,128,512]{2,1,0:T(8,128)(2,1)}, bf16[2,128,512]{2,1,0:T(8,128)(2,1)S(1)}, u32[]{:S(2)}, u32[]{:S(2)}) collective-permute-start(bf16[2,128,512]{2,1,0:T(8,128)(2,1)} %bitcast.10), channel_id=1, source_target_pairs={{0,1},{1,0},{2,3},{3,2},{4,5},{5,4},{6,7},{7,6},{8,9},{9,8},{10,11... | collective-permute-start | bytes 786440 | tf_op jit(solution)/shard_map/ppermute | solution.py:22
  2.9 1.7 %copy-start.2 = (bf16[1,2,128,512]{3,2,1,0:T(8,128)(2,1)S(1)}, bf16[1,2,128,512]{3,2,1,0:T(8,128)(2,1)}, u32[]{:S(2)}) copy-start(bf16[1,2,128,512]{3,2,1,0:T(8,128)(2,1)} %param.7) | copy-start | bytes 786436
  2.9 1.7 %copy-start.3 = (s32[8,2,256]{2,1,0:T(2,128)S(1)}, s32[8,2,256]{2,1,0:T(2,128)}, u32[]{:S(2)}) copy-start(s32[8,2,256]{2,1,0:T(2,128)} %refs_1_.1) | copy-start | bytes 49156
  2.9 1.7 %copy-start.4 = (f32[512]{0:T(512)S(1)}, f32[512]{0:T(512)}, u32[]{:S(2)}) copy-start(f32[512]{0:T(512)} %param.8) | copy-start | bytes 6148
  3.0 1.7 %copy-start.5 = (s32[8,2]{0,1:T(2,128)S(1)}, s32[8,2]{0,1:T(2,128)}, u32[]{:S(2)}) copy-start(s32[8,2]{0,1:T(2,128)} %param.10) | copy-start | bytes 196
  3.0 4.8 %collective-permute-start = (bf16[128,256]{1,0:T(8,128)(2,1)}, bf16[128,256]{1,0:T(8,128)(2,1)S(1)}, u32[]{:S(2)}, u32[]{:S(2)}) collective-permute-start(bf16[128,256]{1,0:T(8,128)(2,1)} %bitcast.6), channel_id=1, source_target_pairs={{0,4},{4,0},{8,12},{12,8},{16,20},{20,16},{24,28},{28,24},{1,5},{5... | collective-permute-start | bytes 196616 | tf_op jit(solution)/shard_map/ppermute | solution.py:22
  4.5 3.2 %copy-start = (bf16[2,256,64]{1,2,0:T(8,128)(2,1)S(1)}, bf16[2,256,64]{1,2,0:T(8,128)(2,1)}, u32[]{:S(2)}) copy-start(bf16[2,256,64]{1,2,0:T(8,128)(2,1)} %param.11) | copy-start | bytes 196612
  4.7 6.4 %copy-start.1 = (bf16[2,512,512]{2,1,0:T(8,128)(2,1)S(1)}, bf16[2,512,512]{2,1,0:T(8,128)(2,1)}, u32[]{:S(2)}) copy-start(bf16[2,512,512]{2,1,0:T(8,128)(2,1)} %refs_0_.3) | copy-start | bytes 3145732
  9.5 1.6 %collective-permute-start.4 = (bf16[2,128,512]{2,1,0:T(8,128)(2,1)S(1)}, bf16[2,128,512]{2,1,0:T(8,128)(2,1)S(1)}, u32[]{:S(2)}, u32[]{:S(2)}) collective-permute-start(bf16[2,128,512]{2,1,0:T(8,128)(2,1)S(1)} %relay.1.refs_1_.p2_ref), channel_id=1, source_target_pairs={{0,1},{1,0},{2,3},{3,2},{4,5},{5,4},{6,7},{7,6},{8,9},{9,8},{10,11... | collective-permute-start | bytes 786440 | tf_op jit(solution)/shard_map/ppermute | solution.py:22
  11.9 6.6 %collective-permute-start.5 = (s16[336,256]{1,0:T(8,128)(2,1)S(1)}, s16[336,256]{1,0:T(8,128)(2,1)S(1)}, u32[]{:S(2)}, u32[]{:S(2)}) collective-permute-start(s16[336,256]{1,0:T(8,128)(2,1)S(1)} %get-tuple-element.42), channel_id=1, source_target_pairs={{0,4},{4,0},{8,12},{12,8},{16,20},{20,16},{24,28},{28,24},{1,5},{5... | collective-permute-start | bytes 516104 | tf_op jit(solution)/shard_map/ppermute | solution.py:22
  13.7 10.4 %collective-permute-start.2 = (bf16[2,128,256]{2,1,0:T(8,128)(2,1)S(1)}, bf16[2,128,256]{2,1,0:T(8,128)(2,1)S(1)}, u32[]{:S(2)}, u32[]{:S(2)}) collective-permute-start(bf16[2,128,256]{2,1,0:T(8,128)(2,1)S(1)} %pair.1.rest_0_), channel_id=1, source_target_pairs={{0,8},{4,12},{8,0},{12,4},{16,24},{20,28},{24,16},{28,20},{1,9},{5... | collective-permute-start | bytes 393224 | tf_op jit(solution)/shard_map/ppermute | solution.py:22
  16.0 8.9 %collective-permute-start.9 = (s16[400,256]{1,0:T(8,128)(2,1)S(1)}, s16[400,256]{1,0:T(8,128)(2,1)S(1)}, u32[]{:S(2)}, u32[]{:S(2)}) collective-permute-start(s16[400,256]{1,0:T(8,128)(2,1)S(1)} %ready1.1), channel_id=1, source_target_pairs={{0,4},{4,0},{8,12},{12,8},{16,20},{20,16},{24,28},{28,24},{1,5},{5... | collective-permute-start | bytes 614408 | tf_op jit(solution)/shard_map/ppermute | solution.py:22
  19.3 7.0 %collective-permute-start.7 = (s16[336,256]{1,0:T(8,128)(2,1)S(1)}, s16[336,256]{1,0:T(8,128)(2,1)S(1)}, u32[]{:S(2)}, u32[]{:S(2)}) collective-permute-start(s16[336,256]{1,0:T(8,128)(2,1)S(1)} %get-tuple-element.54), channel_id=1, source_target_pairs={{0,8},{4,12},{8,0},{12,4},{16,24},{20,28},{24,16},{28,20},{1,9},{5... | collective-permute-start | bytes 516104 | tf_op jit(solution)/shard_map/ppermute | solution.py:22
  22.5 5.6 %collective-permute-start.6 = (s16[336,256]{1,0:T(8,128)(2,1)S(1)}, s16[336,256]{1,0:T(8,128)(2,1)S(1)}, u32[]{:S(2)}, u32[]{:S(2)}) collective-permute-start(s16[336,256]{1,0:T(8,128)(2,1)S(1)} %ready2.1), channel_id=1, source_target_pairs={{0,4},{4,0},{8,12},{12,8},{16,20},{20,16},{24,28},{28,24},{1,5},{5... | collective-permute-start | bytes 516104 | tf_op jit(solution)/shard_map/ppermute | solution.py:22
  25.8 7.7 %collective-permute-start.10 = (s16[400,256]{1,0:T(8,128)(2,1)S(1)}, s16[400,256]{1,0:T(8,128)(2,1)S(1)}, u32[]{:S(2)}, u32[]{:S(2)}) collective-permute-start(s16[400,256]{1,0:T(8,128)(2,1)S(1)} %get-tuple-element.64), channel_id=1, source_target_pairs={{0,8},{4,12},{8,0},{12,4},{16,24},{20,28},{24,16},{28,20},{1,9},{5... | collective-permute-start | bytes 614408 | tf_op jit(solution)/shard_map/ppermute | solution.py:22
  28.9 6.6 %collective-permute-start.8 = (s16[336,256]{1,0:T(8,128)(2,1)S(1)}, s16[336,256]{1,0:T(8,128)(2,1)S(1)}, u32[]{:S(2)}, u32[]{:S(2)}) collective-permute-start(s16[336,256]{1,0:T(8,128)(2,1)S(1)} %get-tuple-element.58), channel_id=1, source_target_pairs={{0,8},{4,12},{8,0},{12,4},{16,24},{20,28},{24,16},{28,20},{1,9},{5... | collective-permute-start | bytes 516104 | tf_op jit(solution)/shard_map/ppermute | solution.py:22

commit v3 on v2

--- a/solution.py
+++ b/solution.py
@@ -9,9 +9,10 @@
 WAVENUM = 0.7
 BF = jnp.bfloat16
 F32 = jnp.float32
-SHARES = (10, 12, 10)
+SHARES = (10, 11, 11)
 TOP = 32766.0
 STEPS = 128.0
+LANES = 128
 VMEM = pl.BlockSpec(memory_space=pltpu.VMEM)
 SMEM = pl.BlockSpec(memory_space=pltpu.SMEM)
 ANY = pl.BlockSpec(memory_space=pl.ANY)
@@ -23,7 +24,8 @@
 
 
 def call(body, name, outs, ins, specs=None, scratch=(), cost=1.0, **kw):
-    return pl.pallas_call(
+    return list(
+        pl.pallas_call(
         body,
         name=name,
         out_shape=outs,
@@ -34,10 +36,15 @@
         cost_estimate=pl.CostEstimate(flops=int(cost * 1e9), bytes_accessed=int(cost * 3e6), transcendentals=0),
         **kw,
     )(*ins)
+    )
 
 
 def shape(*dims, dtype=F32):
     return jax.ShapeDtypeStruct(dims, dtype)
+
+
+def packed_shape(n, kmax):
+    return shape(2 * n * kmax // LANES + 16, LANES, dtype=jnp.int16)
 
 
 def nn(a, b):
@@ -91,12 +98,16 @@
     )
 
 
+def stacked(*refs):
+    return jnp.concatenate([jnp.concatenate([ref[0], ref[1]], axis=1) for ref in refs], axis=0)
+
+
 def open_body(out_ref):
     out_ref[...] = jnp.zeros(out_ref.shape, out_ref.dtype)
 
 
 def plan_body(ranks_ref, skel_ref, contrast_ref, own_ref, beside_ref, dep_ref, *refs, parts):
-    e0_ref, er_ref, e1_ref, q_ref, ghi_ref, glo_ref, g1_ref, j_ref, d_ref, part_ref = refs
+    e0_ref, e1_ref, q_ref, ghi_ref, glo_ref, g1_ref, j_ref, d_ref, part_ref = refs
     box = lax.axis_index("box")
     me = lax.axis_index("field")
     kmax = skel_ref.shape[2]
@@ -104,6 +115,9 @@
     contrast = contrast_ref[...]
     ranks = ranks_ref[...].astype(F32)
     ranks = jnp.sum(jnp.where(iota(ranks.shape, 1) == box, ranks, 0.0), axis=1, keepdims=True).astype(jnp.int32)
+    n = width // parts
+    lane = iota((kmax, width), 1)
+    turned = (((lane // n) ^ me) * n) + lane % n
     rows = []
     cols = []
     rank = []
@@ -117,14 +131,10 @@
         rows.append(own_row)
         cols.append(own_col)
         rank.append(r)
-        hit = (own_col == iota((kmax, width), 1)) & (iota((kmax, width), 0) < r)
+        hit = (own_col == turned) & (iota((kmax, width), 0) < r)
         (e0_ref, e1_ref)[level][...] = hit.astype(F32).astype(BF)
-        if level == 0:
-            n = width // parts
-            lane = iota((kmax, width), 1)
-            turned = (((lane // n) ^ me) * n) + lane % n
-            er_ref[...] = ((own_col == turned) & (iota((kmax, width), 0) < r)).astype(F32).astype(BF)
-        q_col = jnp.sum(jnp.where(hit, contrast, 0.0), axis=1, keepdims=True)
+        true_hit = (own_col == iota((kmax, width), 1)) & (iota((kmax, width), 0) < r)
+        q_col = jnp.sum(jnp.where(true_hit, contrast, 0.0), axis=1, keepdims=True)
         q_ref[pl.ds(level, 1), :] = to_row(q_col, kmax)
         ox, oy, oz = place(own_row, box)
         fx, fy, fz = place(far_col, far)
@@ -152,15 +162,7 @@
     other = iota((kmax, kmax), 1)
     j_ref[...] = ((cols[0] == rows[1]) & (mine < rank[0]) & (other < rank[1])).astype(F32).astype(BF)
     d_ref[...] = ((cols[1] == rows[1]) & (mine < rank[1]) & (other < rank[1])).astype(F32).astype(BF)
-    n = own_ref.shape[1]
-    both = jnp.concatenate(
-        [
-            jnp.concatenate([own_ref[0], own_ref[1]], axis=1),
-            jnp.concatenate([beside_ref[0], beside_ref[1]], axis=1),
-        ],
-        axis=0,
-    )
-    part_ref[...] = nn(er_ref[:, : 2 * n], both).astype(BF)
+    part_ref[...] = nn(e0_ref[:, : 2 * n], stacked(own_ref, beside_ref)).astype(BF)
 
 
 def core_body(own_ref, near_ref, far_ref, g1_ref, d_ref, dep_ref, mc_ref, khi_ref, klo_ref, ct_ref):
@@ -220,17 +222,9 @@
     pack(w, out_ref)
 
 
-def first_body(part_ref, across_ref, beyond_ref, er_ref, x_ref, q_ref, *outs, start, n):
-    picked_ref, out_ref = outs
+def first_body(part_ref, across_ref, beyond_ref, e0_ref, x_ref, q_ref, picked_ref, out_ref, *, start, n):
     rows = across_ref.shape[1]
-    both = jnp.concatenate(
-        [
-            jnp.concatenate([across_ref[0], across_ref[1]], axis=1),
-            jnp.concatenate([beyond_ref[0], beyond_ref[1]], axis=1),
-        ],
-        axis=0,
-    )
-    picked = (nn(er_ref[:, 2 * rows :], both) + part_ref[...].astype(F32)).astype(BF)
+    picked = (nn(e0_ref[:, 2 * rows :], stacked(across_ref, beyond_ref)) + part_ref[...].astype(F32)).astype(BF)
     picked_ref[...] = picked
     send(x_ref, picked, q_ref, out_ref, start, n)
 
@@ -239,48 +233,50 @@
     send(x_ref, picked_ref[...], q_ref, out_ref, start, n)
 
 
-def rows_body(x_ref, p0_ref, p1_ref, p2_ref, p3_ref, e_ref, v_ref, a_ref):
-    width = x_ref.shape[2]
+def rows_body(x_ref, p0_ref, p1_ref, p2_ref, p3_ref, e_ref, dep_ref, v_ref):
     kmax = e_ref.shape[0]
-    me = lax.axis_index("field")
-    n = p0_ref.shape[1]
-    for mask, ref in enumerate((p0_ref, p1_ref, p2_ref, p3_ref)):
-        start = pl.multiple_of((me ^ mask) * n, n)
-        a_ref[pl.ds(start, n), 0:width] = ref[0]
-        a_ref[pl.ds(start, n), width:] = ref[1]
     left, right = turned_fields(x_ref, 0, x_ref.shape[1])
-    picked = nn(e_ref[...], a_ref[...]).astype(BF)
+    picked = nn(e_ref[...], stacked(p0_ref, p1_ref, p2_ref, p3_ref)).astype(BF)
     v_ref[:, 0:kmax] = nt(left, picked)
     v_ref[:, kmax:] = nt(right, picked)
 
 
-def leaf_body(x_ref, a_ref, dep_ref, y_ref):
-    width = x_ref.shape[2]
+def leaf_body(x_ref, p_ref, q_ref, dep_ref, y_ref):
     left, right = turned_fields(x_ref, 0, x_ref.shape[1])
-    a = a_ref[...]
-    y_ref[:, 0:width] = nt(left, a)
-    y_ref[:, width:] = nt(right, a)
+    a = stacked(p_ref, q_ref)
+    y_ref[0] = nt(left, a)
+    y_ref[1] = nt(right, a)
 
 
 def pack(w, out_ref):
     n, both = w.shape
-    k = both // 2
+    lanes = out_ref.shape[1]
     most = jnp.max(jnp.abs(w), axis=1, keepdims=True)
     step = jnp.ceil(jnp.log2(jnp.maximum(most, 1e-30)) * STEPS)
     inv = TOP / jnp.exp2(step / STEPS)
     v = jnp.floor(w * inv + 0.5).astype(jnp.int32).astype(jnp.int16)
-    out_ref[0:n, :] = v[:, :k]
-    out_ref[n : 2 * n, :] = v[:, k:]
-    out_ref[2 * n :, :] = jnp.broadcast_to(to_row(step, k), (16, k)).astype(jnp.int32).astype(jnp.int16)
+    for i in range(both // lanes):
+        out_ref[i * n : (i + 1) * n, :] = v[:, i * lanes : (i + 1) * lanes]
+    groups = -(-n // lanes)
+    step = to_row(step, groups * lanes)
+    tile = jnp.zeros((16, lanes), F32)
+    for i in range(groups):
+        tile = jnp.where(iota(tile.shape, 0) == i, step[:, i * lanes : (i + 1) * lanes], tile)
+    out_ref[both // lanes * n :, :] = tile.astype(jnp.int32).astype(jnp.int16)
 
 
 def apply_packed(in_ref, mhi, mlo):
-    n = (in_ref.shape[0] - 16) // 2
-    k = in_ref.shape[1]
-    steps = in_ref[2 * n :, :].astype(jnp.int32).astype(F32)[0:1, :]
-    step = jnp.sum(jnp.where(iota((n, k), 0) == iota((n, k), 1), steps, 0.0), axis=1, keepdims=True)
+    k = mhi.shape[0]
+    lanes = in_ref.shape[1]
+    pieces = k // lanes
+    n = (in_ref.shape[0] - 16) // pieces
+    groups = -(-n // lanes)
+    steps = in_ref[pieces * n :, :].astype(jnp.int32).astype(F32)
+    steps = jnp.concatenate([steps[i : i + 1, :] for i in range(groups)], axis=1)
+    own = iota((n, groups * lanes), 0) == iota((n, groups * lanes), 1)
+    step = jnp.sum(jnp.where(own, steps, 0.0), axis=1, keepdims=True)
     scale = jnp.exp2(step / STEPS) * (1.0 / TOP)
-    v = jnp.concatenate([in_ref[0:n, :], in_ref[n : 2 * n, :]], axis=1).astype(jnp.int32)
+    v = jnp.concatenate([in_ref[i * n : (i + 1) * n, :] for i in range(pieces)], axis=1).astype(jnp.int32)
     upper = (v + 128) & -256
     lower = (v - upper).astype(F32).astype(BF)
     upper = upper.astype(F32).astype(BF)
@@ -289,8 +285,8 @@
 
 def second_body(in_ref, ghi_ref, glo_ref, v_ref, j_ref, q_ref, *rest, start):
     out_ref, gs_ref, us_ref = rest[-3:]
-    n = (in_ref.shape[0] - 16) // 2
-    k = in_ref.shape[1]
+    n = gs_ref.shape[1]
+    k = j_ref.shape[0]
     g = apply_packed(in_ref, ghi_ref[...], glo_ref[...])
     hi, lo = halves(g)
     gs_ref[0] = hi
@@ -306,41 +302,52 @@
     us_ref[1] = lo
 
 
-def third_body(gs_ref, us_ref, y_ref, e0_ref, mc_ref, part_ref, p_ref, *, start):
+def third_body(gs_ref, us_ref, near_ref, far_ref, e0_ref, mc_ref, part_ref, p_ref, *, start):
     n = gs_ref.shape[1]
     k = e0_ref.shape[0]
-    width = e0_ref.shape[1]
     e = e0_ref[...]
     for i in range(2):
         cols = slice(i * k, i * k + k)
-        part_ref[i] = y_ref[start : start + n, i * width : (i + 1) * width] - (
-            nn(gs_ref[0, :, cols], e) + nn(gs_ref[1, :, cols], e)
-        )
+        y = jnp.concatenate([near_ref[i, start : start + n], far_ref[i, start : start + n]], axis=1)
+        part_ref[i] = y - (nn(gs_ref[0, :, cols], e) + nn(gs_ref[1, :, cols], e))
     mc = mc_ref[...]
     p_ref[...] = nn(us_ref[0], mc) + nn(us_ref[1], mc)
 
 
-def fourth_body(*refs, parts):
-    khi_ref, klo_ref, e1_ref = refs[:3]
-    chunks = refs[3 : 3 + 3 * len(parts)]
-    out_ref, hold_ref, sem = refs[-3:]
-    base = parts[0][0]
-    e = e1_ref[...]
-    khi = khi_ref[...]
-    klo = klo_ref[...]
-    k = e1_ref.shape[0]
+def finish(in_ref, part_ref, p_ref, khi, klo, e):
+    k = e.shape[0]
+    p = p_ref[...] + apply_packed(in_ref, khi, klo)
+    hi, lo = halves(p)
+    for i in range(2):
+        cols = slice(i * k, i * k + k)
+        yield i, part_ref[i] - (nn(hi[:, cols], e) + nn(lo[:, cols], e))
+
+
+def writer(out_ref, sem, blocks):
+    me = lax.axis_index("field")
     copies = []
-    for c, (start, n) in enumerate(parts):
-        in_ref, part_ref, p_ref = chunks[3 * c : 3 * c + 3]
-        p = p_ref[...] + apply_packed(in_ref, khi, klo)
-        hi, lo = halves(p)
-        for i in range(2):
-            cols = slice(i * k, i * k + k)
-            spot = pl.ds(start - base, n)
-            hold_ref[i, spot] = part_ref[i] - (nn(hi[:, cols], e) + nn(lo[:, cols], e))
-            copy = pltpu.make_async_copy(hold_ref.at[i, spot], out_ref.at[i, pl.ds(start, n), :], sem.at[2 * c + i])
+
+    def write(src_ref, i, row):
+        n = src_ref.shape[2] // blocks
+        for m in range(blocks):
+            col = pl.multiple_of((me ^ m) * n, n)
+            copy = pltpu.make_async_copy(
+                src_ref.at[i, :, pl.ds(m * n, n)],
+                out_ref.at[i, pl.ds(row, src_ref.shape[1]), pl.ds(col, n)],
+                sem.at[len(copies)],
+            )
             copy.start()
             copies.append(copy)
+
+    return write, copies
+
+
+def last_body(khi_ref, klo_ref, e1_ref, in_ref, part_ref, p_ref, *rest, start, blocks):
+    out_ref, hold_ref, sem = rest[-3:]
+    write, copies = writer(out_ref, sem, blocks)
+    for i, value in finish(in_ref, part_ref, p_ref, khi_ref[...], klo_ref[...], e1_ref[...]):
+        hold_ref[i] = value
+        write(hold_ref, i, start)
     for copy in copies:
         copy.wait()
 
@@ -354,13 +361,12 @@
     beside = swap(own, "field", 1)
     core_own = jnp.swapaxes(top_core, 1, 2).reshape(2 * quarter, kmax)
     core_near = swap(core_own, "box", 1)
-    n = own.shape[1]
+    n = n_rows = own.shape[1]
     (opened,) = call(open_body, "open", [shape(8, 128)], [], cost=4.0)
-    e0, er, e1, q, ghi, glo, g1, dup01, dup11, part = call(
+    e0, e1, q, ghi, glo, g1, dup01, dup11, part = call(
         lambda *refs: plan_body(*refs, parts=lax.axis_size("field")),
         "plan",
         [
-            shape(kmax, width, dtype=BF),
             shape(kmax, width, dtype=BF),
             shape(kmax, width, dtype=BF),
             shape(8, kmax),
@@ -375,12 +381,15 @@
         [VMEM] * 5 + [ANY],
     )
     x = incident
+    (near,) = call(
+        leaf_body, "near", [shape(2, nf, 2 * n)], [x, own, beside, part], [VMEM] * 3 + [ANY], cost=0.7
+    )
     (pair,) = call(
-        pair_body, "pair", [shape(2, 2 * quarter, kmax, dtype=BF)], [core_own, core_near, part], [VMEM, VMEM, ANY], cost=0.05
+        pair_body, "pair", [shape(2, 2 * quarter, kmax, dtype=BF)], [core_own, core_near, near], [VMEM, VMEM, ANY], cost=0.05
     )
     core_far = swap(pair, "box", 2)
     (across,) = call(
-        relay_body, "relay", [shape(*across.shape, dtype=BF)], [across, pair], [VMEM, ANY], cost=0.05
+        relay_body, "relay", [shape(*across.shape, dtype=BF)], [across, pair, near], [VMEM, ANY, ANY], cost=0.05
     )
     beyond = swap(across, "field", 1)
     chunks = [nf // sum(SHARES) * share for share in SHARES]
@@ -391,33 +400,38 @@
         "first",
         [
             shape(kmax, 2 * width, dtype=BF),
-            shape(2 * n + 16, kmax, dtype=jnp.int16),
+            packed_shape(n, kmax),
         ],
-        [part, across, beyond, er, x, q],
+        [part, across, beyond, e0, x, q],
         cost=0.8,
     )
 
-    def ready(i, dep):
+    def ready(i, dep, gate=None):
         start, n = sizes[i]
         (packed,) = call(
             lambda *refs: rest_body(*refs, start=start, n=n),
             f"ready{i}",
-            [shape(2 * n + 16, kmax, dtype=jnp.int16)],
+            [packed_shape(n, kmax)],
             [x, picked, q, dep],
             [VMEM] * 3 + [ANY],
             cost=0.6,
         )
+        if i > 1:
+            (packed,) = call(
+                relay_body, f"gate{i}", [packed_shape(n, kmax)], [packed, gate], [VMEM, ANY], cost=0.05
+            )
         return swap(packed, "box", 1)
 
     got = swap(head, "box", 1)
-    v1, a_all = call(
+    (v1,) = call(
         rows_body,
         "rows",
-        [shape(nf, 2 * kmax), shape(width, 2 * width, dtype=BF)],
-        [x, own, beside, across, beyond, e1],
+        [shape(nf, 2 * kmax)],
+        [x, own, beside, across, beyond, e1, e0],
+        [VMEM] * 6 + [ANY],
     )
     late = []
-    coming = ready(1, q)
+    coming = ready(1, v1)
 
     def core(dep):
         return call(
@@ -435,7 +449,7 @@
             lambda *refs, start=start: third_body(*refs, start=start),
             f"third{i}",
             [shape(2, n, width), shape(n, 2 * kmax)],
-            [late[i][1], late[i][2], y, e0, mc],
+            [late[i][1], late[i][2], near, y, e0, mc],
             cost=0.5,
         )
 
@@ -443,50 +457,47 @@
         dep = e1
         if i == 1 and 1:
             dep = mc
-        if i == 2 and 2:
-            dep = mc if 2 == 1 else late[2 - 2][2]
+        if i >= 2 and 0:
+            dep = mc if 0 == 1 else late[i - 0][2]
         back, gs, us = call(
             lambda *refs, start=start: second_body(*refs, start=start),
             f"second{i}",
-            [shape(2 * n + 16, kmax, dtype=jnp.int16), shape(2, n, 2 * kmax, dtype=BF), shape(2, n, 2 * kmax, dtype=BF)],
+            [packed_shape(n, kmax), shape(2, n, 2 * kmax, dtype=BF), shape(2, n, 2 * kmax, dtype=BF)],
             [got, ghi, glo, v1, dup01, q, dep],
             [VMEM] * 6 + [ANY],
             cost=0.8,
         )
         got = coming
-        if 0:
+        if 1:
             late.append([swap(back, "box", 2), gs, us])
         if i + 2 < len(sizes):
-            coming = ready(i + 2, gs)
-        if not 0:
+            coming = ready(i + 2, e1, gs)
+        if not 1:
             late.append([swap(back, "box", 2), gs, us])
         if i == 0:
-            mc, khi, klo = core(gs)
+            mc, khi, klo = core(v1)
         if i == 1:
-            (y,) = call(leaf_body, "leaf", [shape(nf, 2 * width)], [x, a_all, late[0][0]], [VMEM, VMEM, ANY], cost=1.3)
+            (y,) = call(
+                leaf_body, "leaf", [shape(2, nf, 2 * n_rows)], [x, across, beyond, gs], [VMEM] * 3 + [ANY], cost=0.7
+            )
             for j in range(i + 1):
                 third(j)
         if i > 1:
             third(i)
-    out = None
-    for name, at in (("most", slice(0, -1)), ("last", slice(-1, None))):
-        parts = sizes[at]
-        ins = [khi, klo, e1] + [a for group in late[at] for a in group]
-        specs = [VMEM] * len(ins)
-        if out is not None:
-            ins.append(out)
-            specs.append(ANY)
-        (out,) = call(
-            lambda *refs, parts=parts: fourth_body(*refs, parts=parts),
-            name,
+    blocks = lax.axis_size("field")
+    out = []
+    for i, (start, n) in enumerate(sizes):
+        out = call(
+            lambda *refs, start=start: last_body(*refs, start=start, blocks=blocks),
+            f"last{i}",
             [shape(2, nf, width)],
-            ins,
-            specs,
-            [pltpu.VMEM((2, sum(n for _, n in parts), width), F32), pltpu.SemaphoreType.DMA((2 * len(parts),))],
+            [khi, klo, e1] + late[i] + out,
+            [VMEM] * 6 + [ANY] * len(out),
+            [pltpu.VMEM((2, n, width), F32), pltpu.SemaphoreType.DMA((2 * blocks,))],
             out_specs=[ANY],
-            input_output_aliases={} if len(specs) == len(ins) and specs[-1] is VMEM else {len(ins) - 1: 0},
+            input_output_aliases={6: 0} if out else {},
         )
-    return out
+    return out[0]
 
 
 def solution(mesh):

time: 37.2 us -> 35.6 us (0.957)
  waiting for transfers between devices: 7.45 us -> 5.23 us
  Pallas kernels: 14.6 us -> 15.9 us
  starting transfers between devices: 14.9 us -> 14.1 us
    ppermute x11, waiting for transfers between devices: 7.45 us -> 5.23 us  [swap(): lax.ppermute(value, axis, [(s, s ^ mask) for s in range(lax.axis_size(axi...]
    pallas_call x18 -> x21, Pallas kernels: 14.6 us -> 15.9 us  [call(): pl.pallas_call(body, name=name, out_shape=outs, in_specs=specs or [VMEM]...]
    ppermute x11, starting transfers between devices: 14.9 us -> 14.1 us  [swap(): lax.ppermute(value, axis, [(s, s ^ mask) for s in range(lax.axis_size(axi...]
  transfers between devices with their start and end apart: 11 -> 11, of which waited for: 6 -> 5; matrix products, arithmetic and copies ran while one was open for 0% -> 0% of each run, Pallas kernels for 33% -> 40%
where the time goes in v3:
time: 35.6 us; the launch traced here: 35.4 us
  Pallas kernels  15.9 us (45%)
  starting transfers between devices  14.1 us (40%)
  waiting for transfers between devices  5.23 us (15%)
    pallas_call x21, Pallas kernels, call(): pl.pallas_call(body, name=name, out_shape=outs, in_specs=specs or [VMEM]...  15.9 us
    ppermute x11, starting transfers between devices, swap(): lax.ppermute(value, axis, [(s, s ^ mask) for s in range(lax.axis_size(axi...  14.1 us
    ppermute x11, waiting for transfers between devices, swap(): lax.ppermute(value, axis, [(s, s ^ mask) for s in range(lax.axis_size(axi...  5.23 us
  transfers between devices with their start and end apart: 11, of which 5 were waited for; matrix products, arithmetic and copies ran while one was open for 0% of the time, Pallas kernels for 40%

profile of v3, /device:TPU:0, one launch (start us, length us, event | category | flops | bytes accessed | tf_op | source)
XLA Modules:
  0.0 35.4 jit_solution(12414672041208920556)
XLA Ops:
  0.0 2.9 %collective-permute-start.3 = (bf16[2,128,512]{2,1,0:T(8,128)(2,1)}, bf16[2,128,512]{2,1,0:T(8,128)(2,1)S(1)}, u32[]{:S(2)}, u32[]{:S(2)}) collective-permute-start(bf16[2,128,512]{2,1,0:T(8,128)(2,1)} %bitcast.6), channel_id=1, source_target_pairs={{0,2},{1,3},{2,0},{3,1},{4,6},{5,7},{6,4},{7,5},{8,10},{9,11},{10,... | collective-permute-start | bytes 786440 | tf_op jit(solution)/shard_map/ppermute | solution.py:23
  2.9 0.0 collective-permute-start.1
  2.9 0.0 copy-start.1
  3.0 0.0 copy-start.5
  3.0 1.6 %collective-permute-start = (bf16[128,256]{1,0:T(8,128)(2,1)}, bf16[128,256]{1,0:T(8,128)(2,1)S(1)}, u32[]{:S(2)}, u32[]{:S(2)}) collective-permute-start(bf16[128,256]{1,0:T(8,128)(2,1)} %bitcast.11), channel_id=1, source_target_pairs={{0,4},{4,0},{8,12},{12,8},{16,20},{20,16},{24,28},{28,24},{1,5},{5... | collective-permute-start | bytes 196616 | tf_op jit(solution)/shard_map/ppermute | solution.py:23
  4.6 0.1 collective-permute-done.1.refs_4_.q_ref.p1_ref
  4.7 0.0 copy-done.1
  4.7 0.0 copy-done.3
  4.7 0.0 copy-done.4
  4.7 0.0 copy-done.5
  4.7 1.7 %plan.1 = (bf16[256,512]{1,0:T(8,128)(2,1)S(1)}, bf16[256,512]{1,0:T(8,128)(2,1)S(1)}, f32[8,256]{1,0:T(8,128)S(1)}, bf16[512,512]{1,0:T(8,128)(2,1)S(1)}, bf16[...) custom-call(s32[2,8]{1,0:T(2,128)S(1)} %bitcast.15, ...), custom_call_target="tpu_custom_call" | custom-call | flops 1000000000 | bytes 3000000 | tf_op jit(solution)/shard_map/plan/pallas_call | solution.py:28
  6.4 0.0 copy-start.2
  6.4 0.0 copy-done
  6.4 0.7 %near.1.dep_ref.rest_1_.refs_2_ = f32[2,512,256]{2,1,0:T(8,128)S(1)} custom-call(bf16[2,512,512]{2,1,0:T(8,128)(2,1)S(1)} %copy-done, bf16[2,128,512]{2,1,0:T(8,128)(2,1)S(1)} %bitcast.9, bf16[2,128,512]{2,1,0:T(8,128)(2,1)S(1)} %collective-permute-done.1.refs_4_.q_ref.p1_ref, bf16[256,1024]{1,0:T(8,128)(2,1)S(1)} %get-tuple-element.34.dep_ref.refs_0_), custom_call_target="tpu_custom_call" | custom-call | flops 700000000 | bytes 2100000 | tf_op jit(solution)/shard_map/near/pallas_call | solution.py:28
  7.2 0.6 %collective-permute-done.b_ref.near_ref = bf16[128,256]{1,0:T(8,128)(2,1)S(1)} collective-permute-done((bf16[128,256]{1,0:T(8,128)(2,1)}, bf16[128,256]{1,0:T(8,128)(2,1)S(1)}, u32[]{:S(2)}, u32[]{:S(2)}) %collective-permute-start) | collective-permute-done | bytes 65568 | tf_op jit(solution)/shard_map/ppermute | solution.py:23
  7.7 0.0 copy-done.2
  7.8 1.7 %collective-permute-done.3.in_ref = bf16[2,128,512]{2,1,0:T(8,128)(2,1)S(1)} collective-permute-done((bf16[2,128,512]{2,1,0:T(8,128)(2,1)}, bf16[2,128,512]{2,1,0:T(8,128)(2,1)S(1)}, u32[]{:S(2)}, u32[]{:S(2)}) %collective-permute-start.3) | collective-permute-done | bytes 262176 | tf_op jit(solution)/shard_map/ppermute | solution.py:23
  9.5 0.1 collective-permute-start.4
  9.6 1.9 %collective-permute-start.2 = (bf16[2,128,256]{2,1,0:T(8,128)(2,1)S(1)}, bf16[2,128,256]{2,1,0:T(8,128)(2,1)S(1)}, u32[]{:S(2)}, u32[]{:S(2)}) collective-permute-start(bf16[2,128,256]{2,1,0:T(8,128)(2,1)S(1)} %pair.1.rest_0_), channel_id=1, source_target_pairs={{0,8},{4,12},{8,0},{12,4},{16,24},{20,28},{24,16},{28,20},{1,9},{5... | collective-permute-start | bytes 393224 | tf_op jit(solution)/shard_map/ppermute | solution.py:23
  11.4 0.0 collective-permute-done.4.p3_ref.refs_2_.q_ref
  11.5 0.8 %first.1 = (bf16[256,1024]{1,0:T(8,128)(2,1)S(1)}, s16[656,128]{1,0:T(8,128)(2,1)S(1)}) custom-call(bf16[256,1024]{1,0:T(8,128)(2,1)S(1)} %get-tuple-element.34.dep_ref.refs_0_, bf16[2,128,512]{2,1,0:T(8,128)(2,1)S(1)} %relay.1.p2_ref.refs_1_.p_ref, bf16[2,128,512]{2,1,0:T(8,128)(2,1)S(1)} %collective-permute-done.4.p3_ref.refs_2_.q_ref, ...), custom_call_target="tpu_custom_call" | custom-call | flops 800000000 | bytes 2400000 | tf_op jit(solution)/shard_map/first/pallas_call | solution.py:28
  12.3 1.6 %collective-permute-start.5 = (s16[656,128]{1,0:T(8,128)(2,1)S(1)}, s16[656,128]{1,0:T(8,128)(2,1)S(1)}, u32[]{:S(2)}, u32[]{:S(2)}) collective-permute-start(s16[656,128]{1,0:T(8,128)(2,1)S(1)} %get-tuple-element.43), channel_id=1, source_target_pairs={{0,4},{4,0},{8,12},{12,8},{16,20},{20,16},{24,28},{28,24},{1,5},{5... | collective-permute-start | bytes 503816 | tf_op jit(solution)/shard_map/ppermute | solution.py:23
  13.9 1.0 %rows.1.dep_ref.refs_3_ = f32[512,512]{1,0:T(8,128)S(1)} custom-call(bf16[2,512,512]{2,1,0:T(8,128)(2,1)S(1)} %copy-done, bf16[2,128,512]{2,1,0:T(8,128)(2,1)S(1)} %bitcast.10, bf16[2,128,512]{2,1,0:T(8,128)(2,1)S(1)} %collective-permute-done.1.refs_4_.q_ref.p1_ref, bf16[2,128,512]{2,1,0:T(8,128)(2,1)S(1)} %relay.1.p2_ref.refs_1_.p_ref, ...), custom_call_target="tpu_custom_call" | custom-call | flops 1000000000 | bytes 3000000 | tf_op jit(solution)/shard_map/rows/pallas_call | solution.py:28
  14.8 0.6 %ready1.1 = s16[720,128]{1,0:T(8,128)(2,1)S(1)} custom-call(bf16[2,512,512]{2,1,0:T(8,128)(2,1)S(1)} %copy-done, bf16[256,1024]{1,0:T(8,128)(2,1)S(1)} %get-tuple-element.42.refs_1_, f32[8,256]{1,0:T(8,128)S(1)} %get-tuple-element.41.refs_5_.refs_2_, f32[512,512]{1,0:T(8,128)S(1)} %rows.1.dep_ref.refs_3_), custom_call_target="tpu_custom_call" | custom-call | flops 600000000 | bytes 1800000 | tf_op jit(solution)/shard_map/ready1/pallas_call | solution.py:28
  15.5 0.6 %collective-permute-start.8 = (s16[720,128]{1,0:T(8,128)(2,1)S(1)}, s16[720,128]{1,0:T(8,128)(2,1)S(1)}, u32[]{:S(2)}, u32[]{:S(2)}) collective-permute-start(s16[720,128]{1,0:T(8,128)(2,1)S(1)} %ready1.1), channel_id=1, source_target_pairs={{0,4},{4,0},{8,12},{12,8},{16,20},{20,16},{24,28},{28,24},{1,5},{5... | collective-permute-start | bytes 552968 | tf_op jit(solution)/shard_map/ppermute | solution.py:23
  16.1 0.6 %ready2.1.in_ref = s16[720,128]{1,0:T(8,128)(2,1)S(1)} custom-call(bf16[2,512,512]{2,1,0:T(8,128)(2,1)S(1)} %copy-done, bf16[256,1024]{1,0:T(8,128)(2,1)S(1)} %get-tuple-element.42.refs_1_, f32[8,256]{1,0:T(8,128)S(1)} %get-tuple-element.41.refs_5_.refs_2_, bf16[256,512]{1,0:T(8,128)(2,1)S(1)} %get-tuple-element.37.e_ref.refs_3_.refs_6_.refs_2_), custom_call_target="tpu_custom_call" | custom-call | flops 600000000 | bytes 1800000 | tf_op jit(solution)/shard_map/ready2/pallas_call | solution.py:28
  16.7 0.0 collective-permute-done.2.far_ref
  16.7 0.8 %core.1 = (bf16[512,512]{1,0:T(8,128)(2,1)S(1)}, bf16[512,512]{1,0:T(8,128)(2,1)S(1)}, bf16[512,512]{1,0:T(8,128)(2,1)S(1)}) custom-call(bf16[128,256]{1,0:T(8,128)(2,1)S(1)} %bitcast.13, bf16[128,256]{1,0:T(8,128)(2,1)S(1)} %collective-permute-done.b_ref.near_ref, bf16[2,128,256]{2,1,0:T(8,128)(2,1)S(1)} %collective-permute-done.2.far_ref, ...), custom_call_target="tpu_custom_call" | custom-call | flops 1000000000 | bytes 3000000 | tf_op jit(solution)/shard_map/core/pallas_call | solution.py:28
  17.5 1.8 %collective-permute-done.5.refs_0_ = s16[656,128]{1,0:T(8,128)(2,1)S(1)} collective-permute-done((s16[656,128]{1,0:T(8,128)(2,1)S(1)}, s16[656,128]{1,0:T(8,128)(2,1)S(1)}, u32[]{:S(2)}, u32[]{:S(2)}) %collective-permute-start.5) | collective-permute-done | bytes 167968 | tf_op jit(solution)/shard_map/ppermute | solution.py:23
  19.3 0.8 %second0.1 = (s16[656,128]{1,0:T(8,128)(2,1)S(1)}, bf16[2,160,512]{2,1,0:T(8,128)(2,1)S(1)}, bf16[2,160,512]{2,1,0:T(8,128)(2,1)S(1)}) custom-call(s16[656,128]{1,0:T(8,128)(2,1)S(1)} %collective-permute-done.5.refs_0_, bf16[512,512]{1,0:T(8,128)(2,1)S(1)} %get-tuple-element.44.refs_1_, bf16[512,512]{1,0:T(8,128)(2,1)S(1)} %get-tuple-element.45.refs_2_, ...), custom_call_target="tpu_custom_call" | custom-call | flops 800000000 | bytes 2400000 | tf_op jit(solution)/shard_map/second0/pallas_call | solution.py:28
  20.1 1.5 %collective-permute-start.10 = (s16[656,128]{1,0:T(8,128)(2,1)S(1)}, s16[656,128]{1,0:T(8,128)(2,1)S(1)}, u32[]{:S(2)}, u32[]{:S(2)}) collective-permute-start(s16[656,128]{1,0:T(8,128)(2,1)S(1)} %get-tuple-element.59), channel_id=1, source_target_pairs={{0,8},{4,12},{8,0},{12,4},{16,24},{20,28},{24,16},{28,20},{1,9},{5... | collective-permute-start | bytes 503816 | tf_op jit(solution)/shard_map/ppermute | solution.py:23
  21.6 1.8 %collective-permute-start.6 = (s16[720,128]{1,0:T(8,128)(2,1)S(1)}, s16[720,128]{1,0:T(8,128)(2,1)S(1)}, u32[]{:S(2)}, u32[]{:S(2)}) collective-permute-start(s16[720,128]{1,0:T(8,128)(2,1)S(1)} %gate2.1), channel_id=1, source_target_pairs={{0,4},{4,0},{8,12},{12,8},{16,20},{20,16},{24,28},{28,24},{1,5},{5... | collective-permute-start | bytes 552968 | tf_op jit(solution)/shard_map/ppermute | solution.py:23
  23.4 0.0 collective-permute-done.8.refs_0_
  23.4 0.9 %second1.1 = (s16[720,128]{1,0:T(8,128)(2,1)S(1)}, bf16[2,176,512]{2,1,0:T(8,128)(2,1)S(1)}, bf16[2,176,512]{2,1,0:T(8,128)(2,1)S(1)}) custom-call(s16[720,128]{1,0:T(8,128)(2,1)S(1)} %collective-permute-done.8.refs_0_, bf16[512,512]{1,0:T(8,128)(2,1)S(1)} %get-tuple-element.44.refs_1_, bf16[512,512]{1,0:T(8,128)(2,1)S(1)} %get-tuple-element.45.refs_2_, ...), custom_call_target="tpu_custom_call" | custom-call | flops 800000000 | bytes 2400000 | tf_op jit(solution)/shard_map/second1/pallas_call | solution.py:28
  24.3 1.3 %collective-permute-start.9 = (s16[720,128]{1,0:T(8,128)(2,1)S(1)}, s16[720,128]{1,0:T(8,128)(2,1)S(1)}, u32[]{:S(2)}, u32[]{:S(2)}) collective-permute-start(s16[720,128]{1,0:T(8,128)(2,1)S(1)} %get-tuple-element.55), channel_id=1, source_target_pairs={{0,8},{4,12},{8,0},{12,4},{16,24},{20,28},{24,16},{28,20},{1,9},{5... | collective-permute-start | bytes 552968 | tf_op jit(solution)/shard_map/ppermute | solution.py:23
  25.6 0.7 %leaf.1.refs_3_ = f32[2,512,256]{2,1,0:T(8,128)S(1)} custom-call(bf16[2,512,512]{2,1,0:T(8,128)(2,1)S(1)} %copy-done, bf16[2,128,512]{2,1,0:T(8,128)(2,1)S(1)} %relay.1.p2_ref.refs_1_.p_ref, bf16[2,128,512]{2,1,0:T(8,128)(2,1)S(1)} %collective-permute-done.4.p3_ref.refs_2_.q_ref, bf16[2,176,512]{2,1,0:T(8,128)(2,1)S(1)} %get-tuple-element.52.dep_ref.refs_0_), custom_call_target="tpu_custom_call" | custom-call | flops 700000000 | bytes 2100000 | tf_op jit(solution)/shard_map/leaf/pallas_call | solution.py:28
  26.3 0.5 %third0.1 = (f32[2,160,512]{2,1,0:T(8,128)S(1)}, f32[160,512]{1,0:T(8,128)S(1)}) custom-call(bf16[2,160,512]{2,1,0:T(8,128)(2,1)S(1)} %get-tuple-element.47.rest_0_.refs_0_, bf16[2,160,512]{2,1,0:T(8,128)(2,1)S(1)} %get-tuple-element.60.refs_1_, f32[2,512,256]{2,1,0:T(8,128)S(1)} %near.1.dep_ref.rest_1_.refs_2_, f32[2,512,256]{2,1,0:T(8,128)S(1)} %leaf.1.refs_3_, ...), custom_call_target="tpu_custom_call" | custom-call | flops 500000000 | bytes 1500000 | tf_op jit(solution)/shard_map/third0/pallas_call | solution.py:28
  26.8 0.5 %third1.1 = (f32[2,176,512]{2,1,0:T(8,128)S(1)}, f32[176,512]{1,0:T(8,128)S(1)}) custom-call(bf16[2,176,512]{2,1,0:T(8,128)(2,1)S(1)} %get-tuple-element.52.dep_ref.refs_0_, bf16[2,176,512]{2,1,0:T(8,128)(2,1)S(1)} %get-tuple-element.56.refs_1_, f32[2,512,256]{2,1,0:T(8,128)S(1)} %near.1.dep_ref.rest_1_.refs_2_, f32[2,512,256]{2,1,0:T(8,128)S(1)} %leaf.1.refs_3_, ...), custom_call_target="tpu_custom_call" | custom-call | flops 500000000 | bytes 1500000 | tf_op jit(solution)/shard_map/third1/pallas_call | solution.py:28
  27.4 0.0 collective-permute-done.6.refs_0_
  27.4 0.8 %second2.1 = (s16[720,128]{1,0:T(8,128)(2,1)S(1)}, bf16[2,176,512]{2,1,0:T(8,128)(2,1)S(1)}, bf16[2,176,512]{2,1,0:T(8,128)(2,1)S(1)}) custom-call(s16[720,128]{1,0:T(8,128)(2,1)S(1)} %collective-permute-done.6.refs_0_, bf16[512,512]{1,0:T(8,128)(2,1)S(1)} %get-tuple-element.44.refs_1_, bf16[512,512]{1,0:T(8,128)(2,1)S(1)} %get-tuple-element.45.refs_2_, ...), custom_call_target="tpu_custom_call" | custom-call | flops 800000000 | bytes 2400000 | tf_op jit(solution)/shard_map/second2/pallas_call | solution.py:28
  28.2 0.8 %collective-permute-start.7 = (s16[720,128]{1,0:T(8,128)(2,1)S(1)}, s16[720,128]{1,0:T(8,128)(2,1)S(1)}, u32[]{:S(2)}, u32[]{:S(2)}) collective-permute-start(s16[720,128]{1,0:T(8,128)(2,1)S(1)} %get-tuple-element.48), channel_id=1, source_target_pairs={{0,8},{4,12},{8,0},{12,4},{16,24},{20,28},{24,16},{28,20},{1,9},{5... | collective-permute-start | bytes 552968 | tf_op jit(solution)/shard_map/ppermute | solution.py:23
  29.1 0.0 collective-permute-done.10.refs_3_
  29.1 1.5 %last0.1.refs_6_ = f32[2,512,512]{2,1,0:T(8,128)} custom-call(bf16[512,512]{1,0:T(8,128)(2,1)S(1)} %get-tuple-element.39.refs_0_, bf16[512,512]{1,0:T(8,128)(2,1)S(1)} %get-tuple-element.40.refs_1_, bf16[256,512]{1,0:T(8,128)(2,1)S(1)} %get-tuple-element.37.e_ref.refs_3_.refs_6_.refs_2_, s16[656,128]{1,0:T(8,128)(2,1)S(1)} %collective-permute-done.10.refs_3_, ...), custom_call_target="tpu_custom_call" | custom-call | flops 1000000000 | bytes 3000000 | tf_op jit(solution)/shard_map/last0/pallas_call | solution.py:28
  30.6 0.6 %third2.1 = (f32[2,176,512]{2,1,0:T(8,128)S(1)}, f32[176,512]{1,0:T(8,128)S(1)}) custom-call(bf16[2,176,512]{2,1,0:T(8,128)(2,1)S(1)} %get-tuple-element.49.refs_0_, bf16[2,176,512]{2,1,0:T(8,128)(2,1)S(1)} %get-tuple-element.50.refs_1_, f32[2,512,256]{2,1,0:T(8,128)S(1)} %near.1.dep_ref.rest_1_.refs_2_, f32[2,512,256]{2,1,0:T(8,128)S(1)} %leaf.1.refs_3_, ...), custom_call_target="tpu_custom_call" | custom-call | flops 500000000 | bytes 1500000 | tf_op jit(solution)/shard_map/third2/pallas_call | solution.py:28
  31.2 0.0 collective-permute-done.9.refs_3_
  31.2 1.6 %last1.1.refs_6_ = f32[2,512,512]{2,1,0:T(8,128)} custom-call(bf16[512,512]{1,0:T(8,128)(2,1)S(1)} %get-tuple-element.39.refs_0_, bf16[512,512]{1,0:T(8,128)(2,1)S(1)} %get-tuple-element.40.refs_1_, bf16[256,512]{1,0:T(8,128)(2,1)S(1)} %get-tuple-element.37.e_ref.refs_3_.refs_6_.refs_2_, ...), custom_call_target="tpu_custom_call", output_to_operand_aliasing={{}: (6, {})} | custom-call | flops 1000000000 | bytes 3000000 | tf_op jit(solution)/shard_map/last1/pallas_call | solution.py:28
  32.8 1.0 %collective-permute-done.7.refs_3_ = s16[720,128]{1,0:T(8,128)(2,1)S(1)} collective-permute-done((s16[720,128]{1,0:T(8,128)(2,1)S(1)}, s16[720,128]{1,0:T(8,128)(2,1)S(1)}, u32[]{:S(2)}, u32[]{:S(2)}) %collective-permute-start.7) | collective-permute-done | bytes 184352 | tf_op jit(solution)/shard_map/ppermute | solution.py:23
  33.8 1.6 %last2.1 = f32[2,512,512]{2,1,0:T(8,128)} custom-call(bf16[512,512]{1,0:T(8,128)(2,1)S(1)} %get-tuple-element.39.refs_0_, bf16[512,512]{1,0:T(8,128)(2,1)S(1)} %get-tuple-element.40.refs_1_, bf16[256,512]{1,0:T(8,128)(2,1)S(1)} %get-tuple-element.37.e_ref.refs_3_.refs_6_.refs_2_, ...), custom_call_target="tpu_custom_call", output_to_operand_aliasing={{}: (6, {})} | custom-call | flops 1000000000 | bytes 3000000 | tf_op jit(solution)/shard_map/last2/pallas_call | solution.py:28
  (7 shorter events, 0.0 us)
Async XLA Ops:
  0.0 9.5 %collective-permute-start.3 = (bf16[2,128,512]{2,1,0:T(8,128)(2,1)}, bf16[2,128,512]{2,1,0:T(8,128)(2,1)S(1)}, u32[]{:S(2)}, u32[]{:S(2)}) collective-permute-start(bf16[2,128,512]{2,1,0:T(8,128)(2,1)} %bitcast.6), channel_id=1, source_target_pairs={{0,2},{1,3},{2,0},{3,1},{4,6},{5,7},{6,4},{7,5},{8,10},{9,11},{10,... | collective-permute-start | bytes 786440 | tf_op jit(solution)/shard_map/ppermute | solution.py:23
  2.9 1.7 %collective-permute-start.1 = (bf16[2,128,512]{2,1,0:T(8,128)(2,1)}, bf16[2,128,512]{2,1,0:T(8,128)(2,1)S(1)}, u32[]{:S(2)}, u32[]{:S(2)}) collective-permute-start(bf16[2,128,512]{2,1,0:T(8,128)(2,1)} %bitcast.7), channel_id=1, source_target_pairs={{0,1},{1,0},{2,3},{3,2},{4,5},{5,4},{6,7},{7,6},{8,9},{9,8},{10,11... | collective-permute-start | bytes 786440 | tf_op jit(solution)/shard_map/ppermute | solution.py:23
  2.9 1.7 %copy-start.1 = (bf16[1,2,128,512]{3,2,1,0:T(8,128)(2,1)S(1)}, bf16[1,2,128,512]{3,2,1,0:T(8,128)(2,1)}, u32[]{:S(2)}) copy-start(bf16[1,2,128,512]{3,2,1,0:T(8,128)(2,1)} %param.7) | copy-start | bytes 786436
  2.9 1.7 %copy-start.3 = (s32[8,2,256]{2,1,0:T(2,128)S(1)}, s32[8,2,256]{2,1,0:T(2,128)}, u32[]{:S(2)}) copy-start(s32[8,2,256]{2,1,0:T(2,128)} %refs_1_.1) | copy-start | bytes 49156
  2.9 1.7 %copy-start.4 = (f32[512]{0:T(512)S(1)}, f32[512]{0:T(512)}, u32[]{:S(2)}) copy-start(f32[512]{0:T(512)} %param.8) | copy-start | bytes 6148
  3.0 1.7 %copy-start.5 = (s32[8,2]{0,1:T(2,128)S(1)}, s32[8,2]{0,1:T(2,128)}, u32[]{:S(2)}) copy-start(s32[8,2]{0,1:T(2,128)} %param.10) | copy-start | bytes 196
  3.0 4.8 %collective-permute-start = (bf16[128,256]{1,0:T(8,128)(2,1)}, bf16[128,256]{1,0:T(8,128)(2,1)S(1)}, u32[]{:S(2)}, u32[]{:S(2)}) collective-permute-start(bf16[128,256]{1,0:T(8,128)(2,1)} %bitcast.11), channel_id=1, source_target_pairs={{0,4},{4,0},{8,12},{12,8},{16,20},{20,16},{24,28},{28,24},{1,5},{5... | collective-permute-start | bytes 196616 | tf_op jit(solution)/shard_map/ppermute | solution.py:23
  4.5 1.9 %copy-start = (bf16[2,512,512]{2,1,0:T(8,128)(2,1)S(1)}, bf16[2,512,512]{2,1,0:T(8,128)(2,1)}, u32[]{:S(2)}) copy-start(bf16[2,512,512]{2,1,0:T(8,128)(2,1)} %x_ref.5) | copy-start | bytes 3145732
  6.4 1.3 %copy-start.2 = (bf16[2,256,64]{1,2,0:T(8,128)(2,1)S(1)}, bf16[2,256,64]{1,2,0:T(8,128)(2,1)}, u32[]{:S(2)}) copy-start(bf16[2,256,64]{1,2,0:T(8,128)(2,1)} %param.11) | copy-start | bytes 196612
  9.5 2.0 %collective-permute-start.4 = (bf16[2,128,512]{2,1,0:T(8,128)(2,1)S(1)}, bf16[2,128,512]{2,1,0:T(8,128)(2,1)S(1)}, u32[]{:S(2)}, u32[]{:S(2)}) collective-permute-start(bf16[2,128,512]{2,1,0:T(8,128)(2,1)S(1)} %relay.1.p2_ref.refs_1_.p_ref), channel_id=1, source_target_pairs={{0,1},{1,0},{2,3},{3,2},{4,5},{5,4},{6,7},{7,6},{8,9},{9,8},{10,11... | collective-permute-start | bytes 786440 | tf_op jit(solution)/shard_map/ppermute | solution.py:23
  9.6 7.2 %collective-permute-start.2 = (bf16[2,128,256]{2,1,0:T(8,128)(2,1)S(1)}, bf16[2,128,256]{2,1,0:T(8,128)(2,1)S(1)}, u32[]{:S(2)}, u32[]{:S(2)}) collective-permute-start(bf16[2,128,256]{2,1,0:T(8,128)(2,1)S(1)} %pair.1.rest_0_), channel_id=1, source_target_pairs={{0,8},{4,12},{8,0},{12,4},{16,24},{20,28},{24,16},{28,20},{1,9},{5... | collective-permute-start | bytes 393224 | tf_op jit(solution)/shard_map/ppermute | solution.py:23
  12.3 7.0 %collective-permute-start.5 = (s16[656,128]{1,0:T(8,128)(2,1)S(1)}, s16[656,128]{1,0:T(8,128)(2,1)S(1)}, u32[]{:S(2)}, u32[]{:S(2)}) collective-permute-start(s16[656,128]{1,0:T(8,128)(2,1)S(1)} %get-tuple-element.43), channel_id=1, source_target_pairs={{0,4},{4,0},{8,12},{12,8},{16,20},{20,16},{24,28},{28,24},{1,5},{5... | collective-permute-start | bytes 503816 | tf_op jit(solution)/shard_map/ppermute | solution.py:23
  15.5 7.9 %collective-permute-start.8 = (s16[720,128]{1,0:T(8,128)(2,1)S(1)}, s16[720,128]{1,0:T(8,128)(2,1)S(1)}, u32[]{:S(2)}, u32[]{:S(2)}) collective-permute-start(s16[720,128]{1,0:T(8,128)(2,1)S(1)} %ready1.1), channel_id=1, source_target_pairs={{0,4},{4,0},{8,12},{12,8},{16,20},{20,16},{24,28},{28,24},{1,5},{5... | collective-permute-start | bytes 552968 | tf_op jit(solution)/shard_map/ppermute | solution.py:23
  20.1 9.0 %collective-permute-start.10 = (s16[656,128]{1,0:T(8,128)(2,1)S(1)}, s16[656,128]{1,0:T(8,128)(2,1)S(1)}, u32[]{:S(2)}, u32[]{:S(2)}) collective-permute-start(s16[656,128]{1,0:T(8,128)(2,1)S(1)} %get-tuple-element.59), channel_id=1, source_target_pairs={{0,8},{4,12},{8,0},{12,4},{16,24},{20,28},{24,16},{28,20},{1,9},{5... | collective-permute-start | bytes 503816 | tf_op jit(solution)/shard_map/ppermute | solution.py:23
  21.6 5.8 %collective-permute-start.6 = (s16[720,128]{1,0:T(8,128)(2,1)S(1)}, s16[720,128]{1,0:T(8,128)(2,1)S(1)}, u32[]{:S(2)}, u32[]{:S(2)}) collective-permute-start(s16[720,128]{1,0:T(8,128)(2,1)S(1)} %gate2.1), channel_id=1, source_target_pairs={{0,4},{4,0},{8,12},{12,8},{16,20},{20,16},{24,28},{28,24},{1,5},{5... | collective-permute-start | bytes 552968 | tf_op jit(solution)/shard_map/ppermute | solution.py:23
  24.3 6.9 %collective-permute-start.9 = (s16[720,128]{1,0:T(8,128)(2,1)S(1)}, s16[720,128]{1,0:T(8,128)(2,1)S(1)}, u32[]{:S(2)}, u32[]{:S(2)}) collective-permute-start(s16[720,128]{1,0:T(8,128)(2,1)S(1)} %get-tuple-element.55), channel_id=1, source_target_pairs={{0,8},{4,12},{8,0},{12,4},{16,24},{20,28},{24,16},{28,20},{1,9},{5... | collective-permute-start | bytes 552968 | tf_op jit(solution)/shard_map/ppermute | solution.py:23
  28.2 5.6 %collective-permute-start.7 = (s16[720,128]{1,0:T(8,128)(2,1)S(1)}, s16[720,128]{1,0:T(8,128)(2,1)S(1)}, u32[]{:S(2)}, u32[]{:S(2)}) collective-permute-start(s16[720,128]{1,0:T(8,128)(2,1)S(1)} %get-tuple-element.48), channel_id=1, source_target_pairs={{0,8},{4,12},{8,0},{12,4},{16,24},{20,28},{24,16},{28,20},{1,9},{5... | collective-permute-start | bytes 552968 | tf_op jit(solution)/shard_map/ppermute | solution.py:23

commit v4 on v3

--- a/solution.py
+++ b/solution.py
@@ -9,7 +9,7 @@
 WAVENUM = 0.7
 BF = jnp.bfloat16
 F32 = jnp.float32
-SHARES = (10, 11, 11)
+SHARES = (13, 12, 7)
 TOP = 32766.0
 STEPS = 128.0
 LANES = 128
@@ -106,63 +106,85 @@
     out_ref[...] = jnp.zeros(out_ref.shape, out_ref.dtype)
 
 
+def green(own_row, own_box, far_col, far_box):
+    ox, oy, oz = place(own_row, own_box)
+    fx, fy, fz = place(far_col, far_box)
+    d2 = (fx - ox) * (fx - ox) + (fy - oy) * (fy - oy) + (fz - oz) * (fz - oz)
+    dist = jnp.sqrt(d2)
+    inv = 1.0 / dist
+    c, s = cos_sin(WAVENUM * dist)
+    return c * inv, s * inv
+
+
+def store_complex(ref, re, im):
+    k = re.shape[0]
+    ref[0:k, 0:k] = re
+    ref[0:k, k:] = im
+    ref[k:, 0:k] = -im
+    ref[k:, k:] = re
+
+
+def store_halves(hi_ref, lo_ref, re, im):
+    rhi, rlo = halves(re)
+    ihi, ilo = halves(im)
+    store_complex(hi_ref, rhi, ihi)
+    store_complex(lo_ref, rlo, ilo)
+
+
+def matches(col, rank_col, row, rank_row):
+    k = col.shape[0]
+    hit = (col == row) & (iota((k, k), 0) < rank_col) & (iota((k, k), 1) < rank_row)
+    return hit.astype(F32).astype(BF)
+
+
 def plan_body(ranks_ref, skel_ref, contrast_ref, own_ref, beside_ref, dep_ref, *refs, parts):
-    e0_ref, e1_ref, q_ref, ghi_ref, glo_ref, g1_ref, j_ref, d_ref, part_ref = refs
+    e0_ref, e1_ref, q_ref, ghi_ref, glo_ref, g1_ref, j_ref, d_ref, part_ref, hhi_ref, hlo_ref, jp_ref = refs
     box = lax.axis_index("box")
     me = lax.axis_index("field")
     kmax = skel_ref.shape[2]
     width = contrast_ref.shape[1]
     contrast = contrast_ref[...]
-    ranks = ranks_ref[...].astype(F32)
-    ranks = jnp.sum(jnp.where(iota(ranks.shape, 1) == box, ranks, 0.0), axis=1, keepdims=True).astype(jnp.int32)
+    all_ranks = ranks_ref[...].astype(F32)
+
+    def ranks_of(at):
+        mine = jnp.where(iota(all_ranks.shape, 1) == at, all_ranks, 0.0)
+        return jnp.sum(mine, axis=1, keepdims=True).astype(jnp.int32)
+
+    def row_of(at, level):
+        return skel_ref[at][level : level + 1, :]
+
+    def col_of(at, level):
+        return to_column(row_of(at, level).astype(F32)).astype(jnp.int32)
+
+    ranks = ranks_of(box)
     n = width // parts
     lane = iota((kmax, width), 1)
     turned = (((lane // n) ^ me) * n) + lane % n
-    rows = []
     cols = []
-    rank = []
     for level in range(2):
         far = box ^ (1 << level)
-        own_row = skel_ref[box][level : level + 1, :]
-        far_row = skel_ref[far][level : level + 1, :]
-        own_col = to_column(own_row.astype(F32)).astype(jnp.int32)
-        far_col = to_column(far_row.astype(F32)).astype(jnp.int32)
+        own_col = col_of(box, level)
         r = ranks[level : level + 1, :]
-        rows.append(own_row)
         cols.append(own_col)
-        rank.append(r)
         hit = (own_col == turned) & (iota((kmax, width), 0) < r)
         (e0_ref, e1_ref)[level][...] = hit.astype(F32).astype(BF)
         true_hit = (own_col == iota((kmax, width), 1)) & (iota((kmax, width), 0) < r)
         q_col = jnp.sum(jnp.where(true_hit, contrast, 0.0), axis=1, keepdims=True)
         q_ref[pl.ds(level, 1), :] = to_row(q_col, kmax)
-        ox, oy, oz = place(own_row, box)
-        fx, fy, fz = place(far_col, far)
-        d2 = (fx - ox) * (fx - ox) + (fy - oy) * (fy - oy) + (fz - oz) * (fz - oz)
-        dist = jnp.sqrt(d2)
-        inv = 1.0 / dist
-        c, s = cos_sin(WAVENUM * dist)
-        c = c * inv
-        s = s * inv
+        c, s = green(row_of(box, level), box, col_of(far, level), far)
         if level == 0:
-            chi, clo = halves(c)
-            shi, slo = halves(s)
-            ghi_ref[0:kmax, 0:kmax] = chi
-            ghi_ref[0:kmax, kmax:] = shi
-            ghi_ref[kmax:, 0:kmax] = -shi
-            ghi_ref[kmax:, kmax:] = chi
-            glo_ref[0:kmax, 0:kmax] = clo
-            glo_ref[0:kmax, kmax:] = slo
-            glo_ref[kmax:, 0:kmax] = -slo
-            glo_ref[kmax:, kmax:] = clo
+            store_halves(ghi_ref, glo_ref, c, s)
         else:
             g1_ref[:, 0:kmax] = c
             g1_ref[:, kmax:] = s
-    mine = iota((kmax, kmax), 0)
-    other = iota((kmax, kmax), 1)
-    j_ref[...] = ((cols[0] == rows[1]) & (mine < rank[0]) & (other < rank[1])).astype(F32).astype(BF)
-    d_ref[...] = ((cols[1] == rows[1]) & (mine < rank[1]) & (other < rank[1])).astype(F32).astype(BF)
+    j_ref[...] = matches(cols[0], ranks[0:1, :], row_of(box, 1), ranks[1:2, :])
+    d_ref[...] = matches(cols[1], ranks[1:2, :], row_of(box, 1), ranks[1:2, :])
     part_ref[...] = nn(e0_ref[:, : 2 * n], stacked(own_ref, beside_ref)).astype(BF)
+    mate = box ^ 2
+    mate_ranks = ranks_of(mate)
+    c, s = green(row_of(mate, 0), mate, col_of(box ^ 3, 0), box ^ 3)
+    store_halves(hhi_ref, hlo_ref, c, s)
+    jp_ref[...] = matches(col_of(mate, 0), mate_ranks[0:1, :], row_of(mate, 1), mate_ranks[1:2, :])
 
 
 def core_body(own_ref, near_ref, far_ref, g1_ref, d_ref, dep_ref, mc_ref, khi_ref, klo_ref, ct_ref):
@@ -233,12 +255,71 @@
     send(x_ref, picked_ref[...], q_ref, out_ref, start, n)
 
 
-def rows_body(x_ref, p0_ref, p1_ref, p2_ref, p3_ref, e_ref, dep_ref, v_ref):
-    kmax = e_ref.shape[0]
+def rows_body(x_ref, picked_ref, dep_ref, v_ref):
+    kmax = picked_ref.shape[0]
     left, right = turned_fields(x_ref, 0, x_ref.shape[1])
-    picked = nn(e_ref[...], stacked(p0_ref, p1_ref, p2_ref, p3_ref)).astype(BF)
+    picked = picked_ref[...]
     v_ref[:, 0:kmax] = nt(left, picked)
     v_ref[:, kmax:] = nt(right, picked)
+
+
+def ahead_body(x_ref, p0_ref, p1_ref, p2_ref, p3_ref, e1_ref, picked0_ref, q_ref, dep_ref, picked_ref, out_ref, *, start, n):
+    half = out_ref.shape[0] // 2
+    picked0 = picked0_ref[...]
+    picked = nn(e1_ref[...], stacked(p0_ref, p1_ref, p2_ref, p3_ref)).astype(BF)
+    picked_ref[...] = picked
+    left, right = turned_fields(x_ref, start, n)
+    for i, rows in enumerate((picked0, picked)):
+        q = q_ref[i : i + 1, :]
+        w = jnp.concatenate([nt(left, rows) * q, nt(right, rows) * q], axis=1)
+        pack(w, out_ref.at[i * half : (i + 1) * half], q_ref[1:2, :])
+
+
+def onward_body(own_ref, got_ref, out_ref):
+    half = own_ref.shape[0] // 2
+    out_ref[0:half] = own_ref[0:half]
+    out_ref[half:] = got_ref[0:half]
+
+
+def pick(hi, lo, sel):
+    k = sel.shape[0]
+    parts = [nn(hi[:, i : i + k], sel) + nn(lo[:, i : i + k], sel) for i in (0, k)]
+    return jnp.concatenate(parts, axis=1)
+
+
+def around_body(*refs, start):
+    (near_in_ref, mate_ref, ghi_ref, glo_ref, hhi_ref, hlo_ref, j_ref, jp_ref) = refs[:8]
+    (v_ref, near_ref, far_ref, e0_ref, e1_ref, mc_ref, khi_ref, klo_ref, out_ref) = refs[8:]
+    half = near_in_ref.shape[0] // 2
+    n = out_ref.shape[1]
+    k = j_ref.shape[0]
+    lanes = mate_ref.shape[1]
+    count = k // lanes
+    mhi = khi_ref[...]
+    mlo = klo_ref[...]
+    t = apply_packed(near_in_ref.at[half : 2 * half], hhi_ref[...], hlo_ref[...])
+    tail = mate_ref[half - 16 : half, :].astype(jnp.int32).astype(F32)
+    upper = jnp.concatenate([tail[2 + i : 3 + i, :] for i in range(count)], axis=1)
+    lower = jnp.concatenate([tail[2 + count + i : 3 + count + i, :] for i in range(count)], axis=1)
+    q = (upper + lower * (1.0 / 32768.0)) * (1.0 / 16384.0)
+    v, scale = unpack(mate_ref.at[half : 2 * half], 2 * k)
+    w = v.astype(F32) * scale - pick(*halves(t), jp_ref[...]) * jnp.concatenate([q, q], axis=1)
+    hi, lo = halves(w)
+    p = nn(hi, mhi) + (nn(lo, mhi) + nn(hi, mlo))
+    g = apply_packed(near_in_ref.at[0:half], ghi_ref[...], glo_ref[...])
+    gh, gl = halves(g)
+    u = v_ref[start : start + n, :] - pick(gh, gl, j_ref[...])
+    uh, ul = halves(u)
+    mc = mc_ref[...]
+    p = p + (nn(uh, mc) + nn(ul, mc))
+    ph, pl_ = halves(p)
+    e0 = e0_ref[...]
+    e1 = e1_ref[...]
+    for i in range(2):
+        cols = slice(i * k, i * k + k)
+        y = jnp.concatenate([near_ref[i, start : start + n], far_ref[i, start : start + n]], axis=1)
+        scattered = (nn(gh[:, cols], e0) + nn(gl[:, cols], e0)) + (nn(ph[:, cols], e1) + nn(pl_[:, cols], e1))
+        out_ref[i] = y - scattered
 
 
 def leaf_body(x_ref, p_ref, q_ref, dep_ref, y_ref):
@@ -248,7 +329,7 @@
     y_ref[1] = nt(right, a)
 
 
-def pack(w, out_ref):
+def pack(w, out_ref, weight=None):
     n, both = w.shape
     lanes = out_ref.shape[1]
     most = jnp.max(jnp.abs(w), axis=1, keepdims=True)
@@ -262,11 +343,18 @@
     tile = jnp.zeros((16, lanes), F32)
     for i in range(groups):
         tile = jnp.where(iota(tile.shape, 0) == i, step[:, i * lanes : (i + 1) * lanes], tile)
+    if weight is not None:
+        upper = jnp.floor(weight * 16384.0)
+        lower = jnp.floor((weight * 16384.0 - upper) * 32768.0)
+        count = weight.shape[1] // lanes
+        for j, value in enumerate((upper, lower)):
+            for i in range(count):
+                at = iota(tile.shape, 0) == 2 + j * count + i
+                tile = jnp.where(at, value[:, i * lanes : (i + 1) * lanes], tile)
     out_ref[both // lanes * n :, :] = tile.astype(jnp.int32).astype(jnp.int16)
 
 
-def apply_packed(in_ref, mhi, mlo):
-    k = mhi.shape[0]
+def unpack(in_ref, k):
     lanes = in_ref.shape[1]
     pieces = k // lanes
     n = (in_ref.shape[0] - 16) // pieces
@@ -277,6 +365,11 @@
     step = jnp.sum(jnp.where(own, steps, 0.0), axis=1, keepdims=True)
     scale = jnp.exp2(step / STEPS) * (1.0 / TOP)
     v = jnp.concatenate([in_ref[i * n : (i + 1) * n, :] for i in range(pieces)], axis=1).astype(jnp.int32)
+    return v, scale
+
+
+def apply_packed(in_ref, mhi, mlo):
+    v, scale = unpack(in_ref, mhi.shape[0])
     upper = (v + 128) & -256
     lower = (v - upper).astype(F32).astype(BF)
     upper = upper.astype(F32).astype(BF)
@@ -342,9 +435,12 @@
     return write, copies
 
 
-def last_body(khi_ref, klo_ref, e1_ref, in_ref, part_ref, p_ref, *rest, start, blocks):
+def last_body(khi_ref, klo_ref, e1_ref, in_ref, part_ref, p_ref, *rest, start, blocks, done_at):
     out_ref, hold_ref, sem = rest[-3:]
     write, copies = writer(out_ref, sem, blocks)
+    if done_at is not None:
+        for i in range(2):
+            write(rest[0], i, done_at)
     for i, value in finish(in_ref, part_ref, p_ref, khi_ref[...], klo_ref[...], e1_ref[...]):
         hold_ref[i] = value
         write(hold_ref, i, start)
@@ -363,7 +459,7 @@
     core_near = swap(core_own, "box", 1)
     n = n_rows = own.shape[1]
     (opened,) = call(open_body, "open", [shape(8, 128)], [], cost=4.0)
-    e0, e1, q, ghi, glo, g1, dup01, dup11, part = call(
+    e0, e1, q, ghi, glo, g1, dup01, dup11, part, hhi, hlo, dupm = call(
         lambda *refs: plan_body(*refs, parts=lax.axis_size("field")),
         "plan",
         [
@@ -376,6 +472,9 @@
             shape(kmax, kmax, dtype=BF),
             shape(kmax, kmax, dtype=BF),
             shape(kmax, 2 * width, dtype=BF),
+            shape(2 * kmax, 2 * kmax, dtype=BF),
+            shape(2 * kmax, 2 * kmax, dtype=BF),
+            shape(kmax, kmax, dtype=BF),
         ],
         [ranks.T, skel_index, contrast.reshape(1, width), own, beside, opened],
         [VMEM] * 5 + [ANY],
@@ -406,96 +505,85 @@
         cost=0.8,
     )
 
-    def ready(i, dep, gate=None):
-        start, n = sizes[i]
-        (packed,) = call(
-            lambda *refs: rest_body(*refs, start=start, n=n),
-            f"ready{i}",
-            [packed_shape(n, kmax)],
-            [x, picked, q, dep],
-            [VMEM] * 3 + [ANY],
-            cost=0.6,
+    got = swap(head, "box", 1)
+    side_start, side_n = sizes[2]
+    picked1, ahead = call(
+        lambda *refs: ahead_body(*refs, start=side_start, n=side_n),
+        "ahead",
+        [shape(kmax, 2 * width, dtype=BF), shape(2 * packed_shape(side_n, kmax).shape[0], LANES, dtype=jnp.int16)],
+        [x, own, beside, across, beyond, e1, picked, q, e0],
+        [VMEM] * 8 + [ANY],
+        cost=1.4,
+    )
+    mate = swap(ahead, "box", 2)
+    start, n = sizes[1]
+    (packed,) = call(
+        lambda *refs: rest_body(*refs, start=start, n=n),
+        "ready",
+        [packed_shape(n, kmax)],
+        [x, picked, q, ahead],
+        [VMEM] * 3 + [ANY],
+        cost=0.6,
+    )
+    coming = swap(packed, "box", 1)
+    (v1,) = call(rows_body, "rows", [shape(nf, 2 * kmax)], [x, picked1, picked1], [VMEM] * 2 + [ANY])
+    late = []
+    for i, (start, n) in enumerate(sizes[:2]):
+        back, gs, us = call(
+            lambda *refs, start=start: second_body(*refs, start=start),
+            f"second{i}",
+            [packed_shape(n, kmax), shape(2, n, 2 * kmax, dtype=BF), shape(2, n, 2 * kmax, dtype=BF)],
+            [got, ghi, glo, v1, dup01, q, mc if i else e1],
+            [VMEM] * 6 + [ANY],
+            cost=0.8,
         )
-        if i > 1:
-            (packed,) = call(
-                relay_body, f"gate{i}", [packed_shape(n, kmax)], [packed, gate], [VMEM, ANY], cost=0.05
+        got = coming
+        late.append([swap(back, "box", 2), gs, us])
+        if i == 0:
+            (onward,) = call(onward_body, "onward", [shape(*ahead.shape, dtype=jnp.int16)], [ahead, mate], cost=0.05)
+            sent = onward
+            onward = swap(onward, "box", 1)
+            mc, khi, klo = call(
+                core_body,
+                "core",
+                [shape(2 * kmax, 2 * kmax, dtype=BF)] * 3,
+                [core_own, core_near, core_far, g1, dup11, picked1],
+                [VMEM] * 5 + [ANY],
+                [pltpu.VMEM((kmax, 2 * kmax), BF)],
             )
-        return swap(packed, "box", 1)
-
-    got = swap(head, "box", 1)
-    (v1,) = call(
-        rows_body,
-        "rows",
-        [shape(nf, 2 * kmax)],
-        [x, own, beside, across, beyond, e1, e0],
-        [VMEM] * 6 + [ANY],
-    )
-    late = []
-    coming = ready(1, v1)
-
-    def core(dep):
-        return call(
-            core_body,
-            "core",
-            [shape(2 * kmax, 2 * kmax, dtype=BF)] * 3,
-            [core_own, core_near, core_far, g1, dup11, dep],
-            [VMEM] * 5 + [ANY],
-            [pltpu.VMEM((kmax, 2 * kmax), BF)],
-        )
-
-    def third(i):
-        start, n = sizes[i]
+    (far,) = call(
+        leaf_body, "leaf", [shape(2, nf, 2 * n_rows)], [x, across, beyond, mc], [VMEM] * 3 + [ANY], cost=0.7
+    )
+    for i, (start, n) in enumerate(sizes[:2]):
         late[i][1:] = call(
             lambda *refs, start=start: third_body(*refs, start=start),
             f"third{i}",
             [shape(2, n, width), shape(n, 2 * kmax)],
-            [late[i][1], late[i][2], near, y, e0, mc],
+            [late[i][1], late[i][2], near, far, e0, mc],
             cost=0.5,
         )
-
-    for i, (start, n) in enumerate(sizes):
-        dep = e1
-        if i == 1 and 1:
-            dep = mc
-        if i >= 2 and 0:
-            dep = mc if 0 == 1 else late[i - 0][2]
-        back, gs, us = call(
-            lambda *refs, start=start: second_body(*refs, start=start),
-            f"second{i}",
-            [packed_shape(n, kmax), shape(2, n, 2 * kmax, dtype=BF), shape(2, n, 2 * kmax, dtype=BF)],
-            [got, ghi, glo, v1, dup01, q, dep],
-            [VMEM] * 6 + [ANY],
-            cost=0.8,
-        )
-        got = coming
-        if 1:
-            late.append([swap(back, "box", 2), gs, us])
-        if i + 2 < len(sizes):
-            coming = ready(i + 2, e1, gs)
-        if not 1:
-            late.append([swap(back, "box", 2), gs, us])
-        if i == 0:
-            mc, khi, klo = core(v1)
-        if i == 1:
-            (y,) = call(
-                leaf_body, "leaf", [shape(2, nf, 2 * n_rows)], [x, across, beyond, gs], [VMEM] * 3 + [ANY], cost=0.7
-            )
-            for j in range(i + 1):
-                third(j)
-        if i > 1:
-            third(i)
+    side = call(
+        lambda *refs: around_body(*refs, start=side_start),
+        "around",
+        [shape(2, side_n, width)],
+        [onward, mate, ghi, glo, hhi, hlo, dup01, dupm, v1, near, far, e0, e1, mc, khi, klo],
+        cost=2.5,
+    )
     blocks = lax.axis_size("field")
     out = []
-    for i, (start, n) in enumerate(sizes):
+    for i, (start, n) in enumerate(sizes[:2]):
+        ready = side if i == 1 else []
         out = call(
-            lambda *refs, start=start: last_body(*refs, start=start, blocks=blocks),
+            lambda *refs, start=start, ready=ready: last_body(
+                *refs, start=start, blocks=blocks, done_at=side_start if ready else None
+            ),
             f"last{i}",
             [shape(2, nf, width)],
-            [khi, klo, e1] + late[i] + out,
-            [VMEM] * 6 + [ANY] * len(out),
-            [pltpu.VMEM((2, n, width), F32), pltpu.SemaphoreType.DMA((2 * blocks,))],
+            [khi, klo, e1] + late[i] + ready + out,
+            [VMEM] * (6 + len(ready)) + [ANY] * len(out),
+            [pltpu.VMEM((2, n, width), F32), pltpu.SemaphoreType.DMA(((4 if ready else 2) * blocks,))],
             out_specs=[ANY],
-            input_output_aliases={6: 0} if out else {},
+            input_output_aliases={6 + len(ready): 0} if out else {},
         )
     return out[0]
 

time: 35.6 us -> 33.9 us (0.952)
  waiting for transfers between devices: 5.23 us -> 2.58 us
  Pallas kernels: 15.9 us -> 16.5 us
  starting transfers between devices: 14.1 us -> 14.5 us
    ppermute x11, waiting for transfers between devices: 5.23 us -> 2.58 us  [swap(): lax.ppermute(value, axis, [(s, s ^ mask) for s in range(lax.axis_size(axi...]
    pallas_call x21 -> x19, Pallas kernels: 15.9 us -> 16.5 us  [call(): pl.pallas_call(body, name=name, out_shape=outs, in_specs=specs or [VMEM]...]
    ppermute x11, starting transfers between devices: 14.1 us -> 14.5 us  [swap(): lax.ppermute(value, axis, [(s, s ^ mask) for s in range(lax.axis_size(axi...]
  transfers between devices with their start and end apart: 11 -> 11, of which waited for: 5 -> 5; matrix products, arithmetic and copies ran while one was open for 0% -> 0% of each run, Pallas kernels for 40% -> 43%
where the time goes in v4:
time: 33.9 us; the launch traced here: 33.8 us
  Pallas kernels  16.5 us (49%)
  starting transfers between devices  14.5 us (43%)
  waiting for transfers between devices  2.58 us (8%)
    pallas_call x19, Pallas kernels, call(): pl.pallas_call(body, name=name, out_shape=outs, in_specs=specs or [VMEM]...  16.5 us
    ppermute x11, starting transfers between devices, swap(): lax.ppermute(value, axis, [(s, s ^ mask) for s in range(lax.axis_size(axi...  14.5 us
    ppermute x11, waiting for transfers between devices, swap(): lax.ppermute(value, axis, [(s, s ^ mask) for s in range(lax.axis_size(axi...  2.58 us
  transfers between devices with their start and end apart: 11, of which 5 were waited for; matrix products, arithmetic and copies ran while one was open for 0% of the time, Pallas kernels for 43%

profile of v4, /device:TPU:0, one launch (start us, length us, event | category | flops | bytes accessed | tf_op | source)
XLA Modules:
  0.0 33.8 jit_solution(14725919162968124112)
XLA Ops:
  0.0 2.9 %collective-permute-start.3 = (bf16[2,128,512]{2,1,0:T(8,128)(2,1)}, bf16[2,128,512]{2,1,0:T(8,128)(2,1)S(1)}, u32[]{:S(2)}, u32[]{:S(2)}) collective-permute-start(bf16[2,128,512]{2,1,0:T(8,128)(2,1)} %bitcast.6), channel_id=1, source_target_pairs={{0,2},{1,3},{2,0},{3,1},{4,6},{5,7},{6,4},{7,5},{8,10},{9,11},{10,... | collective-permute-start | bytes 786440 | tf_op jit(solution)/shard_map/ppermute | solution.py:23
  2.9 0.0 collective-permute-start.1
  2.9 0.0 copy-start.1
  2.9 0.0 copy-start.3
  2.9 0.0 copy-start.4
  3.0 0.0 copy-start.5
  3.0 1.6 %collective-permute-start = (bf16[128,256]{1,0:T(8,128)(2,1)}, bf16[128,256]{1,0:T(8,128)(2,1)S(1)}, u32[]{:S(2)}, u32[]{:S(2)}) collective-permute-start(bf16[128,256]{1,0:T(8,128)(2,1)} %bitcast.11), channel_id=1, source_target_pairs={{0,4},{4,0},{8,12},{12,8},{16,20},{20,16},{24,28},{28,24},{1,5},{5... | collective-permute-start | bytes 196616 | tf_op jit(solution)/shard_map/ppermute | solution.py:23
  4.6 0.1 collective-permute-done.1.refs_4_.q_ref.refs_2_
  4.7 0.0 copy-done.1
  4.7 0.0 copy-done.3
  4.7 0.0 copy-done.4
  4.7 0.0 copy-done.5
  4.7 2.4 %plan.1 = (bf16[256,512]{1,0:T(8,128)(2,1)S(1)}, bf16[256,512]{1,0:T(8,128)(2,1)S(1)}, f32[8,256]{1,0:T(8,128)S(1)}, bf16[512,512]{1,0:T(8,128)(2,1)S(1)}, bf16[...) custom-call(s32[2,8]{1,0:T(2,128)S(1)} %bitcast.15, ...), custom_call_target="tpu_custom_call" | custom-call | flops 1000000000 | bytes 3000000 | tf_op jit(solution)/shard_map/plan/pallas_call | solution.py:28
  7.1 0.0 copy-start.2
  7.1 0.0 copy-done
  7.2 0.7 %near.1.dep_ref.rest_1_.refs_2_.refs_9_ = f32[2,512,256]{2,1,0:T(8,128)S(1)} custom-call(bf16[2,512,512]{2,1,0:T(8,128)(2,1)S(1)} %copy-done, bf16[2,128,512]{2,1,0:T(8,128)(2,1)S(1)} %bitcast.9, bf16[2,128,512]{2,1,0:T(8,128)(2,1)S(1)} %collective-permute-done.1.refs_4_.q_ref.refs_2_, bf16[256,1024]{1,0:T(8,128)(2,1)S(1)} %get-tuple-element.34.dep_ref.refs_0_), custom_call_target="tpu_custom_call" | custom-call | flops 700000000 | bytes 2100000 | tf_op jit(solution)/shard_map/near/pallas_call | solution.py:28
  7.9 0.0 collective-permute-done.b_ref.near_ref
  7.9 0.1 copy-done.2
  8.0 1.5 %collective-permute-done.3.in_ref = bf16[2,128,512]{2,1,0:T(8,128)(2,1)S(1)} collective-permute-done((bf16[2,128,512]{2,1,0:T(8,128)(2,1)}, bf16[2,128,512]{2,1,0:T(8,128)(2,1)S(1)}, u32[]{:S(2)}, u32[]{:S(2)}) %collective-permute-start.3) | collective-permute-done | bytes 262176 | tf_op jit(solution)/shard_map/ppermute | solution.py:23
  9.5 0.1 collective-permute-start.4
  9.6 1.9 %collective-permute-start.2 = (bf16[2,128,256]{2,1,0:T(8,128)(2,1)S(1)}, bf16[2,128,256]{2,1,0:T(8,128)(2,1)S(1)}, u32[]{:S(2)}, u32[]{:S(2)}) collective-permute-start(bf16[2,128,256]{2,1,0:T(8,128)(2,1)S(1)} %pair.1.rest_0_), channel_id=1, source_target_pairs={{0,8},{4,12},{8,0},{12,4},{16,24},{20,28},{24,16},{28,20},{1,9},{5... | collective-permute-start | bytes 393224 | tf_op jit(solution)/shard_map/ppermute | solution.py:23
  11.4 0.0 collective-permute-done.4.refs_2_.refs_4_.q_ref
  11.5 0.9 %first.1 = (bf16[256,1024]{1,0:T(8,128)(2,1)S(1)}, s16[848,128]{1,0:T(8,128)(2,1)S(1)}) custom-call(bf16[256,1024]{1,0:T(8,128)(2,1)S(1)} %get-tuple-element.34.dep_ref.refs_0_, bf16[2,128,512]{2,1,0:T(8,128)(2,1)S(1)} %relay.1.refs_1_.refs_3_.p_ref, bf16[2,128,512]{2,1,0:T(8,128)(2,1)S(1)} %collective-permute-done.4.refs_2_.refs_4_.q_ref, ...), custom_call_target="tpu_custom_call" | custom-call | flops 800000000 | bytes 2400000 | tf_op jit(solution)/shard_map/first/pallas_call | solution.py:28
  12.3 1.6 %collective-permute-start.9 = (s16[848,128]{1,0:T(8,128)(2,1)S(1)}, s16[848,128]{1,0:T(8,128)(2,1)S(1)}, u32[]{:S(2)}, u32[]{:S(2)}) collective-permute-start(s16[848,128]{1,0:T(8,128)(2,1)S(1)} %get-tuple-element.57), channel_id=1, source_target_pairs={{0,4},{4,0},{8,12},{12,8},{16,20},{20,16},{24,28},{28,24},{1,5},{5... | collective-permute-start | bytes 651272 | tf_op jit(solution)/shard_map/ppermute | solution.py:23
  13.9 1.2 %ahead.1 = (bf16[256,1024]{1,0:T(8,128)(2,1)S(1)}, s16[928,128]{1,0:T(8,128)(2,1)S(1)}) custom-call(bf16[2,512,512]{2,1,0:T(8,128)(2,1)S(1)} %copy-done, bf16[2,128,512]{2,1,0:T(8,128)(2,1)S(1)} %bitcast.10, bf16[2,128,512]{2,1,0:T(8,128)(2,1)S(1)} %collective-permute-done.1.refs_4_.q_ref.refs_2_, bf16[2,128,512]{2,1,0:T(8,128)(2,1)S(1)} %relay.1.refs_1_.refs_3_.p_ref, ...), custom_call_target="tpu_custom_call" | custom-call | flops 1400000000 | bytes 4200000 | tf_op jit(solution)/shard_map/ahead/pallas_call | solution.py:28
  15.1 1.5 %collective-permute-start.7 = (s16[928,128]{1,0:T(8,128)(2,1)S(1)}, s16[928,128]{1,0:T(8,128)(2,1)S(1)}, u32[]{:S(2)}, u32[]{:S(2)}) collective-permute-start(s16[928,128]{1,0:T(8,128)(2,1)S(1)} %get-tuple-element.44.refs_3_.own_ref), channel_id=1, source_target_pairs={{0,8},{4,12},{8,0},{12,4},{16,24},{20,28},{24,16},{28,20},{1,9},{5... | collective-permute-start | bytes 712712 | tf_op jit(solution)/shard_map/ppermute | solution.py:23
  16.6 0.7 %ready.1 = s16[784,128]{1,0:T(8,128)(2,1)S(1)} custom-call(bf16[2,512,512]{2,1,0:T(8,128)(2,1)S(1)} %copy-done, bf16[256,1024]{1,0:T(8,128)(2,1)S(1)} %get-tuple-element.40.refs_6_.refs_1_, f32[8,256]{1,0:T(8,128)S(1)} %get-tuple-element.39.refs_5_.refs_7_.refs_2_, s16[928,128]{1,0:T(8,128)(2,1)S(1)} %get-tuple-element.44.refs_3_.own_ref), custom_call_target="tpu_custom_call" | custom-call | flops 600000000 | bytes 1800000 | tf_op jit(solution)/shard_map/ready/pallas_call | solution.py:28
  17.3 0.6 %collective-permute-start.5 = (s16[784,128]{1,0:T(8,128)(2,1)S(1)}, s16[784,128]{1,0:T(8,128)(2,1)S(1)}, u32[]{:S(2)}, u32[]{:S(2)}) collective-permute-start(s16[784,128]{1,0:T(8,128)(2,1)S(1)} %ready.1), channel_id=1, source_target_pairs={{0,4},{4,0},{8,12},{12,8},{16,20},{20,16},{24,28},{28,24},{1,5},{5... | collective-permute-start | bytes 602120 | tf_op jit(solution)/shard_map/ppermute | solution.py:23
  17.8 0.7 %rows.1.refs_3_.refs_8_ = f32[512,512]{1,0:T(8,128)S(1)} custom-call(bf16[2,512,512]{2,1,0:T(8,128)(2,1)S(1)} %copy-done, bf16[256,1024]{1,0:T(8,128)(2,1)S(1)} %get-tuple-element.41.dep_ref.picked_ref, bf16[256,1024]{1,0:T(8,128)(2,1)S(1)} %get-tuple-element.41.dep_ref.picked_ref), custom_call_target="tpu_custom_call" | custom-call | flops 1000000000 | bytes 3000000 | tf_op jit(solution)/shard_map/rows/pallas_call | solution.py:28
  18.6 0.0 collective-permute-done.2.far_ref
  18.6 0.8 %core.1 = (bf16[512,512]{1,0:T(8,128)(2,1)S(1)}, bf16[512,512]{1,0:T(8,128)(2,1)S(1)}, bf16[512,512]{1,0:T(8,128)(2,1)S(1)}) custom-call(bf16[128,256]{1,0:T(8,128)(2,1)S(1)} %bitcast.13, bf16[128,256]{1,0:T(8,128)(2,1)S(1)} %collective-permute-done.b_ref.near_ref, bf16[2,128,256]{2,1,0:T(8,128)(2,1)S(1)} %collective-permute-done.2.far_ref, ...), custom_call_target="tpu_custom_call" | custom-call | flops 1000000000 | bytes 3000000 | tf_op jit(solution)/shard_map/core/pallas_call | solution.py:28
  19.4 0.6 %collective-permute-done.9.refs_0_ = s16[848,128]{1,0:T(8,128)(2,1)S(1)} collective-permute-done((s16[848,128]{1,0:T(8,128)(2,1)S(1)}, s16[848,128]{1,0:T(8,128)(2,1)S(1)}, u32[]{:S(2)}, u32[]{:S(2)}) %collective-permute-start.9) | collective-permute-done | bytes 217120 | tf_op jit(solution)/shard_map/ppermute | solution.py:23
  20.0 0.9 %second0.1 = (s16[848,128]{1,0:T(8,128)(2,1)S(1)}, bf16[2,208,512]{2,1,0:T(8,128)(2,1)S(1)}, bf16[2,208,512]{2,1,0:T(8,128)(2,1)S(1)}) custom-call(s16[848,128]{1,0:T(8,128)(2,1)S(1)} %collective-permute-done.9.refs_0_, bf16[512,512]{1,0:T(8,128)(2,1)S(1)} %get-tuple-element.45.refs_1_.refs_2_, bf16[512,512]{1,0:T(8,128)(2,1)S(1)} %get-tuple-element.46.refs_2_.refs_3_, ...), custom_call_target="tpu_custom_call" | custom-call | flops 800000000 | bytes 2400000 | tf_op jit(solution)/shard_map/second0/pallas_call | solution.py:28
  20.9 2.1 %collective-permute-start.10 = (s16[848,128]{1,0:T(8,128)(2,1)S(1)}, s16[848,128]{1,0:T(8,128)(2,1)S(1)}, u32[]{:S(2)}, u32[]{:S(2)}) collective-permute-start(s16[848,128]{1,0:T(8,128)(2,1)S(1)} %get-tuple-element.58), channel_id=1, source_target_pairs={{0,8},{4,12},{8,0},{12,4},{16,24},{20,28},{24,16},{28,20},{1,9},{5... | collective-permute-start | bytes 651272 | tf_op jit(solution)/shard_map/ppermute | solution.py:23
  23.0 0.7 %leaf.1.refs_3_.refs_10_ = f32[2,512,256]{2,1,0:T(8,128)S(1)} custom-call(bf16[2,512,512]{2,1,0:T(8,128)(2,1)S(1)} %copy-done, bf16[2,128,512]{2,1,0:T(8,128)(2,1)S(1)} %relay.1.refs_1_.refs_3_.p_ref, bf16[2,128,512]{2,1,0:T(8,128)(2,1)S(1)} %collective-permute-done.4.refs_2_.refs_4_.q_ref, ...), custom_call_target="tpu_custom_call" | custom-call | flops 700000000 | bytes 2100000 | tf_op jit(solution)/shard_map/leaf/pallas_call | solution.py:28
  23.7 0.0 collective-permute-done.7.got_ref.refs_1_
  23.8 1.6 %collective-permute-start.8 = (s16[928,128]{1,0:T(8,128)(2,1)S(1)}, s16[928,128]{1,0:T(8,128)(2,1)S(1)}, u32[]{:S(2)}, u32[]{:S(2)}) collective-permute-start(s16[928,128]{1,0:T(8,128)(2,1)S(1)} %onward.1), channel_id=1, source_target_pairs={{0,4},{4,0},{8,12},{12,8},{16,20},{20,16},{24,28},{28,24},{1,5},{5... | collective-permute-start | bytes 712712 | tf_op jit(solution)/shard_map/ppermute | solution.py:23
  25.4 0.0 collective-permute-done.5.refs_0_
  25.4 0.9 %second1.1 = (s16[784,128]{1,0:T(8,128)(2,1)S(1)}, bf16[2,192,512]{2,1,0:T(8,128)(2,1)S(1)}, bf16[2,192,512]{2,1,0:T(8,128)(2,1)S(1)}) custom-call(s16[784,128]{1,0:T(8,128)(2,1)S(1)} %collective-permute-done.5.refs_0_, bf16[512,512]{1,0:T(8,128)(2,1)S(1)} %get-tuple-element.45.refs_1_.refs_2_, bf16[512,512]{1,0:T(8,128)(2,1)S(1)} %get-tuple-element.46.refs_2_.refs_3_, ...), custom_call_target="tpu_custom_call" | custom-call | flops 800000000 | bytes 2400000 | tf_op jit(solution)/shard_map/second1/pallas_call | solution.py:28
  26.2 0.6 %collective-permute-start.6 = (s16[784,128]{1,0:T(8,128)(2,1)S(1)}, s16[784,128]{1,0:T(8,128)(2,1)S(1)}, u32[]{:S(2)}, u32[]{:S(2)}) collective-permute-start(s16[784,128]{1,0:T(8,128)(2,1)S(1)} %get-tuple-element.49), channel_id=1, source_target_pairs={{0,8},{4,12},{8,0},{12,4},{16,24},{20,28},{24,16},{28,20},{1,9},{5... | collective-permute-start | bytes 602120 | tf_op jit(solution)/shard_map/ppermute | solution.py:23
  26.9 0.6 %third1.1 = (f32[2,192,512]{2,1,0:T(8,128)S(1)}, f32[192,512]{1,0:T(8,128)S(1)}) custom-call(bf16[2,192,512]{2,1,0:T(8,128)(2,1)S(1)} %get-tuple-element.50.refs_0_, bf16[2,192,512]{2,1,0:T(8,128)(2,1)S(1)} %get-tuple-element.51.refs_1_, f32[2,512,256]{2,1,0:T(8,128)S(1)} %near.1.dep_ref.rest_1_.refs_2_.refs_9_, f32[2,512,256]{2,1,0:T(8,128)S(1)} %leaf.1.refs_3_.refs_10_, ...), custom_call_target="tpu_custom_call" | custom-call | flops 500000000 | bytes 1500000 | tf_op jit(solution)/shard_map/third1/pallas_call | solution.py:28
  27.4 0.6 %third0.1 = (f32[2,208,512]{2,1,0:T(8,128)S(1)}, f32[208,512]{1,0:T(8,128)S(1)}) custom-call(bf16[2,208,512]{2,1,0:T(8,128)(2,1)S(1)} %get-tuple-element.59.refs_0_, bf16[2,208,512]{2,1,0:T(8,128)(2,1)S(1)} %get-tuple-element.60.refs_1_, f32[2,512,256]{2,1,0:T(8,128)S(1)} %near.1.dep_ref.rest_1_.refs_2_.refs_9_, f32[2,512,256]{2,1,0:T(8,128)S(1)} %leaf.1.refs_3_.refs_10_, ...), custom_call_target="tpu_custom_call" | custom-call | flops 500000000 | bytes 1500000 | tf_op jit(solution)/shard_map/third0/pallas_call | solution.py:28
  28.1 0.0 collective-permute-done.10.refs_3_
  28.1 1.7 %last0.1.refs_7_ = f32[2,512,512]{2,1,0:T(8,128)} custom-call(bf16[512,512]{1,0:T(8,128)(2,1)S(1)} %get-tuple-element.42.refs_14_.refs_0_, bf16[512,512]{1,0:T(8,128)(2,1)S(1)} %get-tuple-element.43.refs_15_.refs_1_, bf16[256,512]{1,0:T(8,128)(2,1)S(1)} %get-tuple-element.37.refs_5_.refs_12_.refs_6_.refs_2_, ...), custom_call_target="tpu_custom_call" | custom-call | flops 1000000000 | bytes 3000000 | tf_op jit(solution)/shard_map/last0/pallas_call | solution.py:28
  29.8 0.2 collective-permute-done.8.refs_0_
  29.9 1.9 %around.1.refs_6_ = f32[2,112,512]{2,1,0:T(8,128)S(1)} custom-call(s16[928,128]{1,0:T(8,128)(2,1)S(1)} %collective-permute-done.8.refs_0_, s16[928,128]{1,0:T(8,128)(2,1)S(1)} %collective-permute-done.7.got_ref.refs_1_, bf16[512,512]{1,0:T(8,128)(2,1)S(1)} %get-tuple-element.45.refs_1_.refs_2_, bf16[512,512]{1,0:T(8,128)(2,1)S(1)} %get-tuple-element.46.refs_2_.refs_3_, ...), custom_call_target="tpu_custom_call" | custom-call | flops 2500000000 | bytes 7500000 | tf_op jit(solution)/shard_map/around/pallas_call | solution.py:28
  31.8 0.2 collective-permute-done.6.refs_3_
  32.0 1.8 %last1.1 = f32[2,512,512]{2,1,0:T(8,128)} custom-call(bf16[512,512]{1,0:T(8,128)(2,1)S(1)} %get-tuple-element.42.refs_14_.refs_0_, bf16[512,512]{1,0:T(8,128)(2,1)S(1)} %get-tuple-element.43.refs_15_.refs_1_, bf16[256,512]{1,0:T(8,128)(2,1)S(1)} %get-tuple-element.37.refs_5_.refs_12_.refs_6_.refs_2_, ...), custom_call_target="tpu_custom_call", output_to_operand_aliasing={{}: (7, {})} | custom-call | flops 1000000000 | bytes 3000000 | tf_op jit(solution)/shard_map/last1/pallas_call | solution.py:28
  (5 shorter events, 0.0 us)
Async XLA Ops:
  0.0 9.5 %collective-permute-start.3 = (bf16[2,128,512]{2,1,0:T(8,128)(2,1)}, bf16[2,128,512]{2,1,0:T(8,128)(2,1)S(1)}, u32[]{:S(2)}, u32[]{:S(2)}) collective-permute-start(bf16[2,128,512]{2,1,0:T(8,128)(2,1)} %bitcast.6), channel_id=1, source_target_pairs={{0,2},{1,3},{2,0},{3,1},{4,6},{5,7},{6,4},{7,5},{8,10},{9,11},{10,... | collective-permute-start | bytes 786440 | tf_op jit(solution)/shard_map/ppermute | solution.py:23
  2.9 1.7 %collective-permute-start.1 = (bf16[2,128,512]{2,1,0:T(8,128)(2,1)}, bf16[2,128,512]{2,1,0:T(8,128)(2,1)S(1)}, u32[]{:S(2)}, u32[]{:S(2)}) collective-permute-start(bf16[2,128,512]{2,1,0:T(8,128)(2,1)} %bitcast.7), channel_id=1, source_target_pairs={{0,1},{1,0},{2,3},{3,2},{4,5},{5,4},{6,7},{7,6},{8,9},{9,8},{10,11... | collective-permute-start | bytes 786440 | tf_op jit(solution)/shard_map/ppermute | solution.py:23
  2.9 1.7 %copy-start.1 = (bf16[1,2,128,512]{3,2,1,0:T(8,128)(2,1)S(1)}, bf16[1,2,128,512]{3,2,1,0:T(8,128)(2,1)}, u32[]{:S(2)}) copy-start(bf16[1,2,128,512]{3,2,1,0:T(8,128)(2,1)} %param.7) | copy-start | bytes 786436
  2.9 1.7 %copy-start.3 = (s32[8,2,256]{2,1,0:T(2,128)S(1)}, s32[8,2,256]{2,1,0:T(2,128)}, u32[]{:S(2)}) copy-start(s32[8,2,256]{2,1,0:T(2,128)} %refs_1_.1) | copy-start | bytes 49156
  2.9 1.7 %copy-start.4 = (f32[512]{0:T(512)S(1)}, f32[512]{0:T(512)}, u32[]{:S(2)}) copy-start(f32[512]{0:T(512)} %param.8) | copy-start | bytes 6148
  3.0 1.7 %copy-start.5 = (s32[8,2]{0,1:T(2,128)S(1)}, s32[8,2]{0,1:T(2,128)}, u32[]{:S(2)}) copy-start(s32[8,2]{0,1:T(2,128)} %param.10) | copy-start | bytes 196
  3.0 4.9 %collective-permute-start = (bf16[128,256]{1,0:T(8,128)(2,1)}, bf16[128,256]{1,0:T(8,128)(2,1)S(1)}, u32[]{:S(2)}, u32[]{:S(2)}) collective-permute-start(bf16[128,256]{1,0:T(8,128)(2,1)} %bitcast.11), channel_id=1, source_target_pairs={{0,4},{4,0},{8,12},{12,8},{16,20},{20,16},{24,28},{28,24},{1,5},{5... | collective-permute-start | bytes 196616 | tf_op jit(solution)/shard_map/ppermute | solution.py:23
  4.5 2.6 %copy-start = (bf16[2,512,512]{2,1,0:T(8,128)(2,1)S(1)}, bf16[2,512,512]{2,1,0:T(8,128)(2,1)}, u32[]{:S(2)}) copy-start(bf16[2,512,512]{2,1,0:T(8,128)(2,1)} %x_ref.5) | copy-start | bytes 3145732
  7.1 0.8 %copy-start.2 = (bf16[2,256,64]{1,2,0:T(8,128)(2,1)S(1)}, bf16[2,256,64]{1,2,0:T(8,128)(2,1)}, u32[]{:S(2)}) copy-start(bf16[2,256,64]{1,2,0:T(8,128)(2,1)} %param.11) | copy-start | bytes 196612
  9.5 2.0 %collective-permute-start.4 = (bf16[2,128,512]{2,1,0:T(8,128)(2,1)S(1)}, bf16[2,128,512]{2,1,0:T(8,128)(2,1)S(1)}, u32[]{:S(2)}, u32[]{:S(2)}) collective-permute-start(bf16[2,128,512]{2,1,0:T(8,128)(2,1)S(1)} %relay.1.refs_1_.refs_3_.p_ref), channel_id=1, source_target_pairs={{0,1},{1,0},{2,3},{3,2},{4,5},{5,4},{6,7},{7,6},{8,9},{9,8},{10,11... | collective-permute-start | bytes 786440 | tf_op jit(solution)/shard_map/ppermute | solution.py:23
  9.6 9.0 %collective-permute-start.2 = (bf16[2,128,256]{2,1,0:T(8,128)(2,1)S(1)}, bf16[2,128,256]{2,1,0:T(8,128)(2,1)S(1)}, u32[]{:S(2)}, u32[]{:S(2)}) collective-permute-start(bf16[2,128,256]{2,1,0:T(8,128)(2,1)S(1)} %pair.1.rest_0_), channel_id=1, source_target_pairs={{0,8},{4,12},{8,0},{12,4},{16,24},{20,28},{24,16},{28,20},{1,9},{5... | collective-permute-start | bytes 393224 | tf_op jit(solution)/shard_map/ppermute | solution.py:23
  12.3 7.7 %collective-permute-start.9 = (s16[848,128]{1,0:T(8,128)(2,1)S(1)}, s16[848,128]{1,0:T(8,128)(2,1)S(1)}, u32[]{:S(2)}, u32[]{:S(2)}) collective-permute-start(s16[848,128]{1,0:T(8,128)(2,1)S(1)} %get-tuple-element.57), channel_id=1, source_target_pairs={{0,4},{4,0},{8,12},{12,8},{16,20},{20,16},{24,28},{28,24},{1,5},{5... | collective-permute-start | bytes 651272 | tf_op jit(solution)/shard_map/ppermute | solution.py:23
  15.1 8.7 %collective-permute-start.7 = (s16[928,128]{1,0:T(8,128)(2,1)S(1)}, s16[928,128]{1,0:T(8,128)(2,1)S(1)}, u32[]{:S(2)}, u32[]{:S(2)}) collective-permute-start(s16[928,128]{1,0:T(8,128)(2,1)S(1)} %get-tuple-element.44.refs_3_.own_ref), channel_id=1, source_target_pairs={{0,8},{4,12},{8,0},{12,4},{16,24},{20,28},{24,16},{28,20},{1,9},{5... | collective-permute-start | bytes 712712 | tf_op jit(solution)/shard_map/ppermute | solution.py:23
  17.3 8.1 %collective-permute-start.5 = (s16[784,128]{1,0:T(8,128)(2,1)S(1)}, s16[784,128]{1,0:T(8,128)(2,1)S(1)}, u32[]{:S(2)}, u32[]{:S(2)}) collective-permute-start(s16[784,128]{1,0:T(8,128)(2,1)S(1)} %ready.1), channel_id=1, source_target_pairs={{0,4},{4,0},{8,12},{12,8},{16,20},{20,16},{24,28},{28,24},{1,5},{5... | collective-permute-start | bytes 602120 | tf_op jit(solution)/shard_map/ppermute | solution.py:23
  20.9 7.2 %collective-permute-start.10 = (s16[848,128]{1,0:T(8,128)(2,1)S(1)}, s16[848,128]{1,0:T(8,128)(2,1)S(1)}, u32[]{:S(2)}, u32[]{:S(2)}) collective-permute-start(s16[848,128]{1,0:T(8,128)(2,1)S(1)} %get-tuple-element.58), channel_id=1, source_target_pairs={{0,8},{4,12},{8,0},{12,4},{16,24},{20,28},{24,16},{28,20},{1,9},{5... | collective-permute-start | bytes 651272 | tf_op jit(solution)/shard_map/ppermute | solution.py:23
  23.8 6.2 %collective-permute-start.8 = (s16[928,128]{1,0:T(8,128)(2,1)S(1)}, s16[928,128]{1,0:T(8,128)(2,1)S(1)}, u32[]{:S(2)}, u32[]{:S(2)}) collective-permute-start(s16[928,128]{1,0:T(8,128)(2,1)S(1)} %onward.1), channel_id=1, source_target_pairs={{0,4},{4,0},{8,12},{12,8},{16,20},{20,16},{24,28},{28,24},{1,5},{5... | collective-permute-start | bytes 712712 | tf_op jit(solution)/shard_map/ppermute | solution.py:23
  26.2 5.8 %collective-permute-start.6 = (s16[784,128]{1,0:T(8,128)(2,1)S(1)}, s16[784,128]{1,0:T(8,128)(2,1)S(1)}, u32[]{:S(2)}, u32[]{:S(2)}) collective-permute-start(s16[784,128]{1,0:T(8,128)(2,1)S(1)} %get-tuple-element.49), channel_id=1, source_target_pairs={{0,8},{4,12},{8,0},{12,4},{16,24},{20,28},{24,16},{28,20},{1,9},{5... | collective-permute-start | bytes 602120 | tf_op jit(solution)/shard_map/ppermute | solution.py:23

commit v5 on v4

--- a/solution.py
+++ b/solution.py
@@ -244,11 +244,20 @@
     pack(w, out_ref)
 
 
-def first_body(part_ref, across_ref, beyond_ref, e0_ref, x_ref, q_ref, picked_ref, out_ref, *, start, n):
+def first_body(part_ref, across_ref, beyond_ref, e0_ref, x_ref, q_ref, picked_ref, out_ref, side_ref, *, start, n, side_start):
     rows = across_ref.shape[1]
     picked = (nn(e0_ref[:, 2 * rows :], stacked(across_ref, beyond_ref)) + part_ref[...].astype(F32)).astype(BF)
     picked_ref[...] = picked
-    send(x_ref, picked, q_ref, out_ref, start, n)
+    q = q_ref[0:1, :]
+    kmax = picked.shape[0]
+    side_n = (side_ref.shape[0] - 16) * LANES // (2 * kmax)
+    left, right = turned_fields(x_ref, start, n)
+    more_left, more_right = turned_fields(x_ref, side_start, side_n)
+    left = jnp.concatenate([left, more_left], axis=0)
+    right = jnp.concatenate([right, more_right], axis=0)
+    w = jnp.concatenate([nt(left, picked) * q, nt(right, picked) * q], axis=1)
+    pack(w[:n], out_ref)
+    pack(w[n:], side_ref, q_ref[1:2, :])
 
 
 def rest_body(x_ref, picked_ref, q_ref, dep_ref, out_ref, *, start, n):
@@ -263,16 +272,15 @@
     v_ref[:, kmax:] = nt(right, picked)
 
 
-def ahead_body(x_ref, p0_ref, p1_ref, p2_ref, p3_ref, e1_ref, picked0_ref, q_ref, dep_ref, picked_ref, out_ref, *, start, n):
+def ahead_body(x_ref, p0_ref, p1_ref, p2_ref, p3_ref, e1_ref, side_ref, q_ref, dep_ref, picked_ref, out_ref, *, start, n):
     half = out_ref.shape[0] // 2
-    picked0 = picked0_ref[...]
+    out_ref[0:half] = side_ref[...]
     picked = nn(e1_ref[...], stacked(p0_ref, p1_ref, p2_ref, p3_ref)).astype(BF)
     picked_ref[...] = picked
     left, right = turned_fields(x_ref, start, n)
-    for i, rows in enumerate((picked0, picked)):
-        q = q_ref[i : i + 1, :]
-        w = jnp.concatenate([nt(left, rows) * q, nt(right, rows) * q], axis=1)
-        pack(w, out_ref.at[i * half : (i + 1) * half], q_ref[1:2, :])
+    q = q_ref[1:2, :]
+    w = jnp.concatenate([nt(left, picked) * q, nt(right, picked) * q], axis=1)
+    pack(w, out_ref.at[half : 2 * half])
 
 
 def onward_body(own_ref, got_ref, out_ref):
@@ -395,7 +403,7 @@
     us_ref[1] = lo
 
 
-def third_body(gs_ref, us_ref, near_ref, far_ref, e0_ref, mc_ref, part_ref, p_ref, *, start):
+def third_body(gs_ref, us_ref, near_ref, far_ref, e0_ref, mc_ref, dep_ref, part_ref, p_ref, *, start):
     n = gs_ref.shape[1]
     k = e0_ref.shape[0]
     e = e0_ref[...]
@@ -494,24 +502,25 @@
     chunks = [nf // sum(SHARES) * share for share in SHARES]
     sizes = [(sum(chunks[:i]), n) for i, n in enumerate(chunks)]
     start, n = sizes[0]
-    picked, head = call(
-        lambda *refs, start=start, n=n: first_body(*refs, start=start, n=n),
+    side_start, side_n = sizes[2]
+    picked, head, side = call(
+        lambda *refs, start=start, n=n: first_body(*refs, start=start, n=n, side_start=side_start),
         "first",
         [
             shape(kmax, 2 * width, dtype=BF),
             packed_shape(n, kmax),
+            packed_shape(side_n, kmax),
         ],
         [part, across, beyond, e0, x, q],
         cost=0.8,
     )
 
     got = swap(head, "box", 1)
-    side_start, side_n = sizes[2]
     picked1, ahead = call(
         lambda *refs: ahead_body(*refs, start=side_start, n=side_n),
         "ahead",
         [shape(kmax, 2 * width, dtype=BF), shape(2 * packed_shape(side_n, kmax).shape[0], LANES, dtype=jnp.int16)],
-        [x, own, beside, across, beyond, e1, picked, q, e0],
+        [x, own, beside, across, beyond, e1, side, q, e0],
         [VMEM] * 8 + [ANY],
         cost=1.4,
     )
@@ -526,14 +535,25 @@
         cost=0.6,
     )
     coming = swap(packed, "box", 1)
-    (v1,) = call(rows_body, "rows", [shape(nf, 2 * kmax)], [x, picked1, picked1], [VMEM] * 2 + [ANY])
+    (v1,) = call(rows_body, "rows", [shape(nf, 2 * kmax)], [x, picked1, packed], [VMEM] * 2 + [ANY])
+    mc, khi, klo = call(
+        core_body,
+        "core",
+        [shape(2 * kmax, 2 * kmax, dtype=BF)] * 3,
+        [core_own, core_near, core_far, g1, dup11, v1],
+        [VMEM] * 5 + [ANY],
+        [pltpu.VMEM((kmax, 2 * kmax), BF)],
+    )
+    (far,) = call(
+        leaf_body, "leaf", [shape(2, nf, 2 * n_rows)], [x, across, beyond, mc], [VMEM] * 3 + [ANY], cost=0.7
+    )
     late = []
     for i, (start, n) in enumerate(sizes[:2]):
         back, gs, us = call(
             lambda *refs, start=start: second_body(*refs, start=start),
             f"second{i}",
             [packed_shape(n, kmax), shape(2, n, 2 * kmax, dtype=BF), shape(2, n, 2 * kmax, dtype=BF)],
-            [got, ghi, glo, v1, dup01, q, mc if i else e1],
+            [got, ghi, glo, v1, dup01, q, sent if i else far],
             [VMEM] * 6 + [ANY],
             cost=0.8,
         )
@@ -543,23 +563,13 @@
             (onward,) = call(onward_body, "onward", [shape(*ahead.shape, dtype=jnp.int16)], [ahead, mate], cost=0.05)
             sent = onward
             onward = swap(onward, "box", 1)
-            mc, khi, klo = call(
-                core_body,
-                "core",
-                [shape(2 * kmax, 2 * kmax, dtype=BF)] * 3,
-                [core_own, core_near, core_far, g1, dup11, picked1],
-                [VMEM] * 5 + [ANY],
-                [pltpu.VMEM((kmax, 2 * kmax), BF)],
-            )
-    (far,) = call(
-        leaf_body, "leaf", [shape(2, nf, 2 * n_rows)], [x, across, beyond, mc], [VMEM] * 3 + [ANY], cost=0.7
-    )
     for i, (start, n) in enumerate(sizes[:2]):
         late[i][1:] = call(
             lambda *refs, start=start: third_body(*refs, start=start),
             f"third{i}",
             [shape(2, n, width), shape(n, 2 * kmax)],
-            [late[i][1], late[i][2], near, far, e0, mc],
+            [late[i][1], late[i][2], near, far, e0, mc, gs],
+            [VMEM] * 6 + [ANY],
             cost=0.5,
         )
     side = call(

time: 33.9 us -> 33.6 us (level)
  no operation moved by 1% of the time
where the time goes in v5:
time: 33.6 us; the launch traced here: 33.5 us
  Pallas kernels  16.2 us (48%)
  starting transfers between devices  14.5 us (43%)
  waiting for transfers between devices  2.58 us (8%)
    pallas_call x19, Pallas kernels, call(): pl.pallas_call(body, name=name, out_shape=outs, in_specs=specs or [VMEM]...  16.2 us
    ppermute x11, starting transfers between devices, swap(): lax.ppermute(value, axis, [(s, s ^ mask) for s in range(lax.axis_size(axi...  14.5 us
    ppermute x11, waiting for transfers between devices, swap(): lax.ppermute(value, axis, [(s, s ^ mask) for s in range(lax.axis_size(axi...  2.58 us
  transfers between devices with their start and end apart: 11, of which 5 were waited for; matrix products, arithmetic and copies ran while one was open for 0% of the time, Pallas kernels for 43%

profile of v5, /device:TPU:0, one launch (start us, length us, event | category | flops | bytes accessed | tf_op | source)
XLA Modules:
  0.0 33.5 jit_solution(17683478122923668807)
XLA Ops:
  0.0 2.9 %collective-permute-start.3 = (bf16[2,128,512]{2,1,0:T(8,128)(2,1)}, bf16[2,128,512]{2,1,0:T(8,128)(2,1)S(1)}, u32[]{:S(2)}, u32[]{:S(2)}) collective-permute-start(bf16[2,128,512]{2,1,0:T(8,128)(2,1)} %bitcast.6), channel_id=1, source_target_pairs={{0,2},{1,3},{2,0},{3,1},{4,6},{5,7},{6,4},{7,5},{8,10},{9,11},{10,... | collective-permute-start | bytes 786440 | tf_op jit(solution)/shard_map/ppermute | solution.py:23
  2.9 0.0 collective-permute-start.1
  2.9 0.0 copy-start.1
  2.9 0.0 copy-start.3
  2.9 0.0 copy-start.4
  3.0 0.0 copy-start.5
  3.0 1.6 %collective-permute-start = (bf16[128,256]{1,0:T(8,128)(2,1)}, bf16[128,256]{1,0:T(8,128)(2,1)S(1)}, u32[]{:S(2)}, u32[]{:S(2)}) collective-permute-start(bf16[128,256]{1,0:T(8,128)(2,1)} %bitcast.11), channel_id=1, source_target_pairs={{0,4},{4,0},{8,12},{12,8},{16,20},{20,16},{24,28},{28,24},{1,5},{5... | collective-permute-start | bytes 196616 | tf_op jit(solution)/shard_map/ppermute | solution.py:23
  4.6 0.1 collective-permute-done.1.refs_4_.q_ref.refs_2_
  4.7 0.0 copy-done.1
  4.7 0.0 copy-done.3
  4.7 0.0 copy-done.4
  4.7 0.0 copy-done.5
  4.7 2.4 %plan.1 = (bf16[256,512]{1,0:T(8,128)(2,1)S(1)}, bf16[256,512]{1,0:T(8,128)(2,1)S(1)}, f32[8,256]{1,0:T(8,128)S(1)}, bf16[512,512]{1,0:T(8,128)(2,1)S(1)}, bf16[...) custom-call(s32[2,8]{1,0:T(2,128)S(1)} %bitcast.15, ...), custom_call_target="tpu_custom_call" | custom-call | flops 1000000000 | bytes 3000000 | tf_op jit(solution)/shard_map/plan/pallas_call | solution.py:28
  7.1 0.0 copy-start.2
  7.1 0.0 copy-done
  7.2 0.7 %near.1.dep_ref.rest_1_.refs_2_.refs_9_ = f32[2,512,256]{2,1,0:T(8,128)S(1)} custom-call(bf16[2,512,512]{2,1,0:T(8,128)(2,1)S(1)} %copy-done, bf16[2,128,512]{2,1,0:T(8,128)(2,1)S(1)} %bitcast.9, bf16[2,128,512]{2,1,0:T(8,128)(2,1)S(1)} %collective-permute-done.1.refs_4_.q_ref.refs_2_, bf16[256,1024]{1,0:T(8,128)(2,1)S(1)} %get-tuple-element.35.dep_ref.refs_0_), custom_call_target="tpu_custom_call" | custom-call | flops 700000000 | bytes 2100000 | tf_op jit(solution)/shard_map/near/pallas_call | solution.py:28
  7.9 0.0 collective-permute-done.b_ref.near_ref
  7.9 0.1 copy-done.2
  8.0 1.5 %collective-permute-done.3.in_ref = bf16[2,128,512]{2,1,0:T(8,128)(2,1)S(1)} collective-permute-done((bf16[2,128,512]{2,1,0:T(8,128)(2,1)}, bf16[2,128,512]{2,1,0:T(8,128)(2,1)S(1)}, u32[]{:S(2)}, u32[]{:S(2)}) %collective-permute-start.3) | collective-permute-done | bytes 262176 | tf_op jit(solution)/shard_map/ppermute | solution.py:23
  9.5 0.1 collective-permute-start.4
  9.6 1.9 %collective-permute-start.2 = (bf16[2,128,256]{2,1,0:T(8,128)(2,1)S(1)}, bf16[2,128,256]{2,1,0:T(8,128)(2,1)S(1)}, u32[]{:S(2)}, u32[]{:S(2)}) collective-permute-start(bf16[2,128,256]{2,1,0:T(8,128)(2,1)S(1)} %pair.1.rest_0_), channel_id=1, source_target_pairs={{0,8},{4,12},{8,0},{12,4},{16,24},{20,28},{24,16},{28,20},{1,9},{5... | collective-permute-start | bytes 393224 | tf_op jit(solution)/shard_map/ppermute | solution.py:23
  11.4 0.0 collective-permute-done.4.refs_2_.refs_4_.q_ref
  11.5 0.9 %first.1 = (bf16[256,1024]{1,0:T(8,128)(2,1)S(1)}, s16[848,128]{1,0:T(8,128)(2,1)S(1)}, s16[464,128]{1,0:T(8,128)(2,1)S(1)}) custom-call(bf16[256,1024]{1,0:T(8,128)(2,1)S(1)} %get-tuple-element.35.dep_ref.refs_0_, bf16[2,128,512]{2,1,0:T(8,128)(2,1)S(1)} %relay.1.refs_1_.refs_3_.p_ref, ...), custom_call_target="tpu_custom_call" | custom-call | flops 800000000 | bytes 2400000 | tf_op jit(solution)/shard_map/first/pallas_call | solution.py:28
  12.4 1.6 %collective-permute-start.9 = (s16[848,128]{1,0:T(8,128)(2,1)S(1)}, s16[848,128]{1,0:T(8,128)(2,1)S(1)}, u32[]{:S(2)}, u32[]{:S(2)}) collective-permute-start(s16[848,128]{1,0:T(8,128)(2,1)S(1)} %get-tuple-element.59), channel_id=1, source_target_pairs={{0,4},{4,0},{8,12},{12,8},{16,20},{20,16},{24,28},{28,24},{1,5},{5... | collective-permute-start | bytes 651272 | tf_op jit(solution)/shard_map/ppermute | solution.py:23
  14.0 0.8 %ahead.1 = (bf16[256,1024]{1,0:T(8,128)(2,1)S(1)}, s16[928,128]{1,0:T(8,128)(2,1)S(1)}) custom-call(bf16[2,512,512]{2,1,0:T(8,128)(2,1)S(1)} %copy-done, bf16[2,128,512]{2,1,0:T(8,128)(2,1)S(1)} %bitcast.10, bf16[2,128,512]{2,1,0:T(8,128)(2,1)S(1)} %collective-permute-done.1.refs_4_.q_ref.refs_2_, bf16[2,128,512]{2,1,0:T(8,128)(2,1)S(1)} %relay.1.refs_1_.refs_3_.p_ref, ...), custom_call_target="tpu_custom_call" | custom-call | flops 1400000000 | bytes 4200000 | tf_op jit(solution)/shard_map/ahead/pallas_call | solution.py:28
  14.8 1.5 %collective-permute-start.6 = (s16[928,128]{1,0:T(8,128)(2,1)S(1)}, s16[928,128]{1,0:T(8,128)(2,1)S(1)}, u32[]{:S(2)}, u32[]{:S(2)}) collective-permute-start(s16[928,128]{1,0:T(8,128)(2,1)S(1)} %get-tuple-element.44.refs_3_.own_ref), channel_id=1, source_target_pairs={{0,8},{4,12},{8,0},{12,4},{16,24},{20,28},{24,16},{28,20},{1,9},{5... | collective-permute-start | bytes 712712 | tf_op jit(solution)/shard_map/ppermute | solution.py:23
  16.4 0.7 %ready.1.dep_ref = s16[784,128]{1,0:T(8,128)(2,1)S(1)} custom-call(bf16[2,512,512]{2,1,0:T(8,128)(2,1)S(1)} %copy-done, bf16[256,1024]{1,0:T(8,128)(2,1)S(1)} %get-tuple-element.43.refs_1_, f32[8,256]{1,0:T(8,128)S(1)} %get-tuple-element.40.refs_5_.refs_7_.refs_2_, s16[928,128]{1,0:T(8,128)(2,1)S(1)} %get-tuple-element.44.refs_3_.own_ref), custom_call_target="tpu_custom_call" | custom-call | flops 600000000 | bytes 1800000 | tf_op jit(solution)/shard_map/ready/pallas_call | solution.py:28
  17.0 0.5 %collective-permute-start.5 = (s16[784,128]{1,0:T(8,128)(2,1)S(1)}, s16[784,128]{1,0:T(8,128)(2,1)S(1)}, u32[]{:S(2)}, u32[]{:S(2)}) collective-permute-start(s16[784,128]{1,0:T(8,128)(2,1)S(1)} %ready.1.dep_ref), channel_id=1, source_target_pairs={{0,4},{4,0},{8,12},{12,8},{16,20},{20,16},{24,28},{28,24},{1,5},{5... | collective-permute-start | bytes 602120 | tf_op jit(solution)/shard_map/ppermute | solution.py:23
  17.6 0.7 %rows.1.dep_ref.refs_3_.refs_8_ = f32[512,512]{1,0:T(8,128)S(1)} custom-call(bf16[2,512,512]{2,1,0:T(8,128)(2,1)S(1)} %copy-done, bf16[256,1024]{1,0:T(8,128)(2,1)S(1)} %get-tuple-element.42.picked_ref, s16[784,128]{1,0:T(8,128)(2,1)S(1)} %ready.1.dep_ref), custom_call_target="tpu_custom_call" | custom-call | flops 1000000000 | bytes 3000000 | tf_op jit(solution)/shard_map/rows/pallas_call | solution.py:28
  18.3 0.0 collective-permute-done.2.far_ref
  18.3 0.8 %core.1 = (bf16[512,512]{1,0:T(8,128)(2,1)S(1)}, bf16[512,512]{1,0:T(8,128)(2,1)S(1)}, bf16[512,512]{1,0:T(8,128)(2,1)S(1)}) custom-call(bf16[128,256]{1,0:T(8,128)(2,1)S(1)} %bitcast.13, bf16[128,256]{1,0:T(8,128)(2,1)S(1)} %collective-permute-done.b_ref.near_ref, bf16[2,128,256]{2,1,0:T(8,128)(2,1)S(1)} %collective-permute-done.2.far_ref, ...), custom_call_target="tpu_custom_call" | custom-call | flops 1000000000 | bytes 3000000 | tf_op jit(solution)/shard_map/core/pallas_call | solution.py:28
  19.1 0.7 %leaf.1.refs_3_.refs_10_.refs_6_ = f32[2,512,256]{2,1,0:T(8,128)S(1)} custom-call(bf16[2,512,512]{2,1,0:T(8,128)(2,1)S(1)} %copy-done, bf16[2,128,512]{2,1,0:T(8,128)(2,1)S(1)} %relay.1.refs_1_.refs_3_.p_ref, bf16[2,128,512]{2,1,0:T(8,128)(2,1)S(1)} %collective-permute-done.4.refs_2_.refs_4_.q_ref, ...), custom_call_target="tpu_custom_call" | custom-call | flops 700000000 | bytes 2100000 | tf_op jit(solution)/shard_map/leaf/pallas_call | solution.py:28
  19.8 0.6 %collective-permute-done.9.refs_0_ = s16[848,128]{1,0:T(8,128)(2,1)S(1)} collective-permute-done((s16[848,128]{1,0:T(8,128)(2,1)S(1)}, s16[848,128]{1,0:T(8,128)(2,1)S(1)}, u32[]{:S(2)}, u32[]{:S(2)}) %collective-permute-start.9) | collective-permute-done | bytes 217120 | tf_op jit(solution)/shard_map/ppermute | solution.py:23
  20.4 0.9 %second0.1 = (s16[848,128]{1,0:T(8,128)(2,1)S(1)}, bf16[2,208,512]{2,1,0:T(8,128)(2,1)S(1)}, bf16[2,208,512]{2,1,0:T(8,128)(2,1)S(1)}) custom-call(s16[848,128]{1,0:T(8,128)(2,1)S(1)} %collective-permute-done.9.refs_0_, bf16[512,512]{1,0:T(8,128)(2,1)S(1)} %get-tuple-element.47.refs_1_.refs_2_, bf16[512,512]{1,0:T(8,128)(2,1)S(1)} %get-tuple-element.48.refs_2_.refs_3_, ...), custom_call_target="tpu_custom_call" | custom-call | flops 800000000 | bytes 2400000 | tf_op jit(solution)/shard_map/second0/pallas_call | solution.py:28
  21.3 1.8 %collective-permute-start.10 = (s16[848,128]{1,0:T(8,128)(2,1)S(1)}, s16[848,128]{1,0:T(8,128)(2,1)S(1)}, u32[]{:S(2)}, u32[]{:S(2)}) collective-permute-start(s16[848,128]{1,0:T(8,128)(2,1)S(1)} %get-tuple-element.60), channel_id=1, source_target_pairs={{0,8},{4,12},{8,0},{12,4},{16,24},{20,28},{24,16},{28,20},{1,9},{5... | collective-permute-start | bytes 651272 | tf_op jit(solution)/shard_map/ppermute | solution.py:23
  23.1 0.0 collective-permute-done.6.got_ref.refs_1_
  23.1 1.6 %collective-permute-start.8 = (s16[928,128]{1,0:T(8,128)(2,1)S(1)}, s16[928,128]{1,0:T(8,128)(2,1)S(1)}, u32[]{:S(2)}, u32[]{:S(2)}) collective-permute-start(s16[928,128]{1,0:T(8,128)(2,1)S(1)} %onward.1.refs_6_), channel_id=1, source_target_pairs={{0,4},{4,0},{8,12},{12,8},{16,20},{20,16},{24,28},{28,24},{1,5},{5... | collective-permute-start | bytes 712712 | tf_op jit(solution)/shard_map/ppermute | solution.py:23
  24.7 0.0 collective-permute-done.5.refs_0_
  24.7 0.9 %second1.1 = (s16[784,128]{1,0:T(8,128)(2,1)S(1)}, bf16[2,192,512]{2,1,0:T(8,128)(2,1)S(1)}, bf16[2,192,512]{2,1,0:T(8,128)(2,1)S(1)}) custom-call(s16[784,128]{1,0:T(8,128)(2,1)S(1)} %collective-permute-done.5.refs_0_, bf16[512,512]{1,0:T(8,128)(2,1)S(1)} %get-tuple-element.47.refs_1_.refs_2_, bf16[512,512]{1,0:T(8,128)(2,1)S(1)} %get-tuple-element.48.refs_2_.refs_3_, ...), custom_call_target="tpu_custom_call" | custom-call | flops 800000000 | bytes 2400000 | tf_op jit(solution)/shard_map/second1/pallas_call | solution.py:28
  25.6 1.0 %collective-permute-start.7 = (s16[784,128]{1,0:T(8,128)(2,1)S(1)}, s16[784,128]{1,0:T(8,128)(2,1)S(1)}, u32[]{:S(2)}, u32[]{:S(2)}) collective-permute-start(s16[784,128]{1,0:T(8,128)(2,1)S(1)} %get-tuple-element.50), channel_id=1, source_target_pairs={{0,8},{4,12},{8,0},{12,4},{16,24},{20,28},{24,16},{28,20},{1,9},{5... | collective-permute-start | bytes 602120 | tf_op jit(solution)/shard_map/ppermute | solution.py:23
  26.5 0.6 %third1.1 = (f32[2,192,512]{2,1,0:T(8,128)S(1)}, f32[192,512]{1,0:T(8,128)S(1)}) custom-call(bf16[2,192,512]{2,1,0:T(8,128)(2,1)S(1)} %get-tuple-element.51.refs_0_.refs_6_, bf16[2,192,512]{2,1,0:T(8,128)(2,1)S(1)} %get-tuple-element.52.refs_1_, f32[2,512,256]{2,1,0:T(8,128)S(1)} %near.1.dep_ref.rest_1_.refs_2_.refs_9_, ...), custom_call_target="tpu_custom_call" | custom-call | flops 500000000 | bytes 1500000 | tf_op jit(solution)/shard_map/third1/pallas_call | solution.py:28
  27.1 0.6 %third0.1 = (f32[2,208,512]{2,1,0:T(8,128)S(1)}, f32[208,512]{1,0:T(8,128)S(1)}) custom-call(bf16[2,208,512]{2,1,0:T(8,128)(2,1)S(1)} %get-tuple-element.61.refs_0_, bf16[2,208,512]{2,1,0:T(8,128)(2,1)S(1)} %get-tuple-element.62.refs_1_, f32[2,512,256]{2,1,0:T(8,128)S(1)} %near.1.dep_ref.rest_1_.refs_2_.refs_9_, ...), custom_call_target="tpu_custom_call" | custom-call | flops 500000000 | bytes 1500000 | tf_op jit(solution)/shard_map/third0/pallas_call | solution.py:28
  27.7 0.1 collective-permute-done.10.refs_3_
  27.8 1.7 %last0.1.refs_7_ = f32[2,512,512]{2,1,0:T(8,128)} custom-call(bf16[512,512]{1,0:T(8,128)(2,1)S(1)} %get-tuple-element.45.refs_14_.refs_0_, bf16[512,512]{1,0:T(8,128)(2,1)S(1)} %get-tuple-element.46.refs_15_.refs_1_, bf16[256,512]{1,0:T(8,128)(2,1)S(1)} %get-tuple-element.38.refs_5_.refs_12_.refs_2_, s16[848,128]{1,0:T(8,128)(2,1)S(1)} %collective-permute-done.10.refs_3_, ...), custom_call_target="tpu_custom_call" | custom-call | flops 1000000000 | bytes 3000000 | tf_op jit(solution)/shard_map/last0/pallas_call | solution.py:28
  29.5 0.0 collective-permute-done.8.refs_0_
  29.5 1.9 %around.1.refs_6_ = f32[2,112,512]{2,1,0:T(8,128)S(1)} custom-call(s16[928,128]{1,0:T(8,128)(2,1)S(1)} %collective-permute-done.8.refs_0_, s16[928,128]{1,0:T(8,128)(2,1)S(1)} %collective-permute-done.6.got_ref.refs_1_, bf16[512,512]{1,0:T(8,128)(2,1)S(1)} %get-tuple-element.47.refs_1_.refs_2_, bf16[512,512]{1,0:T(8,128)(2,1)S(1)} %get-tuple-element.48.refs_2_.refs_3_, ...), custom_call_target="tpu_custom_call" | custom-call | flops 2500000000 | bytes 7500000 | tf_op jit(solution)/shard_map/around/pallas_call | solution.py:28
  31.4 0.3 collective-permute-done.7.refs_3_
  31.7 1.8 %last1.1 = f32[2,512,512]{2,1,0:T(8,128)} custom-call(bf16[512,512]{1,0:T(8,128)(2,1)S(1)} %get-tuple-element.45.refs_14_.refs_0_, bf16[512,512]{1,0:T(8,128)(2,1)S(1)} %get-tuple-element.46.refs_15_.refs_1_, bf16[256,512]{1,0:T(8,128)(2,1)S(1)} %get-tuple-element.38.refs_5_.refs_12_.refs_2_, ...), custom_call_target="tpu_custom_call", output_to_operand_aliasing={{}: (7, {})} | custom-call | flops 1000000000 | bytes 3000000 | tf_op jit(solution)/shard_map/last1/pallas_call | solution.py:28
  (5 shorter events, 0.0 us)
Async XLA Ops:
  0.0 9.5 %collective-permute-start.3 = (bf16[2,128,512]{2,1,0:T(8,128)(2,1)}, bf16[2,128,512]{2,1,0:T(8,128)(2,1)S(1)}, u32[]{:S(2)}, u32[]{:S(2)}) collective-permute-start(bf16[2,128,512]{2,1,0:T(8,128)(2,1)} %bitcast.6), channel_id=1, source_target_pairs={{0,2},{1,3},{2,0},{3,1},{4,6},{5,7},{6,4},{7,5},{8,10},{9,11},{10,... | collective-permute-start | bytes 786440 | tf_op jit(solution)/shard_map/ppermute | solution.py:23
  2.9 1.7 %collective-permute-start.1 = (bf16[2,128,512]{2,1,0:T(8,128)(2,1)}, bf16[2,128,512]{2,1,0:T(8,128)(2,1)S(1)}, u32[]{:S(2)}, u32[]{:S(2)}) collective-permute-start(bf16[2,128,512]{2,1,0:T(8,128)(2,1)} %bitcast.7), channel_id=1, source_target_pairs={{0,1},{1,0},{2,3},{3,2},{4,5},{5,4},{6,7},{7,6},{8,9},{9,8},{10,11... | collective-permute-start | bytes 786440 | tf_op jit(solution)/shard_map/ppermute | solution.py:23
  2.9 1.7 %copy-start.1 = (bf16[1,2,128,512]{3,2,1,0:T(8,128)(2,1)S(1)}, bf16[1,2,128,512]{3,2,1,0:T(8,128)(2,1)}, u32[]{:S(2)}) copy-start(bf16[1,2,128,512]{3,2,1,0:T(8,128)(2,1)} %param.7) | copy-start | bytes 786436
  2.9 1.7 %copy-start.3 = (s32[8,2,256]{2,1,0:T(2,128)S(1)}, s32[8,2,256]{2,1,0:T(2,128)}, u32[]{:S(2)}) copy-start(s32[8,2,256]{2,1,0:T(2,128)} %refs_1_.1) | copy-start | bytes 49156
  2.9 1.7 %copy-start.4 = (f32[512]{0:T(512)S(1)}, f32[512]{0:T(512)}, u32[]{:S(2)}) copy-start(f32[512]{0:T(512)} %param.8) | copy-start | bytes 6148
  3.0 1.7 %copy-start.5 = (s32[8,2]{0,1:T(2,128)S(1)}, s32[8,2]{0,1:T(2,128)}, u32[]{:S(2)}) copy-start(s32[8,2]{0,1:T(2,128)} %param.10) | copy-start | bytes 196
  3.0 4.9 %collective-permute-start = (bf16[128,256]{1,0:T(8,128)(2,1)}, bf16[128,256]{1,0:T(8,128)(2,1)S(1)}, u32[]{:S(2)}, u32[]{:S(2)}) collective-permute-start(bf16[128,256]{1,0:T(8,128)(2,1)} %bitcast.11), channel_id=1, source_target_pairs={{0,4},{4,0},{8,12},{12,8},{16,20},{20,16},{24,28},{28,24},{1,5},{5... | collective-permute-start | bytes 196616 | tf_op jit(solution)/shard_map/ppermute | solution.py:23
  4.5 2.6 %copy-start = (bf16[2,512,512]{2,1,0:T(8,128)(2,1)S(1)}, bf16[2,512,512]{2,1,0:T(8,128)(2,1)}, u32[]{:S(2)}) copy-start(bf16[2,512,512]{2,1,0:T(8,128)(2,1)} %x_ref.5) | copy-start | bytes 3145732
  7.1 0.8 %copy-start.2 = (bf16[2,256,64]{1,2,0:T(8,128)(2,1)S(1)}, bf16[2,256,64]{1,2,0:T(8,128)(2,1)}, u32[]{:S(2)}) copy-start(bf16[2,256,64]{1,2,0:T(8,128)(2,1)} %param.11) | copy-start | bytes 196612
  9.5 2.0 %collective-permute-start.4 = (bf16[2,128,512]{2,1,0:T(8,128)(2,1)S(1)}, bf16[2,128,512]{2,1,0:T(8,128)(2,1)S(1)}, u32[]{:S(2)}, u32[]{:S(2)}) collective-permute-start(bf16[2,128,512]{2,1,0:T(8,128)(2,1)S(1)} %relay.1.refs_1_.refs_3_.p_ref), channel_id=1, source_target_pairs={{0,1},{1,0},{2,3},{3,2},{4,5},{5,4},{6,7},{7,6},{8,9},{9,8},{10,11... | collective-permute-start | bytes 786440 | tf_op jit(solution)/shard_map/ppermute | solution.py:23
  9.6 8.8 %collective-permute-start.2 = (bf16[2,128,256]{2,1,0:T(8,128)(2,1)S(1)}, bf16[2,128,256]{2,1,0:T(8,128)(2,1)S(1)}, u32[]{:S(2)}, u32[]{:S(2)}) collective-permute-start(bf16[2,128,256]{2,1,0:T(8,128)(2,1)S(1)} %pair.1.rest_0_), channel_id=1, source_target_pairs={{0,8},{4,12},{8,0},{12,4},{16,24},{20,28},{24,16},{28,20},{1,9},{5... | collective-permute-start | bytes 393224 | tf_op jit(solution)/shard_map/ppermute | solution.py:23
  12.4 8.0 %collective-permute-start.9 = (s16[848,128]{1,0:T(8,128)(2,1)S(1)}, s16[848,128]{1,0:T(8,128)(2,1)S(1)}, u32[]{:S(2)}, u32[]{:S(2)}) collective-permute-start(s16[848,128]{1,0:T(8,128)(2,1)S(1)} %get-tuple-element.59), channel_id=1, source_target_pairs={{0,4},{4,0},{8,12},{12,8},{16,20},{20,16},{24,28},{28,24},{1,5},{5... | collective-permute-start | bytes 651272 | tf_op jit(solution)/shard_map/ppermute | solution.py:23
  14.8 8.3 %collective-permute-start.6 = (s16[928,128]{1,0:T(8,128)(2,1)S(1)}, s16[928,128]{1,0:T(8,128)(2,1)S(1)}, u32[]{:S(2)}, u32[]{:S(2)}) collective-permute-start(s16[928,128]{1,0:T(8,128)(2,1)S(1)} %get-tuple-element.44.refs_3_.own_ref), channel_id=1, source_target_pairs={{0,8},{4,12},{8,0},{12,4},{16,24},{20,28},{24,16},{28,20},{1,9},{5... | collective-permute-start | bytes 712712 | tf_op jit(solution)/shard_map/ppermute | solution.py:23
  17.0 7.7 %collective-permute-start.5 = (s16[784,128]{1,0:T(8,128)(2,1)S(1)}, s16[784,128]{1,0:T(8,128)(2,1)S(1)}, u32[]{:S(2)}, u32[]{:S(2)}) collective-permute-start(s16[784,128]{1,0:T(8,128)(2,1)S(1)} %ready.1.dep_ref), channel_id=1, source_target_pairs={{0,4},{4,0},{8,12},{12,8},{16,20},{20,16},{24,28},{28,24},{1,5},{5... | collective-permute-start | bytes 602120 | tf_op jit(solution)/shard_map/ppermute | solution.py:23
  21.3 6.5 %collective-permute-start.10 = (s16[848,128]{1,0:T(8,128)(2,1)S(1)}, s16[848,128]{1,0:T(8,128)(2,1)S(1)}, u32[]{:S(2)}, u32[]{:S(2)}) collective-permute-start(s16[848,128]{1,0:T(8,128)(2,1)S(1)} %get-tuple-element.60), channel_id=1, source_target_pairs={{0,8},{4,12},{8,0},{12,4},{16,24},{20,28},{24,16},{28,20},{1,9},{5... | collective-permute-start | bytes 651272 | tf_op jit(solution)/shard_map/ppermute | solution.py:23
  23.1 6.4 %collective-permute-start.8 = (s16[928,128]{1,0:T(8,128)(2,1)S(1)}, s16[928,128]{1,0:T(8,128)(2,1)S(1)}, u32[]{:S(2)}, u32[]{:S(2)}) collective-permute-start(s16[928,128]{1,0:T(8,128)(2,1)S(1)} %onward.1.refs_6_), channel_id=1, source_target_pairs={{0,4},{4,0},{8,12},{12,8},{16,20},{20,16},{24,28},{28,24},{1,5},{5... | collective-permute-start | bytes 712712 | tf_op jit(solution)/shard_map/ppermute | solution.py:23
  25.6 6.2 %collective-permute-start.7 = (s16[784,128]{1,0:T(8,128)(2,1)S(1)}, s16[784,128]{1,0:T(8,128)(2,1)S(1)}, u32[]{:S(2)}, u32[]{:S(2)}) collective-permute-start(s16[784,128]{1,0:T(8,128)(2,1)S(1)} %get-tuple-element.50), channel_id=1, source_target_pairs={{0,8},{4,12},{8,0},{12,4},{16,24},{20,28},{24,16},{28,20},{1,9},{5... | collective-permute-start | bytes 602120 | tf_op jit(solution)/shard_map/ppermute | solution.py:23

commit v6 on v5

--- a/solution.py
+++ b/solution.py
@@ -9,7 +9,7 @@
 WAVENUM = 0.7
 BF = jnp.bfloat16
 F32 = jnp.float32
-SHARES = (13, 12, 7)
+SHARES = (12, 13, 7)
 TOP = 32766.0
 STEPS = 128.0
 LANES = 128
@@ -138,7 +138,7 @@
 
 
 def plan_body(ranks_ref, skel_ref, contrast_ref, own_ref, beside_ref, dep_ref, *refs, parts):
-    e0_ref, e1_ref, q_ref, ghi_ref, glo_ref, g1_ref, j_ref, d_ref, part_ref, hhi_ref, hlo_ref, jp_ref = refs
+    e0_ref, e1_ref, q_ref, ghi_ref, glo_ref, g1_ref, j_ref, d_ref, part_ref, part1_ref, hhi_ref, hlo_ref, jp_ref = refs
     box = lax.axis_index("box")
     me = lax.axis_index("field")
     kmax = skel_ref.shape[2]
@@ -179,7 +179,9 @@
             g1_ref[:, kmax:] = s
     j_ref[...] = matches(cols[0], ranks[0:1, :], row_of(box, 1), ranks[1:2, :])
     d_ref[...] = matches(cols[1], ranks[1:2, :], row_of(box, 1), ranks[1:2, :])
-    part_ref[...] = nn(e0_ref[:, : 2 * n], stacked(own_ref, beside_ref)).astype(BF)
+    near_rows = stacked(own_ref, beside_ref)
+    part_ref[...] = nn(e0_ref[:, : 2 * n], near_rows).astype(BF)
+    part1_ref[...] = nn(e1_ref[:, : 2 * n], near_rows).astype(BF)
     mate = box ^ 2
     mate_ranks = ranks_of(mate)
     c, s = green(row_of(mate, 0), mate, col_of(box ^ 3, 0), box ^ 3)
@@ -272,10 +274,11 @@
     v_ref[:, kmax:] = nt(right, picked)
 
 
-def ahead_body(x_ref, p0_ref, p1_ref, p2_ref, p3_ref, e1_ref, side_ref, q_ref, dep_ref, picked_ref, out_ref, *, start, n):
+def ahead_body(x_ref, part_ref, across_ref, beyond_ref, e1_ref, side_ref, q_ref, dep_ref, picked_ref, out_ref, *, start, n):
     half = out_ref.shape[0] // 2
     out_ref[0:half] = side_ref[...]
-    picked = nn(e1_ref[...], stacked(p0_ref, p1_ref, p2_ref, p3_ref)).astype(BF)
+    rows = across_ref.shape[1]
+    picked = (nn(e1_ref[:, 2 * rows :], stacked(across_ref, beyond_ref)) + part_ref[...].astype(F32)).astype(BF)
     picked_ref[...] = picked
     left, right = turned_fields(x_ref, start, n)
     q = q_ref[1:2, :]
@@ -467,7 +470,7 @@
     core_near = swap(core_own, "box", 1)
     n = n_rows = own.shape[1]
     (opened,) = call(open_body, "open", [shape(8, 128)], [], cost=4.0)
-    e0, e1, q, ghi, glo, g1, dup01, dup11, part, hhi, hlo, dupm = call(
+    e0, e1, q, ghi, glo, g1, dup01, dup11, part, part1, hhi, hlo, dupm = call(
         lambda *refs: plan_body(*refs, parts=lax.axis_size("field")),
         "plan",
         [
@@ -479,6 +482,7 @@
             shape(kmax, 2 * kmax),
             shape(kmax, kmax, dtype=BF),
             shape(kmax, kmax, dtype=BF),
+            shape(kmax, 2 * width, dtype=BF),
             shape(kmax, 2 * width, dtype=BF),
             shape(2 * kmax, 2 * kmax, dtype=BF),
             shape(2 * kmax, 2 * kmax, dtype=BF),
@@ -520,8 +524,8 @@
         lambda *refs: ahead_body(*refs, start=side_start, n=side_n),
         "ahead",
         [shape(kmax, 2 * width, dtype=BF), shape(2 * packed_shape(side_n, kmax).shape[0], LANES, dtype=jnp.int16)],
-        [x, own, beside, across, beyond, e1, side, q, e0],
-        [VMEM] * 8 + [ANY],
+        [x, part1, across, beyond, e1, side, q, e0],
+        [VMEM] * 7 + [ANY],
         cost=1.4,
     )
     mate = swap(ahead, "box", 2)

time: 33.6 us -> 33.5 us (level)
  waiting for transfers between devices: 2.58 us -> 1.77 us
  starting transfers between devices: 14.5 us -> 15.1 us
    ppermute x11, waiting for transfers between devices: 2.58 us -> 1.77 us  [swap(): lax.ppermute(value, axis, [(s, s ^ mask) for s in range(lax.axis_size(axi...]
    ppermute x11, starting transfers between devices: 14.5 us -> 15.1 us  [swap(): lax.ppermute(value, axis, [(s, s ^ mask) for s in range(lax.axis_size(axi...]
  transfers between devices with their start and end apart: 11 -> 11, of which waited for: 5 -> 3; matrix products, arithmetic and copies ran while one was open for 0% -> 0% of each run, Pallas kernels for 43% -> 43%
where the time goes in v6:
time: 33.5 us; the launch traced here: 33.4 us
  Pallas kernels  16.2 us (48%)
  starting transfers between devices  15.1 us (45%)
  waiting for transfers between devices  1.77 us (5%)
    pallas_call x19, Pallas kernels, call(): pl.pallas_call(body, name=name, out_shape=outs, in_specs=specs or [VMEM]...  16.2 us
    ppermute x11, starting transfers between devices, swap(): lax.ppermute(value, axis, [(s, s ^ mask) for s in range(lax.axis_size(axi...  15.1 us
    ppermute x11, waiting for transfers between devices, swap(): lax.ppermute(value, axis, [(s, s ^ mask) for s in range(lax.axis_size(axi...  1.77 us
  transfers between devices with their start and end apart: 11, of which 3 were waited for; matrix products, arithmetic and copies ran while one was open for 0% of the time, Pallas kernels for 43%

profile of v6, /device:TPU:0, one launch (start us, length us, event | category | flops | bytes accessed | tf_op | source)
XLA Modules:
  0.0 33.4 jit_solution(15445778956740564890)
XLA Ops:
  0.0 2.9 %collective-permute-start.3 = (bf16[2,128,512]{2,1,0:T(8,128)(2,1)}, bf16[2,128,512]{2,1,0:T(8,128)(2,1)S(1)}, u32[]{:S(2)}, u32[]{:S(2)}) collective-permute-start(bf16[2,128,512]{2,1,0:T(8,128)(2,1)} %bitcast.6), channel_id=1, source_target_pairs={{0,2},{1,3},{2,0},{3,1},{4,6},{5,7},{6,4},{7,5},{8,10},{9,11},{10,... | collective-permute-start | bytes 786440 | tf_op jit(solution)/shard_map/ppermute | solution.py:23
  2.9 0.0 collective-permute-start.1
  2.9 0.0 copy-start.1
  2.9 0.0 copy-start.3
  2.9 0.0 copy-start.4
  3.0 0.0 copy-start.5
  3.0 1.6 %collective-permute-start = (bf16[128,256]{1,0:T(8,128)(2,1)}, bf16[128,256]{1,0:T(8,128)(2,1)S(1)}, u32[]{:S(2)}, u32[]{:S(2)}) collective-permute-start(bf16[128,256]{1,0:T(8,128)(2,1)} %bitcast.10), channel_id=1, source_target_pairs={{0,4},{4,0},{8,12},{12,8},{16,20},{20,16},{24,28},{28,24},{1,5},{5... | collective-permute-start | bytes 196616 | tf_op jit(solution)/shard_map/ppermute | solution.py:23
  4.6 0.1 collective-permute-done.1.refs_4_.q_ref
  4.7 0.0 copy-done.1
  4.7 0.0 copy-done.3
  4.7 0.0 copy-done.4
  4.7 0.0 copy-done.5
  4.7 2.5 %plan.1 = (bf16[256,512]{1,0:T(8,128)(2,1)S(1)}, bf16[256,512]{1,0:T(8,128)(2,1)S(1)}, f32[8,256]{1,0:T(8,128)S(1)}, bf16[512,512]{1,0:T(8,128)(2,1)S(1)}, bf16[...) custom-call(s32[2,8]{1,0:T(2,128)S(1)} %bitcast.14, ...), custom_call_target="tpu_custom_call" | custom-call | flops 1000000000 | bytes 3000000 | tf_op jit(solution)/shard_map/plan/pallas_call | solution.py:28
  7.2 0.0 copy-start.2
  7.2 0.0 copy-done
  7.3 0.7 %near.1.dep_ref.rest_1_.refs_2_.refs_9_ = f32[2,512,256]{2,1,0:T(8,128)S(1)} custom-call(bf16[2,512,512]{2,1,0:T(8,128)(2,1)S(1)} %copy-done, bf16[2,128,512]{2,1,0:T(8,128)(2,1)S(1)} %bitcast.9, bf16[2,128,512]{2,1,0:T(8,128)(2,1)S(1)} %collective-permute-done.1.refs_4_.q_ref, bf16[256,1024]{1,0:T(8,128)(2,1)S(1)} %get-tuple-element.36.dep_ref.refs_0_), custom_call_target="tpu_custom_call" | custom-call | flops 700000000 | bytes 2100000 | tf_op jit(solution)/shard_map/near/pallas_call | solution.py:28
  8.0 0.0 collective-permute-done.b_ref.near_ref
  8.0 0.1 copy-done.2
  8.1 1.4 %collective-permute-done.3.in_ref = bf16[2,128,512]{2,1,0:T(8,128)(2,1)S(1)} collective-permute-done((bf16[2,128,512]{2,1,0:T(8,128)(2,1)}, bf16[2,128,512]{2,1,0:T(8,128)(2,1)S(1)}, u32[]{:S(2)}, u32[]{:S(2)}) %collective-permute-start.3) | collective-permute-done | bytes 262176 | tf_op jit(solution)/shard_map/ppermute | solution.py:23
  9.5 0.1 collective-permute-start.4
  9.6 1.9 %collective-permute-start.2 = (bf16[2,128,256]{2,1,0:T(8,128)(2,1)S(1)}, bf16[2,128,256]{2,1,0:T(8,128)(2,1)S(1)}, u32[]{:S(2)}, u32[]{:S(2)}) collective-permute-start(bf16[2,128,256]{2,1,0:T(8,128)(2,1)S(1)} %pair.1.rest_0_), channel_id=1, source_target_pairs={{0,8},{4,12},{8,0},{12,4},{16,24},{20,28},{24,16},{28,20},{1,9},{5... | collective-permute-start | bytes 393224 | tf_op jit(solution)/shard_map/ppermute | solution.py:23
  11.4 0.0 collective-permute-done.4.refs_2_.refs_3_.q_ref
  11.5 0.9 %first.1 = (bf16[256,1024]{1,0:T(8,128)(2,1)S(1)}, s16[784,128]{1,0:T(8,128)(2,1)S(1)}, s16[464,128]{1,0:T(8,128)(2,1)S(1)}) custom-call(bf16[256,1024]{1,0:T(8,128)(2,1)S(1)} %get-tuple-element.36.dep_ref.refs_0_, bf16[2,128,512]{2,1,0:T(8,128)(2,1)S(1)} %relay.1.refs_1_.refs_2_.p_ref, ...), custom_call_target="tpu_custom_call" | custom-call | flops 800000000 | bytes 2400000 | tf_op jit(solution)/shard_map/first/pallas_call | solution.py:28
  12.4 1.6 %collective-permute-start.9 = (s16[784,128]{1,0:T(8,128)(2,1)S(1)}, s16[784,128]{1,0:T(8,128)(2,1)S(1)}, u32[]{:S(2)}, u32[]{:S(2)}) collective-permute-start(s16[784,128]{1,0:T(8,128)(2,1)S(1)} %get-tuple-element.61), channel_id=1, source_target_pairs={{0,4},{4,0},{8,12},{12,8},{16,20},{20,16},{24,28},{28,24},{1,5},{5... | collective-permute-start | bytes 602120 | tf_op jit(solution)/shard_map/ppermute | solution.py:23
  14.0 0.8 %ahead.1 = (bf16[256,1024]{1,0:T(8,128)(2,1)S(1)}, s16[928,128]{1,0:T(8,128)(2,1)S(1)}) custom-call(bf16[2,512,512]{2,1,0:T(8,128)(2,1)S(1)} %copy-done, bf16[256,1024]{1,0:T(8,128)(2,1)S(1)} %get-tuple-element.39.refs_1_, bf16[2,128,512]{2,1,0:T(8,128)(2,1)S(1)} %relay.1.refs_1_.refs_2_.p_ref, ...), custom_call_target="tpu_custom_call" | custom-call | flops 1400000000 | bytes 4200000 | tf_op jit(solution)/shard_map/ahead/pallas_call | solution.py:28
  14.7 1.5 %collective-permute-start.6 = (s16[928,128]{1,0:T(8,128)(2,1)S(1)}, s16[928,128]{1,0:T(8,128)(2,1)S(1)}, u32[]{:S(2)}, u32[]{:S(2)}) collective-permute-start(s16[928,128]{1,0:T(8,128)(2,1)S(1)} %get-tuple-element.46.refs_3_.own_ref), channel_id=1, source_target_pairs={{0,8},{4,12},{8,0},{12,4},{16,24},{20,28},{24,16},{28,20},{1,9},{5... | collective-permute-start | bytes 712712 | tf_op jit(solution)/shard_map/ppermute | solution.py:23
  16.3 0.7 %ready.1.dep_ref = s16[848,128]{1,0:T(8,128)(2,1)S(1)} custom-call(bf16[2,512,512]{2,1,0:T(8,128)(2,1)S(1)} %copy-done, bf16[256,1024]{1,0:T(8,128)(2,1)S(1)} %get-tuple-element.45.refs_1_, f32[8,256]{1,0:T(8,128)S(1)} %get-tuple-element.42.refs_5_.refs_6_.refs_2_, s16[928,128]{1,0:T(8,128)(2,1)S(1)} %get-tuple-element.46.refs_3_.own_ref), custom_call_target="tpu_custom_call" | custom-call | flops 600000000 | bytes 1800000 | tf_op jit(solution)/shard_map/ready/pallas_call | solution.py:28
  16.9 0.6 %collective-permute-start.5 = (s16[848,128]{1,0:T(8,128)(2,1)S(1)}, s16[848,128]{1,0:T(8,128)(2,1)S(1)}, u32[]{:S(2)}, u32[]{:S(2)}) collective-permute-start(s16[848,128]{1,0:T(8,128)(2,1)S(1)} %ready.1.dep_ref), channel_id=1, source_target_pairs={{0,4},{4,0},{8,12},{12,8},{16,20},{20,16},{24,28},{28,24},{1,5},{5... | collective-permute-start | bytes 651272 | tf_op jit(solution)/shard_map/ppermute | solution.py:23
  17.5 0.7 %rows.1.dep_ref.refs_3_.refs_8_ = f32[512,512]{1,0:T(8,128)S(1)} custom-call(bf16[2,512,512]{2,1,0:T(8,128)(2,1)S(1)} %copy-done, bf16[256,1024]{1,0:T(8,128)(2,1)S(1)} %get-tuple-element.44.picked_ref, s16[848,128]{1,0:T(8,128)(2,1)S(1)} %ready.1.dep_ref), custom_call_target="tpu_custom_call" | custom-call | flops 1000000000 | bytes 3000000 | tf_op jit(solution)/shard_map/rows/pallas_call | solution.py:28
  18.2 0.0 collective-permute-done.2.far_ref
  18.3 0.8 %core.1 = (bf16[512,512]{1,0:T(8,128)(2,1)S(1)}, bf16[512,512]{1,0:T(8,128)(2,1)S(1)}, bf16[512,512]{1,0:T(8,128)(2,1)S(1)}) custom-call(bf16[128,256]{1,0:T(8,128)(2,1)S(1)} %bitcast.12, bf16[128,256]{1,0:T(8,128)(2,1)S(1)} %collective-permute-done.b_ref.near_ref, bf16[2,128,256]{2,1,0:T(8,128)(2,1)S(1)} %collective-permute-done.2.far_ref, ...), custom_call_target="tpu_custom_call" | custom-call | flops 1000000000 | bytes 3000000 | tf_op jit(solution)/shard_map/core/pallas_call | solution.py:28
  19.0 0.7 %leaf.1.refs_3_.refs_10_.refs_6_ = f32[2,512,256]{2,1,0:T(8,128)S(1)} custom-call(bf16[2,512,512]{2,1,0:T(8,128)(2,1)S(1)} %copy-done, bf16[2,128,512]{2,1,0:T(8,128)(2,1)S(1)} %relay.1.refs_1_.refs_2_.p_ref, bf16[2,128,512]{2,1,0:T(8,128)(2,1)S(1)} %collective-permute-done.4.refs_2_.refs_3_.q_ref, ...), custom_call_target="tpu_custom_call" | custom-call | flops 700000000 | bytes 2100000 | tf_op jit(solution)/shard_map/leaf/pallas_call | solution.py:28
  19.8 0.0 collective-permute-done.9.refs_0_
  19.8 0.9 %second0.1 = (s16[784,128]{1,0:T(8,128)(2,1)S(1)}, bf16[2,192,512]{2,1,0:T(8,128)(2,1)S(1)}, bf16[2,192,512]{2,1,0:T(8,128)(2,1)S(1)}) custom-call(s16[784,128]{1,0:T(8,128)(2,1)S(1)} %collective-permute-done.9.refs_0_, bf16[512,512]{1,0:T(8,128)(2,1)S(1)} %get-tuple-element.49.refs_1_.refs_2_, bf16[512,512]{1,0:T(8,128)(2,1)S(1)} %get-tuple-element.50.refs_2_.refs_3_, ...), custom_call_target="tpu_custom_call" | custom-call | flops 800000000 | bytes 2400000 | tf_op jit(solution)/shard_map/second0/pallas_call | solution.py:28
  20.7 2.0 %collective-permute-start.10 = (s16[784,128]{1,0:T(8,128)(2,1)S(1)}, s16[784,128]{1,0:T(8,128)(2,1)S(1)}, u32[]{:S(2)}, u32[]{:S(2)}) collective-permute-start(s16[784,128]{1,0:T(8,128)(2,1)S(1)} %get-tuple-element.62), channel_id=1, source_target_pairs={{0,8},{4,12},{8,0},{12,4},{16,24},{20,28},{24,16},{28,20},{1,9},{5... | collective-permute-start | bytes 602120 | tf_op jit(solution)/shard_map/ppermute | solution.py:23
  22.7 0.0 collective-permute-done.6.got_ref.refs_1_
  22.7 1.6 %collective-permute-start.8 = (s16[928,128]{1,0:T(8,128)(2,1)S(1)}, s16[928,128]{1,0:T(8,128)(2,1)S(1)}, u32[]{:S(2)}, u32[]{:S(2)}) collective-permute-start(s16[928,128]{1,0:T(8,128)(2,1)S(1)} %onward.1.refs_6_), channel_id=1, source_target_pairs={{0,4},{4,0},{8,12},{12,8},{16,20},{20,16},{24,28},{28,24},{1,5},{5... | collective-permute-start | bytes 712712 | tf_op jit(solution)/shard_map/ppermute | solution.py:23
  24.3 0.0 collective-permute-done.5.refs_0_
  24.3 0.9 %second1.1 = (s16[848,128]{1,0:T(8,128)(2,1)S(1)}, bf16[2,208,512]{2,1,0:T(8,128)(2,1)S(1)}, bf16[2,208,512]{2,1,0:T(8,128)(2,1)S(1)}) custom-call(s16[848,128]{1,0:T(8,128)(2,1)S(1)} %collective-permute-done.5.refs_0_, bf16[512,512]{1,0:T(8,128)(2,1)S(1)} %get-tuple-element.49.refs_1_.refs_2_, bf16[512,512]{1,0:T(8,128)(2,1)S(1)} %get-tuple-element.50.refs_2_.refs_3_, ...), custom_call_target="tpu_custom_call" | custom-call | flops 800000000 | bytes 2400000 | tf_op jit(solution)/shard_map/second1/pallas_call | solution.py:28
  25.2 1.4 %collective-permute-start.7 = (s16[848,128]{1,0:T(8,128)(2,1)S(1)}, s16[848,128]{1,0:T(8,128)(2,1)S(1)}, u32[]{:S(2)}, u32[]{:S(2)}) collective-permute-start(s16[848,128]{1,0:T(8,128)(2,1)S(1)} %get-tuple-element.52), channel_id=1, source_target_pairs={{0,8},{4,12},{8,0},{12,4},{16,24},{20,28},{24,16},{28,20},{1,9},{5... | collective-permute-start | bytes 651272 | tf_op jit(solution)/shard_map/ppermute | solution.py:23
  26.6 0.6 %third1.1 = (f32[2,208,512]{2,1,0:T(8,128)S(1)}, f32[208,512]{1,0:T(8,128)S(1)}) custom-call(bf16[2,208,512]{2,1,0:T(8,128)(2,1)S(1)} %get-tuple-element.53.refs_0_.refs_6_, bf16[2,208,512]{2,1,0:T(8,128)(2,1)S(1)} %get-tuple-element.54.refs_1_, f32[2,512,256]{2,1,0:T(8,128)S(1)} %near.1.dep_ref.rest_1_.refs_2_.refs_9_, ...), custom_call_target="tpu_custom_call" | custom-call | flops 500000000 | bytes 1500000 | tf_op jit(solution)/shard_map/third1/pallas_call | solution.py:28
  27.2 0.6 %third0.1 = (f32[2,192,512]{2,1,0:T(8,128)S(1)}, f32[192,512]{1,0:T(8,128)S(1)}) custom-call(bf16[2,192,512]{2,1,0:T(8,128)(2,1)S(1)} %get-tuple-element.63.refs_0_, bf16[2,192,512]{2,1,0:T(8,128)(2,1)S(1)} %get-tuple-element.64.refs_1_, f32[2,512,256]{2,1,0:T(8,128)S(1)} %near.1.dep_ref.rest_1_.refs_2_.refs_9_, ...), custom_call_target="tpu_custom_call" | custom-call | flops 500000000 | bytes 1500000 | tf_op jit(solution)/shard_map/third0/pallas_call | solution.py:28
  27.8 0.0 collective-permute-done.10.refs_3_
  27.8 1.6 %last0.1.refs_7_ = f32[2,512,512]{2,1,0:T(8,128)} custom-call(bf16[512,512]{1,0:T(8,128)(2,1)S(1)} %get-tuple-element.47.refs_14_.refs_0_, bf16[512,512]{1,0:T(8,128)(2,1)S(1)} %get-tuple-element.48.refs_15_.refs_1_, bf16[256,512]{1,0:T(8,128)(2,1)S(1)} %get-tuple-element.40.refs_4_.refs_12_.refs_2_, s16[784,128]{1,0:T(8,128)(2,1)S(1)} %collective-permute-done.10.refs_3_, ...), custom_call_target="tpu_custom_call" | custom-call | flops 1000000000 | bytes 3000000 | tf_op jit(solution)/shard_map/last0/pallas_call | solution.py:28
  29.4 0.0 collective-permute-done.8.refs_0_
  29.4 1.9 %around.1.refs_6_ = f32[2,112,512]{2,1,0:T(8,128)S(1)} custom-call(s16[928,128]{1,0:T(8,128)(2,1)S(1)} %collective-permute-done.8.refs_0_, s16[928,128]{1,0:T(8,128)(2,1)S(1)} %collective-permute-done.6.got_ref.refs_1_, bf16[512,512]{1,0:T(8,128)(2,1)S(1)} %get-tuple-element.49.refs_1_.refs_2_, bf16[512,512]{1,0:T(8,128)(2,1)S(1)} %get-tuple-element.50.refs_2_.refs_3_, ...), custom_call_target="tpu_custom_call" | custom-call | flops 2500000000 | bytes 7500000 | tf_op jit(solution)/shard_map/around/pallas_call | solution.py:28
  31.3 0.3 collective-permute-done.7.refs_3_
  31.6 1.8 %last1.1 = f32[2,512,512]{2,1,0:T(8,128)} custom-call(bf16[512,512]{1,0:T(8,128)(2,1)S(1)} %get-tuple-element.47.refs_14_.refs_0_, bf16[512,512]{1,0:T(8,128)(2,1)S(1)} %get-tuple-element.48.refs_15_.refs_1_, bf16[256,512]{1,0:T(8,128)(2,1)S(1)} %get-tuple-element.40.refs_4_.refs_12_.refs_2_, ...), custom_call_target="tpu_custom_call", output_to_operand_aliasing={{}: (7, {})} | custom-call | flops 1000000000 | bytes 3000000 | tf_op jit(solution)/shard_map/last1/pallas_call | solution.py:28
  (5 shorter events, 0.0 us)
Async XLA Ops:
  0.0 9.5 %collective-permute-start.3 = (bf16[2,128,512]{2,1,0:T(8,128)(2,1)}, bf16[2,128,512]{2,1,0:T(8,128)(2,1)S(1)}, u32[]{:S(2)}, u32[]{:S(2)}) collective-permute-start(bf16[2,128,512]{2,1,0:T(8,128)(2,1)} %bitcast.6), channel_id=1, source_target_pairs={{0,2},{1,3},{2,0},{3,1},{4,6},{5,7},{6,4},{7,5},{8,10},{9,11},{10,... | collective-permute-start | bytes 786440 | tf_op jit(solution)/shard_map/ppermute | solution.py:23
  2.9 1.7 %collective-permute-start.1 = (bf16[2,128,512]{2,1,0:T(8,128)(2,1)}, bf16[2,128,512]{2,1,0:T(8,128)(2,1)S(1)}, u32[]{:S(2)}, u32[]{:S(2)}) collective-permute-start(bf16[2,128,512]{2,1,0:T(8,128)(2,1)} %bitcast.7), channel_id=1, source_target_pairs={{0,1},{1,0},{2,3},{3,2},{4,5},{5,4},{6,7},{7,6},{8,9},{9,8},{10,11... | collective-permute-start | bytes 786440 | tf_op jit(solution)/shard_map/ppermute | solution.py:23
  2.9 1.7 %copy-start.1 = (bf16[1,2,128,512]{3,2,1,0:T(8,128)(2,1)S(1)}, bf16[1,2,128,512]{3,2,1,0:T(8,128)(2,1)}, u32[]{:S(2)}) copy-start(bf16[1,2,128,512]{3,2,1,0:T(8,128)(2,1)} %param.7) | copy-start | bytes 786436
  2.9 1.7 %copy-start.3 = (s32[8,2,256]{2,1,0:T(2,128)S(1)}, s32[8,2,256]{2,1,0:T(2,128)}, u32[]{:S(2)}) copy-start(s32[8,2,256]{2,1,0:T(2,128)} %refs_1_.1) | copy-start | bytes 49156
  2.9 1.7 %copy-start.4 = (f32[512]{0:T(512)S(1)}, f32[512]{0:T(512)}, u32[]{:S(2)}) copy-start(f32[512]{0:T(512)} %param.8) | copy-start | bytes 6148
  3.0 1.7 %copy-start.5 = (s32[8,2]{0,1:T(2,128)S(1)}, s32[8,2]{0,1:T(2,128)}, u32[]{:S(2)}) copy-start(s32[8,2]{0,1:T(2,128)} %param.10) | copy-start | bytes 196
  3.0 5.0 %collective-permute-start = (bf16[128,256]{1,0:T(8,128)(2,1)}, bf16[128,256]{1,0:T(8,128)(2,1)S(1)}, u32[]{:S(2)}, u32[]{:S(2)}) collective-permute-start(bf16[128,256]{1,0:T(8,128)(2,1)} %bitcast.10), channel_id=1, source_target_pairs={{0,4},{4,0},{8,12},{12,8},{16,20},{20,16},{24,28},{28,24},{1,5},{5... | collective-permute-start | bytes 196616 | tf_op jit(solution)/shard_map/ppermute | solution.py:23
  4.5 2.7 %copy-start = (bf16[2,512,512]{2,1,0:T(8,128)(2,1)S(1)}, bf16[2,512,512]{2,1,0:T(8,128)(2,1)}, u32[]{:S(2)}) copy-start(bf16[2,512,512]{2,1,0:T(8,128)(2,1)} %x_ref.5) | copy-start | bytes 3145732
  7.2 0.8 %copy-start.2 = (bf16[2,256,64]{1,2,0:T(8,128)(2,1)S(1)}, bf16[2,256,64]{1,2,0:T(8,128)(2,1)}, u32[]{:S(2)}) copy-start(bf16[2,256,64]{1,2,0:T(8,128)(2,1)} %param.11) | copy-start | bytes 196612
  9.5 2.0 %collective-permute-start.4 = (bf16[2,128,512]{2,1,0:T(8,128)(2,1)S(1)}, bf16[2,128,512]{2,1,0:T(8,128)(2,1)S(1)}, u32[]{:S(2)}, u32[]{:S(2)}) collective-permute-start(bf16[2,128,512]{2,1,0:T(8,128)(2,1)S(1)} %relay.1.refs_1_.refs_2_.p_ref), channel_id=1, source_target_pairs={{0,1},{1,0},{2,3},{3,2},{4,5},{5,4},{6,7},{7,6},{8,9},{9,8},{10,11... | collective-permute-start | bytes 786440 | tf_op jit(solution)/shard_map/ppermute | solution.py:23
  9.6 8.7 %collective-permute-start.2 = (bf16[2,128,256]{2,1,0:T(8,128)(2,1)S(1)}, bf16[2,128,256]{2,1,0:T(8,128)(2,1)S(1)}, u32[]{:S(2)}, u32[]{:S(2)}) collective-permute-start(bf16[2,128,256]{2,1,0:T(8,128)(2,1)S(1)} %pair.1.rest_0_), channel_id=1, source_target_pairs={{0,8},{4,12},{8,0},{12,4},{16,24},{20,28},{24,16},{28,20},{1,9},{5... | collective-permute-start | bytes 393224 | tf_op jit(solution)/shard_map/ppermute | solution.py:23
  12.4 7.4 %collective-permute-start.9 = (s16[784,128]{1,0:T(8,128)(2,1)S(1)}, s16[784,128]{1,0:T(8,128)(2,1)S(1)}, u32[]{:S(2)}, u32[]{:S(2)}) collective-permute-start(s16[784,128]{1,0:T(8,128)(2,1)S(1)} %get-tuple-element.61), channel_id=1, source_target_pairs={{0,4},{4,0},{8,12},{12,8},{16,20},{20,16},{24,28},{28,24},{1,5},{5... | collective-permute-start | bytes 602120 | tf_op jit(solution)/shard_map/ppermute | solution.py:23
  14.7 7.9 %collective-permute-start.6 = (s16[928,128]{1,0:T(8,128)(2,1)S(1)}, s16[928,128]{1,0:T(8,128)(2,1)S(1)}, u32[]{:S(2)}, u32[]{:S(2)}) collective-permute-start(s16[928,128]{1,0:T(8,128)(2,1)S(1)} %get-tuple-element.46.refs_3_.own_ref), channel_id=1, source_target_pairs={{0,8},{4,12},{8,0},{12,4},{16,24},{20,28},{24,16},{28,20},{1,9},{5... | collective-permute-start | bytes 712712 | tf_op jit(solution)/shard_map/ppermute | solution.py:23
  16.9 7.4 %collective-permute-start.5 = (s16[848,128]{1,0:T(8,128)(2,1)S(1)}, s16[848,128]{1,0:T(8,128)(2,1)S(1)}, u32[]{:S(2)}, u32[]{:S(2)}) collective-permute-start(s16[848,128]{1,0:T(8,128)(2,1)S(1)} %ready.1.dep_ref), channel_id=1, source_target_pairs={{0,4},{4,0},{8,12},{12,8},{16,20},{20,16},{24,28},{28,24},{1,5},{5... | collective-permute-start | bytes 651272 | tf_op jit(solution)/shard_map/ppermute | solution.py:23
  20.7 7.1 %collective-permute-start.10 = (s16[784,128]{1,0:T(8,128)(2,1)S(1)}, s16[784,128]{1,0:T(8,128)(2,1)S(1)}, u32[]{:S(2)}, u32[]{:S(2)}) collective-permute-start(s16[784,128]{1,0:T(8,128)(2,1)S(1)} %get-tuple-element.62), channel_id=1, source_target_pairs={{0,8},{4,12},{8,0},{12,4},{16,24},{20,28},{24,16},{28,20},{1,9},{5... | collective-permute-start | bytes 602120 | tf_op jit(solution)/shard_map/ppermute | solution.py:23
  22.7 6.7 %collective-permute-start.8 = (s16[928,128]{1,0:T(8,128)(2,1)S(1)}, s16[928,128]{1,0:T(8,128)(2,1)S(1)}, u32[]{:S(2)}, u32[]{:S(2)}) collective-permute-start(s16[928,128]{1,0:T(8,128)(2,1)S(1)} %onward.1.refs_6_), channel_id=1, source_target_pairs={{0,4},{4,0},{8,12},{12,8},{16,20},{20,16},{24,28},{28,24},{1,5},{5... | collective-permute-start | bytes 712712 | tf_op jit(solution)/shard_map/ppermute | solution.py:23
  25.2 6.4 %collective-permute-start.7 = (s16[848,128]{1,0:T(8,128)(2,1)S(1)}, s16[848,128]{1,0:T(8,128)(2,1)S(1)}, u32[]{:S(2)}, u32[]{:S(2)}) collective-permute-start(s16[848,128]{1,0:T(8,128)(2,1)S(1)} %get-tuple-element.52), channel_id=1, source_target_pairs={{0,8},{4,12},{8,0},{12,4},{16,24},{20,28},{24,16},{28,20},{1,9},{5... | collective-permute-start | bytes 651272 | tf_op jit(solution)/shard_map/ppermute | solution.py:23

commit v7 on v6

--- a/solution.py
+++ b/solution.py
@@ -450,8 +450,7 @@
     out_ref, hold_ref, sem = rest[-3:]
     write, copies = writer(out_ref, sem, blocks)
     if done_at is not None:
-        for i in range(2):
-            write(rest[0], i, done_at)
+        write(rest[0], slice(None), done_at)
     for i, value in finish(in_ref, part_ref, p_ref, khi_ref[...], klo_ref[...], e1_ref[...]):
         hold_ref[i] = value
         write(hold_ref, i, start)
@@ -595,7 +594,7 @@
             [shape(2, nf, width)],
             [khi, klo, e1] + late[i] + ready + out,
             [VMEM] * (6 + len(ready)) + [ANY] * len(out),
-            [pltpu.VMEM((2, n, width), F32), pltpu.SemaphoreType.DMA(((4 if ready else 2) * blocks,))],
+            [pltpu.VMEM((2, n, width), F32), pltpu.SemaphoreType.DMA(((3 if ready else 2) * blocks,))],
             out_specs=[ANY],
             input_output_aliases={6 + len(ready): 0} if out else {},
         )

time: 33.5 us -> 33.5 us (level)
  no operation moved by 1% of the time
where the time goes in v7:
time: 33.5 us; the launch traced here: 33.3 us
  Pallas kernels  16.1 us (48%)
  starting transfers between devices  15.1 us (45%)
  waiting for transfers between devices  1.77 us (5%)
    pallas_call x19, Pallas kernels, call(): pl.pallas_call(body, name=name, out_shape=outs, in_specs=specs or [VMEM]...  16.1 us
    ppermute x11, starting transfers between devices, swap(): lax.ppermute(value, axis, [(s, s ^ mask) for s in range(lax.axis_size(axi...  15.1 us
    ppermute x11, waiting for transfers between devices, swap(): lax.ppermute(value, axis, [(s, s ^ mask) for s in range(lax.axis_size(axi...  1.77 us
  transfers between devices with their start and end apart: 11, of which 3 were waited for; matrix products, arithmetic and copies ran while one was open for 0% of the time, Pallas kernels for 43%

profile of v7, /device:TPU:0, one launch (start us, length us, event | category | flops | bytes accessed | tf_op | source)
XLA Modules:
  0.0 33.3 jit_solution(6827277875930560320)
XLA Ops:
  0.0 2.9 %collective-permute-start.3 = (bf16[2,128,512]{2,1,0:T(8,128)(2,1)}, bf16[2,128,512]{2,1,0:T(8,128)(2,1)S(1)}, u32[]{:S(2)}, u32[]{:S(2)}) collective-permute-start(bf16[2,128,512]{2,1,0:T(8,128)(2,1)} %bitcast.6), channel_id=1, source_target_pairs={{0,2},{1,3},{2,0},{3,1},{4,6},{5,7},{6,4},{7,5},{8,10},{9,11},{10,... | collective-permute-start | bytes 786440 | tf_op jit(solution)/shard_map/ppermute | solution.py:23
  2.9 0.0 collective-permute-start.1
  2.9 0.0 copy-start.1
  2.9 0.0 copy-start.3
  2.9 0.0 copy-start.4
  3.0 0.0 copy-start.5
  3.0 1.6 %collective-permute-start = (bf16[128,256]{1,0:T(8,128)(2,1)}, bf16[128,256]{1,0:T(8,128)(2,1)S(1)}, u32[]{:S(2)}, u32[]{:S(2)}) collective-permute-start(bf16[128,256]{1,0:T(8,128)(2,1)} %bitcast.10), channel_id=1, source_target_pairs={{0,4},{4,0},{8,12},{12,8},{16,20},{20,16},{24,28},{28,24},{1,5},{5... | collective-permute-start | bytes 196616 | tf_op jit(solution)/shard_map/ppermute | solution.py:23
  4.6 0.1 collective-permute-done.1.refs_4_.q_ref
  4.7 0.0 copy-done.1
  4.7 0.0 copy-done.3
  4.7 0.0 copy-done.4
  4.7 0.0 copy-done.5
  4.7 2.5 %plan.1 = (bf16[256,512]{1,0:T(8,128)(2,1)S(1)}, bf16[256,512]{1,0:T(8,128)(2,1)S(1)}, f32[8,256]{1,0:T(8,128)S(1)}, bf16[512,512]{1,0:T(8,128)(2,1)S(1)}, bf16[...) custom-call(s32[2,8]{1,0:T(2,128)S(1)} %bitcast.14, ...), custom_call_target="tpu_custom_call" | custom-call | flops 1000000000 | bytes 3000000 | tf_op jit(solution)/shard_map/plan/pallas_call | solution.py:28
  7.2 0.0 copy-start.2
  7.2 0.0 copy-done
  7.3 0.7 %near.1.dep_ref.rest_1_.refs_2_.refs_9_ = f32[2,512,256]{2,1,0:T(8,128)S(1)} custom-call(bf16[2,512,512]{2,1,0:T(8,128)(2,1)S(1)} %copy-done, bf16[2,128,512]{2,1,0:T(8,128)(2,1)S(1)} %bitcast.9, bf16[2,128,512]{2,1,0:T(8,128)(2,1)S(1)} %collective-permute-done.1.refs_4_.q_ref, bf16[256,1024]{1,0:T(8,128)(2,1)S(1)} %get-tuple-element.36.dep_ref.refs_0_), custom_call_target="tpu_custom_call" | custom-call | flops 700000000 | bytes 2100000 | tf_op jit(solution)/shard_map/near/pallas_call | solution.py:28
  8.0 0.0 collective-permute-done.b_ref.near_ref
  8.0 0.1 copy-done.2
  8.1 1.4 %collective-permute-done.3.in_ref = bf16[2,128,512]{2,1,0:T(8,128)(2,1)S(1)} collective-permute-done((bf16[2,128,512]{2,1,0:T(8,128)(2,1)}, bf16[2,128,512]{2,1,0:T(8,128)(2,1)S(1)}, u32[]{:S(2)}, u32[]{:S(2)}) %collective-permute-start.3) | collective-permute-done | bytes 262176 | tf_op jit(solution)/shard_map/ppermute | solution.py:23
  9.5 0.1 collective-permute-start.4
  9.6 1.9 %collective-permute-start.2 = (bf16[2,128,256]{2,1,0:T(8,128)(2,1)S(1)}, bf16[2,128,256]{2,1,0:T(8,128)(2,1)S(1)}, u32[]{:S(2)}, u32[]{:S(2)}) collective-permute-start(bf16[2,128,256]{2,1,0:T(8,128)(2,1)S(1)} %pair.1.rest_0_), channel_id=1, source_target_pairs={{0,8},{4,12},{8,0},{12,4},{16,24},{20,28},{24,16},{28,20},{1,9},{5... | collective-permute-start | bytes 393224 | tf_op jit(solution)/shard_map/ppermute | solution.py:23
  11.4 0.0 collective-permute-done.4.refs_2_.refs_3_.q_ref
  11.5 0.9 %first.1 = (bf16[256,1024]{1,0:T(8,128)(2,1)S(1)}, s16[784,128]{1,0:T(8,128)(2,1)S(1)}, s16[464,128]{1,0:T(8,128)(2,1)S(1)}) custom-call(bf16[256,1024]{1,0:T(8,128)(2,1)S(1)} %get-tuple-element.36.dep_ref.refs_0_, bf16[2,128,512]{2,1,0:T(8,128)(2,1)S(1)} %relay.1.refs_1_.refs_2_.p_ref, ...), custom_call_target="tpu_custom_call" | custom-call | flops 800000000 | bytes 2400000 | tf_op jit(solution)/shard_map/first/pallas_call | solution.py:28
  12.4 1.6 %collective-permute-start.9 = (s16[784,128]{1,0:T(8,128)(2,1)S(1)}, s16[784,128]{1,0:T(8,128)(2,1)S(1)}, u32[]{:S(2)}, u32[]{:S(2)}) collective-permute-start(s16[784,128]{1,0:T(8,128)(2,1)S(1)} %get-tuple-element.61), channel_id=1, source_target_pairs={{0,4},{4,0},{8,12},{12,8},{16,20},{20,16},{24,28},{28,24},{1,5},{5... | collective-permute-start | bytes 602120 | tf_op jit(solution)/shard_map/ppermute | solution.py:23
  14.0 0.8 %ahead.1 = (bf16[256,1024]{1,0:T(8,128)(2,1)S(1)}, s16[928,128]{1,0:T(8,128)(2,1)S(1)}) custom-call(bf16[2,512,512]{2,1,0:T(8,128)(2,1)S(1)} %copy-done, bf16[256,1024]{1,0:T(8,128)(2,1)S(1)} %get-tuple-element.39.refs_1_, bf16[2,128,512]{2,1,0:T(8,128)(2,1)S(1)} %relay.1.refs_1_.refs_2_.p_ref, ...), custom_call_target="tpu_custom_call" | custom-call | flops 1400000000 | bytes 4200000 | tf_op jit(solution)/shard_map/ahead/pallas_call | solution.py:28
  14.7 1.5 %collective-permute-start.6 = (s16[928,128]{1,0:T(8,128)(2,1)S(1)}, s16[928,128]{1,0:T(8,128)(2,1)S(1)}, u32[]{:S(2)}, u32[]{:S(2)}) collective-permute-start(s16[928,128]{1,0:T(8,128)(2,1)S(1)} %get-tuple-element.46.refs_3_.own_ref), channel_id=1, source_target_pairs={{0,8},{4,12},{8,0},{12,4},{16,24},{20,28},{24,16},{28,20},{1,9},{5... | collective-permute-start | bytes 712712 | tf_op jit(solution)/shard_map/ppermute | solution.py:23
  16.3 0.7 %ready.1.dep_ref = s16[848,128]{1,0:T(8,128)(2,1)S(1)} custom-call(bf16[2,512,512]{2,1,0:T(8,128)(2,1)S(1)} %copy-done, bf16[256,1024]{1,0:T(8,128)(2,1)S(1)} %get-tuple-element.45.refs_1_, f32[8,256]{1,0:T(8,128)S(1)} %get-tuple-element.42.refs_5_.refs_6_.refs_2_, s16[928,128]{1,0:T(8,128)(2,1)S(1)} %get-tuple-element.46.refs_3_.own_ref), custom_call_target="tpu_custom_call" | custom-call | flops 600000000 | bytes 1800000 | tf_op jit(solution)/shard_map/ready/pallas_call | solution.py:28
  16.9 0.6 %collective-permute-start.5 = (s16[848,128]{1,0:T(8,128)(2,1)S(1)}, s16[848,128]{1,0:T(8,128)(2,1)S(1)}, u32[]{:S(2)}, u32[]{:S(2)}) collective-permute-start(s16[848,128]{1,0:T(8,128)(2,1)S(1)} %ready.1.dep_ref), channel_id=1, source_target_pairs={{0,4},{4,0},{8,12},{12,8},{16,20},{20,16},{24,28},{28,24},{1,5},{5... | collective-permute-start | bytes 651272 | tf_op jit(solution)/shard_map/ppermute | solution.py:23
  17.5 0.7 %rows.1.dep_ref.refs_3_.refs_8_ = f32[512,512]{1,0:T(8,128)S(1)} custom-call(bf16[2,512,512]{2,1,0:T(8,128)(2,1)S(1)} %copy-done, bf16[256,1024]{1,0:T(8,128)(2,1)S(1)} %get-tuple-element.44.picked_ref, s16[848,128]{1,0:T(8,128)(2,1)S(1)} %ready.1.dep_ref), custom_call_target="tpu_custom_call" | custom-call | flops 1000000000 | bytes 3000000 | tf_op jit(solution)/shard_map/rows/pallas_call | solution.py:28
  18.2 0.0 collective-permute-done.2.far_ref
  18.3 0.8 %core.1 = (bf16[512,512]{1,0:T(8,128)(2,1)S(1)}, bf16[512,512]{1,0:T(8,128)(2,1)S(1)}, bf16[512,512]{1,0:T(8,128)(2,1)S(1)}) custom-call(bf16[128,256]{1,0:T(8,128)(2,1)S(1)} %bitcast.12, bf16[128,256]{1,0:T(8,128)(2,1)S(1)} %collective-permute-done.b_ref.near_ref, bf16[2,128,256]{2,1,0:T(8,128)(2,1)S(1)} %collective-permute-done.2.far_ref, ...), custom_call_target="tpu_custom_call" | custom-call | flops 1000000000 | bytes 3000000 | tf_op jit(solution)/shard_map/core/pallas_call | solution.py:28
  19.0 0.7 %leaf.1.refs_3_.refs_10_.refs_6_ = f32[2,512,256]{2,1,0:T(8,128)S(1)} custom-call(bf16[2,512,512]{2,1,0:T(8,128)(2,1)S(1)} %copy-done, bf16[2,128,512]{2,1,0:T(8,128)(2,1)S(1)} %relay.1.refs_1_.refs_2_.p_ref, bf16[2,128,512]{2,1,0:T(8,128)(2,1)S(1)} %collective-permute-done.4.refs_2_.refs_3_.q_ref, ...), custom_call_target="tpu_custom_call" | custom-call | flops 700000000 | bytes 2100000 | tf_op jit(solution)/shard_map/leaf/pallas_call | solution.py:28
  19.8 0.0 collective-permute-done.9.refs_0_
  19.8 0.9 %second0.1 = (s16[784,128]{1,0:T(8,128)(2,1)S(1)}, bf16[2,192,512]{2,1,0:T(8,128)(2,1)S(1)}, bf16[2,192,512]{2,1,0:T(8,128)(2,1)S(1)}) custom-call(s16[784,128]{1,0:T(8,128)(2,1)S(1)} %collective-permute-done.9.refs_0_, bf16[512,512]{1,0:T(8,128)(2,1)S(1)} %get-tuple-element.49.refs_1_.refs_2_, bf16[512,512]{1,0:T(8,128)(2,1)S(1)} %get-tuple-element.50.refs_2_.refs_3_, ...), custom_call_target="tpu_custom_call" | custom-call | flops 800000000 | bytes 2400000 | tf_op jit(solution)/shard_map/second0/pallas_call | solution.py:28
  20.7 2.0 %collective-permute-start.10 = (s16[784,128]{1,0:T(8,128)(2,1)S(1)}, s16[784,128]{1,0:T(8,128)(2,1)S(1)}, u32[]{:S(2)}, u32[]{:S(2)}) collective-permute-start(s16[784,128]{1,0:T(8,128)(2,1)S(1)} %get-tuple-element.62), channel_id=1, source_target_pairs={{0,8},{4,12},{8,0},{12,4},{16,24},{20,28},{24,16},{28,20},{1,9},{5... | collective-permute-start | bytes 602120 | tf_op jit(solution)/shard_map/ppermute | solution.py:23
  22.7 0.0 collective-permute-done.6.got_ref.refs_1_
  22.7 1.6 %collective-permute-start.8 = (s16[928,128]{1,0:T(8,128)(2,1)S(1)}, s16[928,128]{1,0:T(8,128)(2,1)S(1)}, u32[]{:S(2)}, u32[]{:S(2)}) collective-permute-start(s16[928,128]{1,0:T(8,128)(2,1)S(1)} %onward.1.refs_6_), channel_id=1, source_target_pairs={{0,4},{4,0},{8,12},{12,8},{16,20},{20,16},{24,28},{28,24},{1,5},{5... | collective-permute-start | bytes 712712 | tf_op jit(solution)/shard_map/ppermute | solution.py:23
  24.3 0.0 collective-permute-done.5.refs_0_
  24.3 0.9 %second1.1 = (s16[848,128]{1,0:T(8,128)(2,1)S(1)}, bf16[2,208,512]{2,1,0:T(8,128)(2,1)S(1)}, bf16[2,208,512]{2,1,0:T(8,128)(2,1)S(1)}) custom-call(s16[848,128]{1,0:T(8,128)(2,1)S(1)} %collective-permute-done.5.refs_0_, bf16[512,512]{1,0:T(8,128)(2,1)S(1)} %get-tuple-element.49.refs_1_.refs_2_, bf16[512,512]{1,0:T(8,128)(2,1)S(1)} %get-tuple-element.50.refs_2_.refs_3_, ...), custom_call_target="tpu_custom_call" | custom-call | flops 800000000 | bytes 2400000 | tf_op jit(solution)/shard_map/second1/pallas_call | solution.py:28
  25.2 1.4 %collective-permute-start.7 = (s16[848,128]{1,0:T(8,128)(2,1)S(1)}, s16[848,128]{1,0:T(8,128)(2,1)S(1)}, u32[]{:S(2)}, u32[]{:S(2)}) collective-permute-start(s16[848,128]{1,0:T(8,128)(2,1)S(1)} %get-tuple-element.52), channel_id=1, source_target_pairs={{0,8},{4,12},{8,0},{12,4},{16,24},{20,28},{24,16},{28,20},{1,9},{5... | collective-permute-start | bytes 651272 | tf_op jit(solution)/shard_map/ppermute | solution.py:23
  26.6 0.6 %third1.1 = (f32[2,208,512]{2,1,0:T(8,128)S(1)}, f32[208,512]{1,0:T(8,128)S(1)}) custom-call(bf16[2,208,512]{2,1,0:T(8,128)(2,1)S(1)} %get-tuple-element.53.refs_0_.refs_6_, bf16[2,208,512]{2,1,0:T(8,128)(2,1)S(1)} %get-tuple-element.54.refs_1_, f32[2,512,256]{2,1,0:T(8,128)S(1)} %near.1.dep_ref.rest_1_.refs_2_.refs_9_, ...), custom_call_target="tpu_custom_call" | custom-call | flops 500000000 | bytes 1500000 | tf_op jit(solution)/shard_map/third1/pallas_call | solution.py:28
  27.2 0.6 %third0.1 = (f32[2,192,512]{2,1,0:T(8,128)S(1)}, f32[192,512]{1,0:T(8,128)S(1)}) custom-call(bf16[2,192,512]{2,1,0:T(8,128)(2,1)S(1)} %get-tuple-element.63.refs_0_, bf16[2,192,512]{2,1,0:T(8,128)(2,1)S(1)} %get-tuple-element.64.refs_1_, f32[2,512,256]{2,1,0:T(8,128)S(1)} %near.1.dep_ref.rest_1_.refs_2_.refs_9_, ...), custom_call_target="tpu_custom_call" | custom-call | flops 500000000 | bytes 1500000 | tf_op jit(solution)/shard_map/third0/pallas_call | solution.py:28
  27.8 0.0 collective-permute-done.10.refs_3_
  27.8 1.6 %last0.1.refs_7_ = f32[2,512,512]{2,1,0:T(8,128)} custom-call(bf16[512,512]{1,0:T(8,128)(2,1)S(1)} %get-tuple-element.47.refs_14_.refs_0_, bf16[512,512]{1,0:T(8,128)(2,1)S(1)} %get-tuple-element.48.refs_15_.refs_1_, bf16[256,512]{1,0:T(8,128)(2,1)S(1)} %get-tuple-element.40.refs_4_.refs_12_.refs_2_, s16[784,128]{1,0:T(8,128)(2,1)S(1)} %collective-permute-done.10.refs_3_, ...), custom_call_target="tpu_custom_call" | custom-call | flops 1000000000 | bytes 3000000 | tf_op jit(solution)/shard_map/last0/pallas_call | solution.py:28
  29.4 0.0 collective-permute-done.8.refs_0_
  29.4 1.9 %around.1.refs_6_ = f32[2,112,512]{2,1,0:T(8,128)S(1)} custom-call(s16[928,128]{1,0:T(8,128)(2,1)S(1)} %collective-permute-done.8.refs_0_, s16[928,128]{1,0:T(8,128)(2,1)S(1)} %collective-permute-done.6.got_ref.refs_1_, bf16[512,512]{1,0:T(8,128)(2,1)S(1)} %get-tuple-element.49.refs_1_.refs_2_, bf16[512,512]{1,0:T(8,128)(2,1)S(1)} %get-tuple-element.50.refs_2_.refs_3_, ...), custom_call_target="tpu_custom_call" | custom-call | flops 2500000000 | bytes 7500000 | tf_op jit(solution)/shard_map/around/pallas_call | solution.py:28
  31.3 0.3 collective-permute-done.7.refs_3_
  31.6 1.7 %last1.1 = f32[2,512,512]{2,1,0:T(8,128)} custom-call(bf16[512,512]{1,0:T(8,128)(2,1)S(1)} %get-tuple-element.47.refs_14_.refs_0_, bf16[512,512]{1,0:T(8,128)(2,1)S(1)} %get-tuple-element.48.refs_15_.refs_1_, bf16[256,512]{1,0:T(8,128)(2,1)S(1)} %get-tuple-element.40.refs_4_.refs_12_.refs_2_, ...), custom_call_target="tpu_custom_call", output_to_operand_aliasing={{}: (7, {})} | custom-call | flops 1000000000 | bytes 3000000 | tf_op jit(solution)/shard_map/last1/pallas_call | solution.py:28
  (5 shorter events, 0.0 us)
Async XLA Ops:
  0.0 9.5 %collective-permute-start.3 = (bf16[2,128,512]{2,1,0:T(8,128)(2,1)}, bf16[2,128,512]{2,1,0:T(8,128)(2,1)S(1)}, u32[]{:S(2)}, u32[]{:S(2)}) collective-permute-start(bf16[2,128,512]{2,1,0:T(8,128)(2,1)} %bitcast.6), channel_id=1, source_target_pairs={{0,2},{1,3},{2,0},{3,1},{4,6},{5,7},{6,4},{7,5},{8,10},{9,11},{10,... | collective-permute-start | bytes 786440 | tf_op jit(solution)/shard_map/ppermute | solution.py:23
  2.9 1.7 %collective-permute-start.1 = (bf16[2,128,512]{2,1,0:T(8,128)(2,1)}, bf16[2,128,512]{2,1,0:T(8,128)(2,1)S(1)}, u32[]{:S(2)}, u32[]{:S(2)}) collective-permute-start(bf16[2,128,512]{2,1,0:T(8,128)(2,1)} %bitcast.7), channel_id=1, source_target_pairs={{0,1},{1,0},{2,3},{3,2},{4,5},{5,4},{6,7},{7,6},{8,9},{9,8},{10,11... | collective-permute-start | bytes 786440 | tf_op jit(solution)/shard_map/ppermute | solution.py:23
  2.9 1.7 %copy-start.1 = (bf16[1,2,128,512]{3,2,1,0:T(8,128)(2,1)S(1)}, bf16[1,2,128,512]{3,2,1,0:T(8,128)(2,1)}, u32[]{:S(2)}) copy-start(bf16[1,2,128,512]{3,2,1,0:T(8,128)(2,1)} %param.7) | copy-start | bytes 786436
  2.9 1.7 %copy-start.3 = (s32[8,2,256]{2,1,0:T(2,128)S(1)}, s32[8,2,256]{2,1,0:T(2,128)}, u32[]{:S(2)}) copy-start(s32[8,2,256]{2,1,0:T(2,128)} %refs_1_.1) | copy-start | bytes 49156
  2.9 1.7 %copy-start.4 = (f32[512]{0:T(512)S(1)}, f32[512]{0:T(512)}, u32[]{:S(2)}) copy-start(f32[512]{0:T(512)} %param.8) | copy-start | bytes 6148
  3.0 1.7 %copy-start.5 = (s32[8,2]{0,1:T(2,128)S(1)}, s32[8,2]{0,1:T(2,128)}, u32[]{:S(2)}) copy-start(s32[8,2]{0,1:T(2,128)} %param.10) | copy-start | bytes 196
  3.0 5.0 %collective-permute-start = (bf16[128,256]{1,0:T(8,128)(2,1)}, bf16[128,256]{1,0:T(8,128)(2,1)S(1)}, u32[]{:S(2)}, u32[]{:S(2)}) collective-permute-start(bf16[128,256]{1,0:T(8,128)(2,1)} %bitcast.10), channel_id=1, source_target_pairs={{0,4},{4,0},{8,12},{12,8},{16,20},{20,16},{24,28},{28,24},{1,5},{5... | collective-permute-start | bytes 196616 | tf_op jit(solution)/shard_map/ppermute | solution.py:23
  4.5 2.7 %copy-start = (bf16[2,512,512]{2,1,0:T(8,128)(2,1)S(1)}, bf16[2,512,512]{2,1,0:T(8,128)(2,1)}, u32[]{:S(2)}) copy-start(bf16[2,512,512]{2,1,0:T(8,128)(2,1)} %x_ref.5) | copy-start | bytes 3145732
  7.2 0.8 %copy-start.2 = (bf16[2,256,64]{1,2,0:T(8,128)(2,1)S(1)}, bf16[2,256,64]{1,2,0:T(8,128)(2,1)}, u32[]{:S(2)}) copy-start(bf16[2,256,64]{1,2,0:T(8,128)(2,1)} %param.11) | copy-start | bytes 196612
  9.5 2.0 %collective-permute-start.4 = (bf16[2,128,512]{2,1,0:T(8,128)(2,1)S(1)}, bf16[2,128,512]{2,1,0:T(8,128)(2,1)S(1)}, u32[]{:S(2)}, u32[]{:S(2)}) collective-permute-start(bf16[2,128,512]{2,1,0:T(8,128)(2,1)S(1)} %relay.1.refs_1_.refs_2_.p_ref), channel_id=1, source_target_pairs={{0,1},{1,0},{2,3},{3,2},{4,5},{5,4},{6,7},{7,6},{8,9},{9,8},{10,11... | collective-permute-start | bytes 786440 | tf_op jit(solution)/shard_map/ppermute | solution.py:23
  9.6 8.7 %collective-permute-start.2 = (bf16[2,128,256]{2,1,0:T(8,128)(2,1)S(1)}, bf16[2,128,256]{2,1,0:T(8,128)(2,1)S(1)}, u32[]{:S(2)}, u32[]{:S(2)}) collective-permute-start(bf16[2,128,256]{2,1,0:T(8,128)(2,1)S(1)} %pair.1.rest_0_), channel_id=1, source_target_pairs={{0,8},{4,12},{8,0},{12,4},{16,24},{20,28},{24,16},{28,20},{1,9},{5... | collective-permute-start | bytes 393224 | tf_op jit(solution)/shard_map/ppermute | solution.py:23
  12.4 7.4 %collective-permute-start.9 = (s16[784,128]{1,0:T(8,128)(2,1)S(1)}, s16[784,128]{1,0:T(8,128)(2,1)S(1)}, u32[]{:S(2)}, u32[]{:S(2)}) collective-permute-start(s16[784,128]{1,0:T(8,128)(2,1)S(1)} %get-tuple-element.61), channel_id=1, source_target_pairs={{0,4},{4,0},{8,12},{12,8},{16,20},{20,16},{24,28},{28,24},{1,5},{5... | collective-permute-start | bytes 602120 | tf_op jit(solution)/shard_map/ppermute | solution.py:23
  14.7 7.9 %collective-permute-start.6 = (s16[928,128]{1,0:T(8,128)(2,1)S(1)}, s16[928,128]{1,0:T(8,128)(2,1)S(1)}, u32[]{:S(2)}, u32[]{:S(2)}) collective-permute-start(s16[928,128]{1,0:T(8,128)(2,1)S(1)} %get-tuple-element.46.refs_3_.own_ref), channel_id=1, source_target_pairs={{0,8},{4,12},{8,0},{12,4},{16,24},{20,28},{24,16},{28,20},{1,9},{5... | collective-permute-start | bytes 712712 | tf_op jit(solution)/shard_map/ppermute | solution.py:23
  16.9 7.4 %collective-permute-start.5 = (s16[848,128]{1,0:T(8,128)(2,1)S(1)}, s16[848,128]{1,0:T(8,128)(2,1)S(1)}, u32[]{:S(2)}, u32[]{:S(2)}) collective-permute-start(s16[848,128]{1,0:T(8,128)(2,1)S(1)} %ready.1.dep_ref), channel_id=1, source_target_pairs={{0,4},{4,0},{8,12},{12,8},{16,20},{20,16},{24,28},{28,24},{1,5},{5... | collective-permute-start | bytes 651272 | tf_op jit(solution)/shard_map/ppermute | solution.py:23
  20.7 7.1 %collective-permute-start.10 = (s16[784,128]{1,0:T(8,128)(2,1)S(1)}, s16[784,128]{1,0:T(8,128)(2,1)S(1)}, u32[]{:S(2)}, u32[]{:S(2)}) collective-permute-start(s16[784,128]{1,0:T(8,128)(2,1)S(1)} %get-tuple-element.62), channel_id=1, source_target_pairs={{0,8},{4,12},{8,0},{12,4},{16,24},{20,28},{24,16},{28,20},{1,9},{5... | collective-permute-start | bytes 602120 | tf_op jit(solution)/shard_map/ppermute | solution.py:23
  22.7 6.7 %collective-permute-start.8 = (s16[928,128]{1,0:T(8,128)(2,1)S(1)}, s16[928,128]{1,0:T(8,128)(2,1)S(1)}, u32[]{:S(2)}, u32[]{:S(2)}) collective-permute-start(s16[928,128]{1,0:T(8,128)(2,1)S(1)} %onward.1.refs_6_), channel_id=1, source_target_pairs={{0,4},{4,0},{8,12},{12,8},{16,20},{20,16},{24,28},{28,24},{1,5},{5... | collective-permute-start | bytes 712712 | tf_op jit(solution)/shard_map/ppermute | solution.py:23
  25.2 6.4 %collective-permute-start.7 = (s16[848,128]{1,0:T(8,128)(2,1)S(1)}, s16[848,128]{1,0:T(8,128)(2,1)S(1)}, u32[]{:S(2)}, u32[]{:S(2)}) collective-permute-start(s16[848,128]{1,0:T(8,128)(2,1)S(1)} %get-tuple-element.52), channel_id=1, source_target_pairs={{0,8},{4,12},{8,0},{12,4},{16,24},{20,28},{24,16},{28,20},{1,9},{5... | collective-permute-start | bytes 651272 | tf_op jit(solution)/shard_map/ppermute | solution.py:23

commit v8 on v7

--- a/solution.py
+++ b/solution.py
@@ -9,7 +9,7 @@
 WAVENUM = 0.7
 BF = jnp.bfloat16
 F32 = jnp.float32
-SHARES = (12, 13, 7)
+SHARES = (13, 12, 7)
 TOP = 32766.0
 STEPS = 128.0
 LANES = 128
@@ -523,7 +523,7 @@
         lambda *refs: ahead_body(*refs, start=side_start, n=side_n),
         "ahead",
         [shape(kmax, 2 * width, dtype=BF), shape(2 * packed_shape(side_n, kmax).shape[0], LANES, dtype=jnp.int16)],
-        [x, part1, across, beyond, e1, side, q, e0],
+        [x, part1, across, beyond, e1, side, q, head],
         [VMEM] * 7 + [ANY],
         cost=1.4,
     )

time: 33.5 us -> 33.6 us (level)
  waiting for transfers between devices: 1.77 us -> 2.57 us
  starting transfers between devices: 15.1 us -> 14.4 us
    ppermute x11, waiting for transfers between devices: 1.77 us -> 2.57 us  [swap(): lax.ppermute(value, axis, [(s, s ^ mask) for s in range(lax.axis_size(axi...]
    ppermute x11, starting transfers between devices: 15.1 us -> 14.4 us  [swap(): lax.ppermute(value, axis, [(s, s ^ mask) for s in range(lax.axis_size(axi...]
  transfers between devices with their start and end apart: 11 -> 11, of which waited for: 3 -> 4; matrix products, arithmetic and copies ran while one was open for 0% -> 0% of each run, Pallas kernels for 43% -> 43%
where the time goes in v8:
time: 33.6 us; the launch traced here: 33.4 us
  Pallas kernels  16.1 us (48%)
  starting transfers between devices  14.4 us (43%)
  waiting for transfers between devices  2.57 us (8%)
    pallas_call x19, Pallas kernels, call(): pl.pallas_call(body, name=name, out_shape=outs, in_specs=specs or [VMEM]...  16.1 us
    ppermute x11, starting transfers between devices, swap(): lax.ppermute(value, axis, [(s, s ^ mask) for s in range(lax.axis_size(axi...  14.4 us
    ppermute x11, waiting for transfers between devices, swap(): lax.ppermute(value, axis, [(s, s ^ mask) for s in range(lax.axis_size(axi...  2.57 us
  transfers between devices with their start and end apart: 11, of which 4 were waited for; matrix products, arithmetic and copies ran while one was open for 0% of the time, Pallas kernels for 43%

profile of v8, /device:TPU:0, one launch (start us, length us, event | category | flops | bytes accessed | tf_op | source)
XLA Modules:
  0.0 33.4 jit_solution(16280532041259079097)
XLA Ops:
  0.0 2.9 %collective-permute-start.3 = (bf16[2,128,512]{2,1,0:T(8,128)(2,1)}, bf16[2,128,512]{2,1,0:T(8,128)(2,1)S(1)}, u32[]{:S(2)}, u32[]{:S(2)}) collective-permute-start(bf16[2,128,512]{2,1,0:T(8,128)(2,1)} %bitcast.6), channel_id=1, source_target_pairs={{0,2},{1,3},{2,0},{3,1},{4,6},{5,7},{6,4},{7,5},{8,10},{9,11},{10,... | collective-permute-start | bytes 786440 | tf_op jit(solution)/shard_map/ppermute | solution.py:23
  2.9 0.0 collective-permute-start.1
  2.9 0.0 copy-start.1
  2.9 0.0 copy-start.3
  2.9 0.0 copy-start.4
  3.0 0.0 copy-start.5
  3.0 1.6 %collective-permute-start = (bf16[128,256]{1,0:T(8,128)(2,1)}, bf16[128,256]{1,0:T(8,128)(2,1)S(1)}, u32[]{:S(2)}, u32[]{:S(2)}) collective-permute-start(bf16[128,256]{1,0:T(8,128)(2,1)} %bitcast.10), channel_id=1, source_target_pairs={{0,4},{4,0},{8,12},{12,8},{16,20},{20,16},{24,28},{28,24},{1,5},{5... | collective-permute-start | bytes 196616 | tf_op jit(solution)/shard_map/ppermute | solution.py:23
  4.6 0.1 collective-permute-done.1.refs_4_.q_ref
  4.7 0.0 copy-done.1
  4.7 0.0 copy-done.3
  4.7 0.0 copy-done.4
  4.7 0.0 copy-done.5
  4.7 2.5 %plan.1 = (bf16[256,512]{1,0:T(8,128)(2,1)S(1)}, bf16[256,512]{1,0:T(8,128)(2,1)S(1)}, f32[8,256]{1,0:T(8,128)S(1)}, bf16[512,512]{1,0:T(8,128)(2,1)S(1)}, bf16[...) custom-call(s32[2,8]{1,0:T(2,128)S(1)} %bitcast.14, ...), custom_call_target="tpu_custom_call" | custom-call | flops 1000000000 | bytes 3000000 | tf_op jit(solution)/shard_map/plan/pallas_call | solution.py:28
  7.2 0.0 copy-start.2
  7.2 0.0 copy-done
  7.3 0.7 %near.1.dep_ref.rest_1_.refs_2_.refs_9_ = f32[2,512,256]{2,1,0:T(8,128)S(1)} custom-call(bf16[2,512,512]{2,1,0:T(8,128)(2,1)S(1)} %copy-done, bf16[2,128,512]{2,1,0:T(8,128)(2,1)S(1)} %bitcast.9, bf16[2,128,512]{2,1,0:T(8,128)(2,1)S(1)} %collective-permute-done.1.refs_4_.q_ref, bf16[256,1024]{1,0:T(8,128)(2,1)S(1)} %get-tuple-element.36.dep_ref.refs_0_), custom_call_target="tpu_custom_call" | custom-call | flops 700000000 | bytes 2100000 | tf_op jit(solution)/shard_map/near/pallas_call | solution.py:28
  8.0 0.0 collective-permute-done.b_ref.near_ref
  8.0 0.1 copy-done.2
  8.1 1.4 %collective-permute-done.3.in_ref = bf16[2,128,512]{2,1,0:T(8,128)(2,1)S(1)} collective-permute-done((bf16[2,128,512]{2,1,0:T(8,128)(2,1)}, bf16[2,128,512]{2,1,0:T(8,128)(2,1)S(1)}, u32[]{:S(2)}, u32[]{:S(2)}) %collective-permute-start.3) | collective-permute-done | bytes 262176 | tf_op jit(solution)/shard_map/ppermute | solution.py:23
  9.5 0.1 collective-permute-start.4
  9.6 1.9 %collective-permute-start.2 = (bf16[2,128,256]{2,1,0:T(8,128)(2,1)S(1)}, bf16[2,128,256]{2,1,0:T(8,128)(2,1)S(1)}, u32[]{:S(2)}, u32[]{:S(2)}) collective-permute-start(bf16[2,128,256]{2,1,0:T(8,128)(2,1)S(1)} %pair.1.rest_0_), channel_id=1, source_target_pairs={{0,8},{4,12},{8,0},{12,4},{16,24},{20,28},{24,16},{28,20},{1,9},{5... | collective-permute-start | bytes 393224 | tf_op jit(solution)/shard_map/ppermute | solution.py:23
  11.4 0.0 collective-permute-done.4.refs_2_.refs_3_.q_ref
  11.5 0.9 %first.1 = (bf16[256,1024]{1,0:T(8,128)(2,1)S(1)}, s16[848,128]{1,0:T(8,128)(2,1)S(1)}, s16[464,128]{1,0:T(8,128)(2,1)S(1)}) custom-call(bf16[256,1024]{1,0:T(8,128)(2,1)S(1)} %get-tuple-element.36.dep_ref.refs_0_, bf16[2,128,512]{2,1,0:T(8,128)(2,1)S(1)} %relay.1.refs_1_.refs_2_.p_ref, ...), custom_call_target="tpu_custom_call" | custom-call | flops 800000000 | bytes 2400000 | tf_op jit(solution)/shard_map/first/pallas_call | solution.py:28
  12.4 1.6 %collective-permute-start.9 = (s16[848,128]{1,0:T(8,128)(2,1)S(1)}, s16[848,128]{1,0:T(8,128)(2,1)S(1)}, u32[]{:S(2)}, u32[]{:S(2)}) collective-permute-start(s16[848,128]{1,0:T(8,128)(2,1)S(1)} %get-tuple-element.44.refs_7_), channel_id=1, source_target_pairs={{0,4},{4,0},{8,12},{12,8},{16,20},{20,16},{24,28},{28,24},{1,5},{5... | collective-permute-start | bytes 651272 | tf_op jit(solution)/shard_map/ppermute | solution.py:23
  14.0 0.8 %ahead.1 = (bf16[256,1024]{1,0:T(8,128)(2,1)S(1)}, s16[928,128]{1,0:T(8,128)(2,1)S(1)}) custom-call(bf16[2,512,512]{2,1,0:T(8,128)(2,1)S(1)} %copy-done, bf16[256,1024]{1,0:T(8,128)(2,1)S(1)} %get-tuple-element.39.refs_1_, bf16[2,128,512]{2,1,0:T(8,128)(2,1)S(1)} %relay.1.refs_1_.refs_2_.p_ref, ...), custom_call_target="tpu_custom_call" | custom-call | flops 1400000000 | bytes 4200000 | tf_op jit(solution)/shard_map/ahead/pallas_call | solution.py:28
  14.7 1.5 %collective-permute-start.6 = (s16[928,128]{1,0:T(8,128)(2,1)S(1)}, s16[928,128]{1,0:T(8,128)(2,1)S(1)}, u32[]{:S(2)}, u32[]{:S(2)}) collective-permute-start(s16[928,128]{1,0:T(8,128)(2,1)S(1)} %get-tuple-element.47.refs_3_.own_ref), channel_id=1, source_target_pairs={{0,8},{4,12},{8,0},{12,4},{16,24},{20,28},{24,16},{28,20},{1,9},{5... | collective-permute-start | bytes 712712 | tf_op jit(solution)/shard_map/ppermute | solution.py:23
  16.3 0.7 %ready.1.dep_ref = s16[784,128]{1,0:T(8,128)(2,1)S(1)} custom-call(bf16[2,512,512]{2,1,0:T(8,128)(2,1)S(1)} %copy-done, bf16[256,1024]{1,0:T(8,128)(2,1)S(1)} %get-tuple-element.46.refs_1_, f32[8,256]{1,0:T(8,128)S(1)} %get-tuple-element.42.refs_5_.refs_6_.refs_2_, s16[928,128]{1,0:T(8,128)(2,1)S(1)} %get-tuple-element.47.refs_3_.own_ref), custom_call_target="tpu_custom_call" | custom-call | flops 600000000 | bytes 1800000 | tf_op jit(solution)/shard_map/ready/pallas_call | solution.py:28
  17.0 0.5 %collective-permute-start.5 = (s16[784,128]{1,0:T(8,128)(2,1)S(1)}, s16[784,128]{1,0:T(8,128)(2,1)S(1)}, u32[]{:S(2)}, u32[]{:S(2)}) collective-permute-start(s16[784,128]{1,0:T(8,128)(2,1)S(1)} %ready.1.dep_ref), channel_id=1, source_target_pairs={{0,4},{4,0},{8,12},{12,8},{16,20},{20,16},{24,28},{28,24},{1,5},{5... | collective-permute-start | bytes 602120 | tf_op jit(solution)/shard_map/ppermute | solution.py:23
  17.5 0.7 %rows.1.dep_ref.refs_3_.refs_8_ = f32[512,512]{1,0:T(8,128)S(1)} custom-call(bf16[2,512,512]{2,1,0:T(8,128)(2,1)S(1)} %copy-done, bf16[256,1024]{1,0:T(8,128)(2,1)S(1)} %get-tuple-element.45.picked_ref, s16[784,128]{1,0:T(8,128)(2,1)S(1)} %ready.1.dep_ref), custom_call_target="tpu_custom_call" | custom-call | flops 1000000000 | bytes 3000000 | tf_op jit(solution)/shard_map/rows/pallas_call | solution.py:28
  18.2 0.0 collective-permute-done.2.far_ref
  18.2 0.8 %core.1 = (bf16[512,512]{1,0:T(8,128)(2,1)S(1)}, bf16[512,512]{1,0:T(8,128)(2,1)S(1)}, bf16[512,512]{1,0:T(8,128)(2,1)S(1)}) custom-call(bf16[128,256]{1,0:T(8,128)(2,1)S(1)} %bitcast.12, bf16[128,256]{1,0:T(8,128)(2,1)S(1)} %collective-permute-done.b_ref.near_ref, bf16[2,128,256]{2,1,0:T(8,128)(2,1)S(1)} %collective-permute-done.2.far_ref, ...), custom_call_target="tpu_custom_call" | custom-call | flops 1000000000 | bytes 3000000 | tf_op jit(solution)/shard_map/core/pallas_call | solution.py:28
  19.0 0.7 %leaf.1.refs_3_.refs_10_.refs_6_ = f32[2,512,256]{2,1,0:T(8,128)S(1)} custom-call(bf16[2,512,512]{2,1,0:T(8,128)(2,1)S(1)} %copy-done, bf16[2,128,512]{2,1,0:T(8,128)(2,1)S(1)} %relay.1.refs_1_.refs_2_.p_ref, bf16[2,128,512]{2,1,0:T(8,128)(2,1)S(1)} %collective-permute-done.4.refs_2_.refs_3_.q_ref, ...), custom_call_target="tpu_custom_call" | custom-call | flops 700000000 | bytes 2100000 | tf_op jit(solution)/shard_map/leaf/pallas_call | solution.py:28
  19.8 0.7 %collective-permute-done.9.refs_0_ = s16[848,128]{1,0:T(8,128)(2,1)S(1)} collective-permute-done((s16[848,128]{1,0:T(8,128)(2,1)S(1)}, s16[848,128]{1,0:T(8,128)(2,1)S(1)}, u32[]{:S(2)}, u32[]{:S(2)}) %collective-permute-start.9) | collective-permute-done | bytes 217120 | tf_op jit(solution)/shard_map/ppermute | solution.py:23
  20.5 0.9 %second0.1 = (s16[848,128]{1,0:T(8,128)(2,1)S(1)}, bf16[2,208,512]{2,1,0:T(8,128)(2,1)S(1)}, bf16[2,208,512]{2,1,0:T(8,128)(2,1)S(1)}) custom-call(s16[848,128]{1,0:T(8,128)(2,1)S(1)} %collective-permute-done.9.refs_0_, bf16[512,512]{1,0:T(8,128)(2,1)S(1)} %get-tuple-element.50.refs_1_.refs_2_, bf16[512,512]{1,0:T(8,128)(2,1)S(1)} %get-tuple-element.51.refs_2_.refs_3_, ...), custom_call_target="tpu_custom_call" | custom-call | flops 800000000 | bytes 2400000 | tf_op jit(solution)/shard_map/second0/pallas_call | solution.py:28
  21.4 1.7 %collective-permute-start.10 = (s16[848,128]{1,0:T(8,128)(2,1)S(1)}, s16[848,128]{1,0:T(8,128)(2,1)S(1)}, u32[]{:S(2)}, u32[]{:S(2)}) collective-permute-start(s16[848,128]{1,0:T(8,128)(2,1)S(1)} %get-tuple-element.62), channel_id=1, source_target_pairs={{0,8},{4,12},{8,0},{12,4},{16,24},{20,28},{24,16},{28,20},{1,9},{5... | collective-permute-start | bytes 651272 | tf_op jit(solution)/shard_map/ppermute | solution.py:23
  23.1 0.0 collective-permute-done.6.got_ref.refs_1_
  23.1 1.6 %collective-permute-start.8 = (s16[928,128]{1,0:T(8,128)(2,1)S(1)}, s16[928,128]{1,0:T(8,128)(2,1)S(1)}, u32[]{:S(2)}, u32[]{:S(2)}) collective-permute-start(s16[928,128]{1,0:T(8,128)(2,1)S(1)} %onward.1.refs_6_), channel_id=1, source_target_pairs={{0,4},{4,0},{8,12},{12,8},{16,20},{20,16},{24,28},{28,24},{1,5},{5... | collective-permute-start | bytes 712712 | tf_op jit(solution)/shard_map/ppermute | solution.py:23
  24.7 0.0 collective-permute-done.5.refs_0_
  24.7 0.9 %second1.1 = (s16[784,128]{1,0:T(8,128)(2,1)S(1)}, bf16[2,192,512]{2,1,0:T(8,128)(2,1)S(1)}, bf16[2,192,512]{2,1,0:T(8,128)(2,1)S(1)}) custom-call(s16[784,128]{1,0:T(8,128)(2,1)S(1)} %collective-permute-done.5.refs_0_, bf16[512,512]{1,0:T(8,128)(2,1)S(1)} %get-tuple-element.50.refs_1_.refs_2_, bf16[512,512]{1,0:T(8,128)(2,1)S(1)} %get-tuple-element.51.refs_2_.refs_3_, ...), custom_call_target="tpu_custom_call" | custom-call | flops 800000000 | bytes 2400000 | tf_op jit(solution)/shard_map/second1/pallas_call | solution.py:28
  25.6 1.0 %collective-permute-start.7 = (s16[784,128]{1,0:T(8,128)(2,1)S(1)}, s16[784,128]{1,0:T(8,128)(2,1)S(1)}, u32[]{:S(2)}, u32[]{:S(2)}) collective-permute-start(s16[784,128]{1,0:T(8,128)(2,1)S(1)} %get-tuple-element.53), channel_id=1, source_target_pairs={{0,8},{4,12},{8,0},{12,4},{16,24},{20,28},{24,16},{28,20},{1,9},{5... | collective-permute-start | bytes 602120 | tf_op jit(solution)/shard_map/ppermute | solution.py:23
  26.6 0.6 %third1.1 = (f32[2,192,512]{2,1,0:T(8,128)S(1)}, f32[192,512]{1,0:T(8,128)S(1)}) custom-call(bf16[2,192,512]{2,1,0:T(8,128)(2,1)S(1)} %get-tuple-element.54.refs_0_.refs_6_, bf16[2,192,512]{2,1,0:T(8,128)(2,1)S(1)} %get-tuple-element.55.refs_1_, f32[2,512,256]{2,1,0:T(8,128)S(1)} %near.1.dep_ref.rest_1_.refs_2_.refs_9_, ...), custom_call_target="tpu_custom_call" | custom-call | flops 500000000 | bytes 1500000 | tf_op jit(solution)/shard_map/third1/pallas_call | solution.py:28
  27.1 0.6 %third0.1 = (f32[2,208,512]{2,1,0:T(8,128)S(1)}, f32[208,512]{1,0:T(8,128)S(1)}) custom-call(bf16[2,208,512]{2,1,0:T(8,128)(2,1)S(1)} %get-tuple-element.63.refs_0_, bf16[2,208,512]{2,1,0:T(8,128)(2,1)S(1)} %get-tuple-element.64.refs_1_, f32[2,512,256]{2,1,0:T(8,128)S(1)} %near.1.dep_ref.rest_1_.refs_2_.refs_9_, ...), custom_call_target="tpu_custom_call" | custom-call | flops 500000000 | bytes 1500000 | tf_op jit(solution)/shard_map/third0/pallas_call | solution.py:28
  27.8 0.0 collective-permute-done.10.refs_3_
  27.8 1.7 %last0.1.refs_7_ = f32[2,512,512]{2,1,0:T(8,128)} custom-call(bf16[512,512]{1,0:T(8,128)(2,1)S(1)} %get-tuple-element.48.refs_14_.refs_0_, bf16[512,512]{1,0:T(8,128)(2,1)S(1)} %get-tuple-element.49.refs_15_.refs_1_, bf16[256,512]{1,0:T(8,128)(2,1)S(1)} %get-tuple-element.40.refs_4_.refs_12_.refs_2_, s16[848,128]{1,0:T(8,128)(2,1)S(1)} %collective-permute-done.10.refs_3_, ...), custom_call_target="tpu_custom_call" | custom-call | flops 1000000000 | bytes 3000000 | tf_op jit(solution)/shard_map/last0/pallas_call | solution.py:28
  29.5 0.0 collective-permute-done.8.refs_0_
  29.5 1.9 %around.1.refs_6_ = f32[2,112,512]{2,1,0:T(8,128)S(1)} custom-call(s16[928,128]{1,0:T(8,128)(2,1)S(1)} %collective-permute-done.8.refs_0_, s16[928,128]{1,0:T(8,128)(2,1)S(1)} %collective-permute-done.6.got_ref.refs_1_, bf16[512,512]{1,0:T(8,128)(2,1)S(1)} %get-tuple-element.50.refs_1_.refs_2_, bf16[512,512]{1,0:T(8,128)(2,1)S(1)} %get-tuple-element.51.refs_2_.refs_3_, ...), custom_call_target="tpu_custom_call" | custom-call | flops 2500000000 | bytes 7500000 | tf_op jit(solution)/shard_map/around/pallas_call | solution.py:28
  31.4 0.3 %collective-permute-done.7.refs_3_ = s16[784,128]{1,0:T(8,128)(2,1)S(1)} collective-permute-done((s16[784,128]{1,0:T(8,128)(2,1)S(1)}, s16[784,128]{1,0:T(8,128)(2,1)S(1)}, u32[]{:S(2)}, u32[]{:S(2)}) %collective-permute-start.7) | collective-permute-done | bytes 200736 | tf_op jit(solution)/shard_map/ppermute | solution.py:23
  31.7 1.7 %last1.1 = f32[2,512,512]{2,1,0:T(8,128)} custom-call(bf16[512,512]{1,0:T(8,128)(2,1)S(1)} %get-tuple-element.48.refs_14_.refs_0_, bf16[512,512]{1,0:T(8,128)(2,1)S(1)} %get-tuple-element.49.refs_15_.refs_1_, bf16[256,512]{1,0:T(8,128)(2,1)S(1)} %get-tuple-element.40.refs_4_.refs_12_.refs_2_, ...), custom_call_target="tpu_custom_call", output_to_operand_aliasing={{}: (7, {})} | custom-call | flops 1000000000 | bytes 3000000 | tf_op jit(solution)/shard_map/last1/pallas_call | solution.py:28
  (5 shorter events, 0.0 us)
Async XLA Ops:
  0.0 9.5 %collective-permute-start.3 = (bf16[2,128,512]{2,1,0:T(8,128)(2,1)}, bf16[2,128,512]{2,1,0:T(8,128)(2,1)S(1)}, u32[]{:S(2)}, u32[]{:S(2)}) collective-permute-start(bf16[2,128,512]{2,1,0:T(8,128)(2,1)} %bitcast.6), channel_id=1, source_target_pairs={{0,2},{1,3},{2,0},{3,1},{4,6},{5,7},{6,4},{7,5},{8,10},{9,11},{10,... | collective-permute-start | bytes 786440 | tf_op jit(solution)/shard_map/ppermute | solution.py:23
  2.9 1.7 %collective-permute-start.1 = (bf16[2,128,512]{2,1,0:T(8,128)(2,1)}, bf16[2,128,512]{2,1,0:T(8,128)(2,1)S(1)}, u32[]{:S(2)}, u32[]{:S(2)}) collective-permute-start(bf16[2,128,512]{2,1,0:T(8,128)(2,1)} %bitcast.7), channel_id=1, source_target_pairs={{0,1},{1,0},{2,3},{3,2},{4,5},{5,4},{6,7},{7,6},{8,9},{9,8},{10,11... | collective-permute-start | bytes 786440 | tf_op jit(solution)/shard_map/ppermute | solution.py:23
  2.9 1.7 %copy-start.1 = (bf16[1,2,128,512]{3,2,1,0:T(8,128)(2,1)S(1)}, bf16[1,2,128,512]{3,2,1,0:T(8,128)(2,1)}, u32[]{:S(2)}) copy-start(bf16[1,2,128,512]{3,2,1,0:T(8,128)(2,1)} %param.7) | copy-start | bytes 786436
  2.9 1.7 %copy-start.3 = (s32[8,2,256]{2,1,0:T(2,128)S(1)}, s32[8,2,256]{2,1,0:T(2,128)}, u32[]{:S(2)}) copy-start(s32[8,2,256]{2,1,0:T(2,128)} %refs_1_.1) | copy-start | bytes 49156
  2.9 1.7 %copy-start.4 = (f32[512]{0:T(512)S(1)}, f32[512]{0:T(512)}, u32[]{:S(2)}) copy-start(f32[512]{0:T(512)} %param.8) | copy-start | bytes 6148
  3.0 1.7 %copy-start.5 = (s32[8,2]{0,1:T(2,128)S(1)}, s32[8,2]{0,1:T(2,128)}, u32[]{:S(2)}) copy-start(s32[8,2]{0,1:T(2,128)} %param.10) | copy-start | bytes 196
  3.0 5.0 %collective-permute-start = (bf16[128,256]{1,0:T(8,128)(2,1)}, bf16[128,256]{1,0:T(8,128)(2,1)S(1)}, u32[]{:S(2)}, u32[]{:S(2)}) collective-permute-start(bf16[128,256]{1,0:T(8,128)(2,1)} %bitcast.10), channel_id=1, source_target_pairs={{0,4},{4,0},{8,12},{12,8},{16,20},{20,16},{24,28},{28,24},{1,5},{5... | collective-permute-start | bytes 196616 | tf_op jit(solution)/shard_map/ppermute | solution.py:23
  4.5 2.7 %copy-start = (bf16[2,512,512]{2,1,0:T(8,128)(2,1)S(1)}, bf16[2,512,512]{2,1,0:T(8,128)(2,1)}, u32[]{:S(2)}) copy-start(bf16[2,512,512]{2,1,0:T(8,128)(2,1)} %x_ref.5) | copy-start | bytes 3145732
  7.2 0.8 %copy-start.2 = (bf16[2,256,64]{1,2,0:T(8,128)(2,1)S(1)}, bf16[2,256,64]{1,2,0:T(8,128)(2,1)}, u32[]{:S(2)}) copy-start(bf16[2,256,64]{1,2,0:T(8,128)(2,1)} %param.11) | copy-start | bytes 196612
  9.5 2.0 %collective-permute-start.4 = (bf16[2,128,512]{2,1,0:T(8,128)(2,1)S(1)}, bf16[2,128,512]{2,1,0:T(8,128)(2,1)S(1)}, u32[]{:S(2)}, u32[]{:S(2)}) collective-permute-start(bf16[2,128,512]{2,1,0:T(8,128)(2,1)S(1)} %relay.1.refs_1_.refs_2_.p_ref), channel_id=1, source_target_pairs={{0,1},{1,0},{2,3},{3,2},{4,5},{5,4},{6,7},{7,6},{8,9},{9,8},{10,11... | collective-permute-start | bytes 786440 | tf_op jit(solution)/shard_map/ppermute | solution.py:23
  9.6 8.7 %collective-permute-start.2 = (bf16[2,128,256]{2,1,0:T(8,128)(2,1)S(1)}, bf16[2,128,256]{2,1,0:T(8,128)(2,1)S(1)}, u32[]{:S(2)}, u32[]{:S(2)}) collective-permute-start(bf16[2,128,256]{2,1,0:T(8,128)(2,1)S(1)} %pair.1.rest_0_), channel_id=1, source_target_pairs={{0,8},{4,12},{8,0},{12,4},{16,24},{20,28},{24,16},{28,20},{1,9},{5... | collective-permute-start | bytes 393224 | tf_op jit(solution)/shard_map/ppermute | solution.py:23
  12.4 8.1 %collective-permute-start.9 = (s16[848,128]{1,0:T(8,128)(2,1)S(1)}, s16[848,128]{1,0:T(8,128)(2,1)S(1)}, u32[]{:S(2)}, u32[]{:S(2)}) collective-permute-start(s16[848,128]{1,0:T(8,128)(2,1)S(1)} %get-tuple-element.44.refs_7_), channel_id=1, source_target_pairs={{0,4},{4,0},{8,12},{12,8},{16,20},{20,16},{24,28},{28,24},{1,5},{5... | collective-permute-start | bytes 651272 | tf_op jit(solution)/shard_map/ppermute | solution.py:23
  14.7 8.3 %collective-permute-start.6 = (s16[928,128]{1,0:T(8,128)(2,1)S(1)}, s16[928,128]{1,0:T(8,128)(2,1)S(1)}, u32[]{:S(2)}, u32[]{:S(2)}) collective-permute-start(s16[928,128]{1,0:T(8,128)(2,1)S(1)} %get-tuple-element.47.refs_3_.own_ref), channel_id=1, source_target_pairs={{0,8},{4,12},{8,0},{12,4},{16,24},{20,28},{24,16},{28,20},{1,9},{5... | collective-permute-start | bytes 712712 | tf_op jit(solution)/shard_map/ppermute | solution.py:23
  17.0 7.7 %collective-permute-start.5 = (s16[784,128]{1,0:T(8,128)(2,1)S(1)}, s16[784,128]{1,0:T(8,128)(2,1)S(1)}, u32[]{:S(2)}, u32[]{:S(2)}) collective-permute-start(s16[784,128]{1,0:T(8,128)(2,1)S(1)} %ready.1.dep_ref), channel_id=1, source_target_pairs={{0,4},{4,0},{8,12},{12,8},{16,20},{20,16},{24,28},{28,24},{1,5},{5... | collective-permute-start | bytes 602120 | tf_op jit(solution)/shard_map/ppermute | solution.py:23
  21.4 6.4 %collective-permute-start.10 = (s16[848,128]{1,0:T(8,128)(2,1)S(1)}, s16[848,128]{1,0:T(8,128)(2,1)S(1)}, u32[]{:S(2)}, u32[]{:S(2)}) collective-permute-start(s16[848,128]{1,0:T(8,128)(2,1)S(1)} %get-tuple-element.62), channel_id=1, source_target_pairs={{0,8},{4,12},{8,0},{12,4},{16,24},{20,28},{24,16},{28,20},{1,9},{5... | collective-permute-start | bytes 651272 | tf_op jit(solution)/shard_map/ppermute | solution.py:23
  23.1 6.4 %collective-permute-start.8 = (s16[928,128]{1,0:T(8,128)(2,1)S(1)}, s16[928,128]{1,0:T(8,128)(2,1)S(1)}, u32[]{:S(2)}, u32[]{:S(2)}) collective-permute-start(s16[928,128]{1,0:T(8,128)(2,1)S(1)} %onward.1.refs_6_), channel_id=1, source_target_pairs={{0,4},{4,0},{8,12},{12,8},{16,20},{20,16},{24,28},{28,24},{1,5},{5... | collective-permute-start | bytes 712712 | tf_op jit(solution)/shard_map/ppermute | solution.py:23
  25.6 6.1 %collective-permute-start.7 = (s16[784,128]{1,0:T(8,128)(2,1)S(1)}, s16[784,128]{1,0:T(8,128)(2,1)S(1)}, u32[]{:S(2)}, u32[]{:S(2)}) collective-permute-start(s16[784,128]{1,0:T(8,128)(2,1)S(1)} %get-tuple-element.53), channel_id=1, source_target_pairs={{0,8},{4,12},{8,0},{12,4},{16,24},{20,28},{24,16},{28,20},{1,9},{5... | collective-permute-start | bytes 602120 | tf_op jit(solution)/shard_map/ppermute | solution.py:23
